TPU v7x, 32 devices: a whole 2x2x4 slice. The times are simulated.
32 devices in a mesh: nodes: 16 (over z, y, x), mp: 2 (over core).
Axes of the slice: x: 2, y: 2, z: 4, core: 2. Of those that a mesh axis runs over, the one named last changes fastest.
Arguments:
- memory: bfloat16 [32768, 512], P('nodes'), may hold values from -6 to 6
- ev_time: int32 [2048], P('nodes'), may hold values from 0 to 1023
- nbr_time: int32 [2048, 2, 16], P('nodes'), may hold values from 0 to 1023
- edge_feat: bfloat16 [2048, 128], P('nodes', 'mp'), may hold values from -6 to 6
- self_slot: int32 [2048, 2], P('nodes'), may hold values from 0 to 511
- nbr_slot: int32 [2048, 2, 16], P('nodes'), may hold values from 0 to 511
- serve_self: int32 [16, 16, 32], P('nodes'), may hold values from 0 to 2047
- serve_rows: int32 [16, 16, 32], P('nodes'), may hold values from 0 to 2047
- freq: float32 [128], replicated, may hold values from 0.001 to 0.5
- phase: float32 [128], replicated, may hold values from -3.140625 to 3.140625
- w_query: bfloat16 [640, 512], P(None, 'mp'), may hold values from -0.25 to 0.25
- w_key: bfloat16 [640, 512], P(None, 'mp'), may hold values from -0.25 to 0.25
- w_value: bfloat16 [640, 512], P(None, 'mp'), may hold values from -0.25 to 0.25
- w_out: bfloat16 [512, 512], P('mp'), may hold values from -0.25 to 0.25
- w_self: bfloat16 [512, 512], P('mp'), may hold values from -0.25 to 0.25
- w_msg_self: bfloat16 [512, 512], P('mp'), may hold values from -0.25 to 0.25
- w_msg_other: bfloat16 [512, 512], P('mp'), may hold values from -0.25 to 0.25
- w_msg_time: bfloat16 [128, 512], P('mp'), may hold values from -0.5 to 0.5
- w_msg_edge: bfloat16 [128, 512], P('mp'), may hold values from -0.5 to 0.5
- w_in: bfloat16 [512, 3, 512], P(None, None, 'mp'), may hold values from -0.25 to 0.25
- w_hid: bfloat16 [512, 3, 512], P(None, None, 'mp'), may hold values from -0.25 to 0.25
Outputs:
- embedding: bfloat16 [2048, 2, 512], P('nodes')
- memory_out: bfloat16 [32768, 512], P('nodes', 'mp')
Inputs may be any that keep to these rules, and one draw needn't show every extreme that they name: `self_slot`: slot index o * 32 + s refers to endpoint slot s of owner o. `nbr_slot`: slot index o * 32 + s refers to neighbour slot s of owner o.
All inputs are finite; a program needn't handle non-finite values.
Results may differ from a plain program's by a relative error of at most 0.0075.
Values may be sent and summed in bfloat16 or wider, within the bound.
No kernel may reach another device: no remote copies, remote signals or barrier semaphores. Data moves between devices by JAX's collectives and lax.ppermute only.
A program may use at most 128 MiB of HBM per device.

v0:
```python
import jax
import jax.numpy as jnp
from jax import lax
from jax.sharding import PartitionSpec as P

HEADS = 8


def encode(delta, freq, phase):
    return jnp.cos(delta.astype(jnp.float32)[..., None] * freq + phase)


def per_device(
    memory,
    ev_time,
    nbr_time,
    edge_feat,
    self_slot,
    nbr_slot,
    serve_self,
    serve_rows,
    freq,
    phase,
    w_query,
    w_key,
    w_value,
    w_out,
    w_self,
    w_msg_self,
    w_msg_other,
    w_msg_time,
    w_msg_edge,
    w_in,
    w_hid,
):
    width = memory.shape[1]
    half = w_out.shape[0]
    core = lax.axis_index("mp")
    serving = serve_rows[0]
    serving_self = serve_self[0]
    peers, capacity = serving.shape
    cap_self = serving_self.shape[1]
    picked = memory[serving]
    picked_self = memory[serving_self]
    fetched, fetched_self = (
        lax.all_to_all(picked, "nodes", split_axis=0, concat_axis=0, tiled=True),
        lax.all_to_all(picked_self, "nodes", split_axis=0, concat_axis=0, tiled=True),
    )
    flat = fetched.reshape(peers * capacity, width)
    flat_self = fetched_self.reshape(peers * cap_self, width)
    events = nbr_slot.shape[0]
    neigh = nbr_slot.shape[2]
    tdim = freq.shape[0]
    self_refs = flat_self[self_slot]
    self_mem = self_refs.reshape(-1, width)
    nbrs = flat[nbr_slot].reshape(-1, width)
    te_nbr = (
        encode(ev_time[:, None, None] - nbr_time, freq, phase)
        .astype(jnp.bfloat16)
        .reshape(-1, tdim)
    )
    te_self = jnp.cos(phase).astype(jnp.bfloat16)[None]
    query = (
        jnp.dot(self_mem, w_query[:width], preferred_element_type=jnp.float32)
        + jnp.dot(te_self, w_query[width:], preferred_element_type=jnp.float32)
    ).astype(jnp.bfloat16)
    keys = (
        jnp.dot(nbrs, w_key[:width], preferred_element_type=jnp.float32)
        + jnp.dot(te_nbr, w_key[width:], preferred_element_type=jnp.float32)
    ).astype(jnp.bfloat16)
    values = (
        jnp.dot(nbrs, w_value[:width], preferred_element_type=jnp.float32)
        + jnp.dot(te_nbr, w_value[width:], preferred_element_type=jnp.float32)
    ).astype(jnp.bfloat16)
    head_size = width // HEADS
    local_heads = half // head_size
    qh = query.reshape(-1, local_heads, head_size)
    kh = keys.reshape(-1, neigh, local_heads, head_size)
    vh = values.reshape(-1, neigh, local_heads, head_size)
    score = jnp.einsum("nhd,nkhd->nhk", qh, kh, preferred_element_type=jnp.float32) / jnp.sqrt(
        jnp.float32(head_size)
    )
    expo = jnp.exp(score)
    weights = (expo / jnp.sum(expo, axis=-1, keepdims=True)).astype(jnp.bfloat16)
    att = (
        jnp.einsum("nhk,nkhd->nhd", weights, vh, preferred_element_type=jnp.float32)
        .astype(jnp.bfloat16)
        .reshape(-1, half)
    )
    self_half = lax.dynamic_slice_in_dim(self_mem, core * half, half, 1)
    other_half = lax.dynamic_slice_in_dim(
        self_refs[:, ::-1].reshape(-1, width), core * half, half, 1
    )
    emb_part = jnp.dot(att, w_out, preferred_element_type=jnp.float32) + jnp.dot(
        self_half, w_self, preferred_element_type=jnp.float32
    )
    time_part = w_msg_time.shape[0]
    te_msg = (
        encode(ev_time[:, None] - nbr_time[:, :, 0], freq, phase)
        .astype(jnp.bfloat16)
        .reshape(-1, tdim)
    )
    te_half = lax.dynamic_slice_in_dim(te_msg, core * time_part, time_part, 1)
    edge_two = jnp.broadcast_to(edge_feat[:, None], (events, 2, edge_feat.shape[1])).reshape(
        -1, edge_feat.shape[1]
    )
    msg_part = (
        jnp.dot(self_half, w_msg_self, preferred_element_type=jnp.float32)
        + jnp.dot(other_half, w_msg_other, preferred_element_type=jnp.float32)
        + jnp.dot(te_half, w_msg_time, preferred_element_type=jnp.float32)
        + jnp.dot(edge_two, w_msg_edge, preferred_element_type=jnp.float32)
    )
    target = self_slot.reshape(-1)
    owned = memory.shape[0]
    local_rows = serving_self.reshape(-1)
    slot_count = (
        jnp.zeros((peers * cap_self,), jnp.float32)
        .at[target]
        .add(jnp.ones(target.shape, jnp.float32))
    )
    emb_sum, msg = lax.psum((emb_part, msg_part), "mp")
    msg_width = msg.shape[1]
    slot_msg = jnp.zeros((peers * cap_self, msg_width), jnp.float32).at[target].add(msg)
    back_msg, back_count = (
        lax.all_to_all(
            slot_msg.reshape(peers, cap_self, msg_width).astype(jnp.bfloat16),
            "nodes",
            split_axis=0,
            concat_axis=0,
            tiled=True,
        ).astype(jnp.float32),
        lax.all_to_all(
            slot_count.reshape(peers, cap_self).astype(jnp.bfloat16),
            "nodes",
            split_axis=0,
            concat_axis=0,
            tiled=True,
        ).astype(jnp.float32),
    )
    total = (
        jnp.zeros((owned, msg_width), jnp.float32)
        .at[local_rows]
        .add(back_msg.reshape(-1, msg_width))
    )
    count = jnp.zeros((owned,), jnp.float32).at[local_rows].add(back_count.reshape(-1))
    mean = (total / jnp.maximum(count, 1.0)[:, None]).astype(jnp.bfloat16)
    embedding = emb_sum.astype(jnp.bfloat16).reshape(events, 2, width)
    msg_width = mean.shape[1]
    gi = jnp.dot(
        mean, w_in.reshape(msg_width, 3 * half), preferred_element_type=jnp.float32
    ).reshape(-1, 3, half)
    gh = jnp.dot(
        memory, w_hid.reshape(width, 3 * half), preferred_element_type=jnp.float32
    ).reshape(-1, 3, half)
    reset = jax.nn.sigmoid(gi[:, 0] + gh[:, 0])
    gate = jax.nn.sigmoid(gi[:, 1] + gh[:, 1])
    cand = jnp.tanh(gi[:, 2] + reset * gh[:, 2])
    old = lax.dynamic_slice_in_dim(memory, core * half, half, 1).astype(jnp.float32)
    fresh = (1.0 - gate) * cand + gate * old
    memory_out = jnp.where(count[:, None] > 0, fresh, old).astype(jnp.bfloat16)
    return (embedding, memory_out)


def solution(mesh):
    return jax.shard_map(
        per_device,
        mesh=mesh,
        in_specs=(
            P("nodes", None),
            P("nodes"),
            P("nodes", None, None),
            P("nodes", "mp"),
            P("nodes", None),
            P("nodes", None, None),
            P("nodes", None, None),
            P("nodes", None, None),
            P(),
            P(),
            P(None, "mp"),
            P(None, "mp"),
            P(None, "mp"),
            P("mp", None),
            P("mp", None),
            P("mp", None),
            P("mp", None),
            P("mp", None),
            P("mp", None),
            P(None, None, "mp"),
            P(None, None, "mp"),
        ),
        out_specs=(P("nodes", None, None), P("nodes", "mp")),
        check_vma=False,
    )
```

profile of v0, /device:TPU:0, one launch (start us, length us, event | category | flops | bytes accessed | tf_op | source)
XLA Modules:
  0.0 207.3 jit_solution(7916861133240797988)
XLA Ops:
  7.2 0.8 copy.53
  8.7 2.3 %scatter_custom_fusion = f32[512]{0:T(512)S(1)} fusion(s32[256]{0:T(256)S(1)} %bitcast.84, f32[256]{0:T(256)S(1)} %broadcast.116, f32[]{:T(128)} %constant.14.clone.1), kind=kCustom, calls=%fused_computation.100 | custom fusion | flops 256 | bytes 2052 | tf_op jit(solution)/shard_map/scatter-add | solution.py:119
  11.8 8.3 %all-to-all-start.2 = ((bf16[16,1,32]{2,1,0:T(2,128)(2,1)}), bf16[16,1,32]{2,1,0:T(2,128)(2,1)S(1)}, u32[]{:S(2)}, u32[]{:S(2)}) async-start(bf16[16,1,32]{2,1,0:T(2,128)(2,1)} %convert_element_type.93), calls=%async_computation.2 | async-start | bytes 16384 | tf_op jit(solution)/shard_map/all_to_all | solution.py:132
  21.5 0.8 reshape_squeeze.3
  22.6 0.7 slice.45
  23.3 0.7 subtract_convert_fusion
  24.7 0.7 compare_select_fusion.1
  25.5 0.7 compare_select_fusion
  26.8 1.6 fusion.53
  28.4 10.7 %fusion.25 = f32[4096,256]{1,0:T(8,128)} fusion(f32[128]{0:T(128)} %param.30, f32[128]{0:T(128)} %param.29, f32[4096]{0:T(1024)S(1)} %mul.49, bf16[640,256]{1,0:T(8,128)(2,1)} %param.32), kind=kOutput, calls=%fused_computation.48 | convolution fusion | flops 270008320 | bytes 4277248 | tf_op jit(solution)/shard_map/dot_general | solution.py:69
  39.1 10.7 %fusion.24 = f32[4096,256]{1,0:T(8,128)} fusion(f32[128]{0:T(128)S(1)} %copy-done.8, f32[128]{0:T(128)S(1)} %copy-done.9, f32[4096]{0:T(1024)S(1)} %mul.49, bf16[640,256]{1,0:T(8,128)(2,1)} %param.33), kind=kOutput, calls=%fused_computation.47 | convolution fusion | flops 270008320 | bytes 4277248 | tf_op jit(solution)/shard_map/dot_general | solution.py:73
  50.3 1.2 copy.58
  51.5 2.3 %copy.59 = bf16[512,3,256]{0,2,1:T(8,128)(2,1)} copy(bf16[512,3,256]{2,0,1:T(8,128)(2,1)} %param.41) | data formatting | bytes 1572864 | tf_op args[20]
  53.8 2.6 %gather_fusion = bf16[512,512]{1,0:T(8,128)(2,1)} fusion(bf16[2048,512]{1,0:T(8,128)(2,1)S(1)} %copy-done.1, s32[1024]{0:T(1024)S(1)} %pad_clamp_fusion.2), kind=kCustom, calls=%fused_computation | custom fusion | bytes 1050624 | tf_op jit(solution)/shard_map/gather | solution.py:44
  56.4 2.6 %gather_fusion.2 = bf16[512,512]{1,0:T(8,128)(2,1)} fusion(bf16[2048,512]{1,0:T(8,128)(2,1)S(1)} %copy-done.1, s32[1024]{0:T(1024)S(1)} %pad_clamp_fusion), kind=kCustom, calls=%fused_computation.2 | custom fusion | bytes 1050624 | tf_op jit(solution)/shard_map/gather | solution.py:43
  59.0 6.9 %all-to-all-start = ((bf16[16,32,512]{2,1,0:T(8,128)(2,1)}), bf16[16,32,512]{2,1,0:T(8,128)(2,1)S(1)}, u32[]{:S(2)}, u32[]{:S(2)}) async-start(bf16[16,32,512]{2,1,0:T(8,128)(2,1)} %bitcast.3), calls=%async_computation | async-start | bytes 1048576 | tf_op jit(solution)/shard_map/all_to_all | solution.py:47
  65.9 5.6 %fusion.18 = f32[2048,3,256]{2,0,1:T(8,128)} fusion(bf16[2048,512]{1,0:T(8,128)(2,1)S(1)} %copy-done.1, bf16[512,3,256]{0,2,1:T(8,128)(2,1)} %copy.59), kind=kOutput, calls=%fused_computation.36 | convolution fusion | flops 1610612736 | bytes 9175040 | tf_op jit(solution)/shard_map/dot_general | solution.py:152
  71.7 3.3 %scatter_custom_fusion.1 = f32[2048]{0:T(1024)S(1)} fusion(s32[512]{0:T(512)S(1)} %bitcast.81, f32[512]{0:T(512)S(1)} %reshape.296, f32[]{:T(128)} %constant.14.clone.1), kind=kCustom, calls=%fused_computation.96 | custom fusion | flops 512 | bytes 8196 | tf_op jit(solution)/shard_map/scatter-add | solution.py:145
  76.1 4.4 %all-to-all-done = bf16[16,32,512]{2,1,0:T(8,128)(2,1)S(1)} async-done(((bf16[16,32,512]{2,1,0:T(8,128)(2,1)}), bf16[16,32,512]{2,1,0:T(8,128)(2,1)S(1)}, u32[]{:S(2)}, u32[]{:S(2)}) %all-to-all-start) | async-done | bytes 524320 | tf_op jit(solution)/shard_map/all_to_all | solution.py:47
  80.5 3.9 %all-to-all-start.1 = ((bf16[16,32,512]{2,1,0:T(8,128)(2,1)}), bf16[16,32,512]{2,1,0:T(8,128)(2,1)S(1)}, u32[]{:S(2)}, u32[]{:S(2)}) async-start(bf16[16,32,512]{2,1,0:T(8,128)(2,1)} %bitcast.74), calls=%async_computation.1 | async-start | bytes 1048576 | tf_op jit(solution)/shard_map/all_to_all | solution.py:46
  84.6 1.9 gather_fusion.1
  86.5 1.1 reshape.261
  87.6 1.4 rev.3
  89.1 1.2 fusion.45
  90.3 1.2 convolution_add_fusion.4
  92.3 1.0 convolution_add_fusion.2
  93.3 1.2 fusion.26
  94.7 4.1 %all-to-all-done.1 = bf16[16,32,512]{2,1,0:T(8,128)(2,1)S(1)} async-done(((bf16[16,32,512]{2,1,0:T(8,128)(2,1)}), bf16[16,32,512]{2,1,0:T(8,128)(2,1)S(1)}, u32[]{:S(2)}, u32[]{:S(2)}) %all-to-all-start.1) | async-done | bytes 524320 | tf_op jit(solution)/shard_map/all_to_all | solution.py:46
  98.8 17.3 %gather_fusion.3 = bf16[4096,512]{1,0:T(8,128)(2,1)} fusion(bf16[512,512]{1,0:T(8,128)(2,1)S(1)} %bitcast.72, s32[4096]{0:T(1024)S(1)} %broadcast_clamp_fusion), kind=kCustom, calls=%fused_computation.3 | custom fusion | bytes 8404992 | tf_op jit(solution)/shard_map/gather | solution.py:56
  116.1 6.1 %fusion.1 = bf16[4096,256]{1,0:T(8,128)(2,1)} fusion(f32[4096,256]{1,0:T(8,128)} %fusion.25, bf16[4096,512]{1,0:T(8,128)(2,1)} %gather_fusion.3, bf16[640,256]{1,0:T(8,128)(2,1)} %param.32), kind=kOutput, calls=%fused_computation.13 | convolution fusion | flops 1075838976 | bytes 10747904 | tf_op jit(solution)/shard_map/dot_general | solution.py:68
  122.2 7.1 %reshape.231 = bf16[256,16,4,64]{3,2,1,0:T(4,128)(2,1)} reshape(bf16[4096,256]{1,0:T(8,128)(2,1)} %fusion.1) | data formatting | bytes 4194304 | tf_op jit(solution)/shard_map/reshape | solution.py:78
  129.2 8.0 %multiply_reduce_fusion.1 = f32[256,4,16]{1,2,0:T(8,128)} fusion(f32[256,4,64]{2,1,0:T(4,128)S(1)} %copy.75, bf16[256,16,4,64]{3,2,1,0:T(4,128)(2,1)} %reshape.231), kind=kLoop, calls=%fused_computation.10 | loop fusion | flops 3129344 | bytes 2424832
  137.3 2.6 %copy.66 = f32[256,4,16]{0,2,1:T(8,128)S(1)} copy(f32[256,4,16]{1,2,0:T(8,128)} %multiply_reduce_fusion.1) | data formatting | bytes 131072 | tf_op jit(solution)/shard_map/nhd,nkhd->nhk/dot_general | solution.py:80
  140.3 2.4 %copy.76 = f32[256,4,16]{1,2,0:T(8,128)} copy(f32[256,4,16]{0,2,1:T(8,128)S(1)} %fusion.29) | data formatting | bytes 131072
  142.6 6.1 %fusion.2 = bf16[4096,256]{1,0:T(8,128)(2,1)} fusion(f32[4096,256]{1,0:T(8,128)} %fusion.24, bf16[4096,512]{1,0:T(8,128)(2,1)} %gather_fusion.3, bf16[640,256]{1,0:T(8,128)(2,1)S(1)} %copy-done.4), kind=kOutput, calls=%fused_computation.14 | convolution fusion | flops 1075838976 | bytes 10747904 | tf_op jit(solution)/shard_map/dot_general | solution.py:72
  148.7 7.1 %reshape.232 = bf16[256,16,4,64]{3,2,1,0:T(4,128)(2,1)} reshape(bf16[4096,256]{1,0:T(8,128)(2,1)} %fusion.2) | data formatting | bytes 4194304 | tf_op jit(solution)/shard_map/reshape | solution.py:79
  155.8 7.9 %multiply_reduce_fusion = bf16[256,4,64]{2,1,0:T(4,128)(2,1)S(1)} fusion(f32[256,4,16]{1,2,0:T(8,128)} %copy.76, bf16[256,16,4,64]{3,2,1,0:T(4,128)(2,1)} %reshape.232), kind=kLoop, calls=%fused_computation.9 | loop fusion | flops 3080192 | bytes 2293760
  163.9 2.8 %scatter_custom_fusion.2 = f32[512,512]{1,0:T(8,128)S(1)} fusion(s32[256]{0:T(256)} %bitcast.85, f32[256,512]{1,0:T(8,128)} %all-reduce.3.cloned.1.call-done, f32[]{:T(128)} %constant.14.clone.1), kind=kCustom, calls=%fused_computation.63 | custom fusion | flops 131072 | bytes 1049088 | tf_op jit(solution)/shard_map/scatter-add | solution.py:123
  166.7 0.9 convert_element_type.87
  167.6 3.8 %all-to-all-start.3 = ((bf16[16,32,512]{2,1,0:T(8,128)(2,1)}), bf16[16,32,512]{2,1,0:T(8,128)(2,1)S(1)}, u32[]{:S(2)}, u32[]{:S(2)}) async-start(bf16[16,32,512]{2,1,0:T(8,128)(2,1)} %bitcast.76), calls=%async_computation.3 | async-start | bytes 1048576 | tf_op jit(solution)/shard_map/all_to_all | solution.py:125
  171.4 1.2 fusion.68
  172.6 1.3 convolution_add_fusion.5
  173.9 5.3 %all-reduce.4 = bf16[256,512]{1,0:T(8,128)(2,1)} all-reduce(f32[256,512]{1,0:T(8,128)S(1)} %convolution_add_fusion.5), channel_id=1, replica_groups=mesh['nodes'=16,'mp'=2] {'mp'}, use_global_device_ids=true, to_apply=%region_1.0 | all-reduce | flops 131072 | bytes 786432 | tf_op jit(solution)/shard_map/psum | solution.py:121
  179.2 1.8 reshape.234
  181.0 4.8 %all-to-all-done.3 = bf16[16,32,512]{2,1,0:T(8,128)(2,1)S(1)} async-done(((bf16[16,32,512]{2,1,0:T(8,128)(2,1)}), bf16[16,32,512]{2,1,0:T(8,128)(2,1)S(1)}, u32[]{:S(2)}, u32[]{:S(2)}) %all-to-all-start.3) | async-done | bytes 524320 | tf_op jit(solution)/shard_map/all_to_all | solution.py:125
  185.8 6.0 %scatter_custom_fusion.3 = f32[2048,512]{1,0:T(8,128)} fusion(s32[512]{0:T(512)} %bitcast.82, f32[]{:T(128)} %constant.14.clone.1, bf16[512,512]{1,0:T(8,128)(2,1)S(1)} %bitcast.75), kind=kCustom, calls=%fused_computation.40 | custom fusion | flops 524288 | bytes 4719104 | tf_op jit(solution)/shard_map/scatter-add | solution.py:143
  191.8 4.2 %fusion.20 = f32[2048,3,256]{2,0,1:T(8,128)S(1)} fusion(f32[2048,512]{1,0:T(8,128)} %scatter_custom_fusion.3, f32[2048]{0:T(1024)S(1)} %copy-done.11, bf16[512,3,256]{0,2,1:T(8,128)(2,1)} %copy.58), kind=kOutput, calls=%fused_computation.38 | convolution fusion | flops 1612709888 | bytes 11280384 | tf_op jit(solution)/shard_map/dot_general | solution.py:149
  196.1 4.3 %fusion.4 = bf16[2048,256]{1,0:T(8,128)(2,1)} fusion(f32[2048,3,256]{2,0,1:T(8,128)} %fusion.18, f32[2048,3,256]{2,0,1:T(8,128)S(1)} %fusion.20, bf16[2048,512]{1,0:T(8,128)(2,1)S(1)} %copy-done.1, s32[]{:T(128)S(6)} %select_n.64, pred[2048]{0:T(1024)(128)(4,1)S(1)} %copy-done.10), kind=kLoop, calls=%fused_computation.19 | loop fusion | flops 8912896 | bytes 14682116 | tf_op jit(solution)/shard_map/convert_element_type | solution.py:160
  (70 shorter events, 8.1 us)
Async XLA Ops:
  7.2 81.9 %copy-start = (bf16[256,512]{1,0:T(8,128)(2,1)S(1)}, bf16[256,512]{1,0:T(8,128)(2,1)}, u32[]{:S(2)}) copy-start(bf16[256,512]{1,0:T(8,128)(2,1)} %param.36) | copy-start | bytes 786436
  8.2 0.6 copy-start.14
  11.8 47.3 %all-to-all-start.2 = ((bf16[16,1,32]{2,1,0:T(2,128)(2,1)}), bf16[16,1,32]{2,1,0:T(2,128)(2,1)S(1)}, u32[]{:S(2)}, u32[]{:S(2)}) async-start(bf16[16,1,32]{2,1,0:T(2,128)(2,1)} %convert_element_type.93), calls=%async_computation.2 | async-start | bytes 16384 | tf_op jit(solution)/shard_map/all_to_all | solution.py:132
  24.7 47.0 %copy-start.12 = (s32[512,1]{0,1:T(1,128)}, s32[512,1]{0,1:T(1,128)S(1)}, u32[]{:S(2)}) copy-start(s32[512,1]{0,1:T(1,128)S(1)} %compare_select_fusion.3) | copy-start | bytes 6148
  28.3 10.7 %copy-start.8 = (f32[128]{0:T(128)S(1)}, f32[128]{0:T(128)}, u32[]{:S(2)}) copy-start(f32[128]{0:T(128)} %param.30) | copy-start | bytes 1540
  28.4 10.7 %copy-start.9 = (f32[128]{0:T(128)S(1)}, f32[128]{0:T(128)}, u32[]{:S(2)}) copy-start(f32[128]{0:T(128)} %param.29) | copy-start | bytes 1540
  39.0 11.1 %copy-start.7 = (bf16[128,64]{0,1:T(8,128)(2,1)S(1)}, bf16[128,64]{0,1:T(8,128)(2,1)}, u32[]{:S(2)}) copy-start(bf16[128,64]{0,1:T(8,128)(2,1)} %param.24) | copy-start | bytes 49156
  39.0 11.3 %copy-start.3 = (bf16[512,3,256]{2,0,1:T(8,128)(2,1)S(1)}, bf16[512,3,256]{2,0,1:T(8,128)(2,1)}, u32[]{:S(2)}) copy-start(bf16[512,3,256]{2,0,1:T(8,128)(2,1)} %param.40) | copy-start | bytes 2359300
  49.8 4.0 %copy-start.1 = (bf16[2048,512]{1,0:T(8,128)(2,1)S(1)}, bf16[2048,512]{1,0:T(8,128)(2,1)}, u32[]{:S(2)}) copy-start(bf16[2048,512]{1,0:T(8,128)(2,1)} %param.21) | copy-start | bytes 6291460
  59.0 21.5 %all-to-all-start = ((bf16[16,32,512]{2,1,0:T(8,128)(2,1)}), bf16[16,32,512]{2,1,0:T(8,128)(2,1)S(1)}, u32[]{:S(2)}, u32[]{:S(2)}) async-start(bf16[16,32,512]{2,1,0:T(8,128)(2,1)} %bitcast.3), calls=%async_computation | async-start | bytes 1048576 | tf_op jit(solution)/shard_map/all_to_all | solution.py:47
  80.5 18.3 %all-to-all-start.1 = ((bf16[16,32,512]{2,1,0:T(8,128)(2,1)}), bf16[16,32,512]{2,1,0:T(8,128)(2,1)S(1)}, u32[]{:S(2)}, u32[]{:S(2)}) async-start(bf16[16,32,512]{2,1,0:T(8,128)(2,1)} %bitcast.74), calls=%async_computation.1 | async-start | bytes 1048576 | tf_op jit(solution)/shard_map/all_to_all | solution.py:46
  84.4 79.5 %all-reduce.3.cloned.1.call-start = ((), (), s32[]{:S(2)}) async-start(), calls=%async_computation.4 | async-start | bytes 1048576 | tf_op jit(solution)/shard_map/psum | solution.py:121
  86.5 5.0 %copy-start.5 = (bf16[64,512]{1,0:T(8,128)(2,1)S(1)}, bf16[64,512]{1,0:T(8,128)(2,1)}, u32[]{:S(2)}) copy-start(bf16[64,512]{1,0:T(8,128)(2,1)} %param.38) | copy-start | bytes 196612
  89.1 3.1 %copy-start.6 = (bf16[64,512]{1,0:T(8,128)(2,1)S(1)}, bf16[64,512]{1,0:T(8,128)(2,1)}, u32[]{:S(2)}) copy-start(bf16[64,512]{1,0:T(8,128)(2,1)} %param.39) | copy-start | bytes 196612
  90.3 3.0 %copy-start.2 = (bf16[256,512]{1,0:T(8,128)(2,1)S(1)}, bf16[256,512]{1,0:T(8,128)(2,1)}, u32[]{:S(2)}) copy-start(bf16[256,512]{1,0:T(8,128)(2,1)} %gather_fusion.1) | copy-start | bytes 786436
  91.5 1.8 copy-start.13
  137.3 5.4 %copy-start.4 = (bf16[640,256]{1,0:T(8,128)(2,1)S(1)}, bf16[640,256]{1,0:T(8,128)(2,1)}, u32[]{:S(2)}) copy-start(bf16[640,256]{1,0:T(8,128)(2,1)} %param.33) | copy-start | bytes 983044
  167.6 18.2 %all-to-all-start.3 = ((bf16[16,32,512]{2,1,0:T(8,128)(2,1)}), bf16[16,32,512]{2,1,0:T(8,128)(2,1)S(1)}, u32[]{:S(2)}, u32[]{:S(2)}) async-start(bf16[16,32,512]{2,1,0:T(8,128)(2,1)} %bitcast.76), calls=%async_computation.3 | async-start | bytes 1048576 | tf_op jit(solution)/shard_map/all_to_all | solution.py:125
  185.8 6.0 %copy-start.11 = (f32[2048]{0:T(1024)S(1)}, f32[2048]{0:T(1024)}, u32[]{:S(2)}) copy-start(f32[2048]{0:T(1024)} %broadcast_maximum_fusion) | copy-start | bytes 24580
  191.8 4.3 %copy-start.10 = (pred[2048]{0:T(1024)(128)(4,1)S(1)}, pred[2048]{0:T(1024)(128)(4,1)}, u32[]{:S(2)}) copy-start(pred[2048]{0:T(1024)(128)(4,1)} %broadcast_compare_fusion) | copy-start | bytes 6148
Sparse Core Ops, SparseCore 0:
  93.4 20.0 all-reduce.2
where the time goes:
time: 209 us; the launch traced here: 207 us
  local copies, waits for them, and re-layouts  57 us (27%)
  matrix products  52.7 us (25%)
  other arithmetic  41.4 us (20%)
  starting transfers between devices  23.2 us (11%)
  between operations  14.4 us (7%)
  waiting for transfers between devices  13.3 us (6%)
  blocking collectives  5.32 us (3%)
    gather x1, local copies, waits for them, and re-layouts, per_device(): nbrs = flat[nbr_slot].reshape(-1, width)  17.3 us
    unnamed x2, other arithmetic  15.9 us
    dot_general x1, matrix products, per_device(): jnp.dot(te_nbr, w_value[width:], preferred_element_type=jnp.float32)  10.7 us
    dot_general x1, matrix products, per_device(): jnp.dot(te_nbr, w_key[width:], preferred_element_type=jnp.float32)  10.7 us
    all_to_all x1, starting transfers between devices, per_device(): lax.all_to_all(slot_count.reshape(peers, cap_self).astype(jnp.bfloat16),...  8.31 us
    unnamed x36, local copies, waits for them, and re-layouts  7.57 us
    reshape x1, local copies, waits for them, and re-layouts, per_device(): kh = keys.reshape(-1, neigh, local_heads, head_size)  7.07 us
    reshape x1, local copies, waits for them, and re-layouts, per_device(): vh = values.reshape(-1, neigh, local_heads, head_size)  7.06 us
  transfers between devices with their start and end apart: 5, of which 3 were waited for; matrix products, arithmetic and copies ran while one was open for 62% of the time, Pallas kernels for 0%

commit v1 on v0

v1 whole, which is shorter than its diff:
```python
import functools

import jax
import jax.numpy as jnp
from jax import lax
from jax.experimental import pallas as pl
from jax.experimental.pallas import tpu as pltpu
from jax.sharding import PartitionSpec as P

HEADS = 8
GROUP = 16
BF = jnp.bfloat16
F32 = jnp.float32
I32 = jnp.int32
VMEM = pl.BlockSpec(memory_space=pltpu.VMEM)
TURN = 6.283185307179586
COS = (
    6.52861337,
    -25.9675685,
    60.1676231,
    -85.4501386,
    64.9391174,
    -19.7392045,
    0.999999989,
)


def dot(a, b):
    return jnp.dot(a, b, preferred_element_type=F32)


def dot_nt(a, b):
    return lax.dot_general(a, b, (((1,), (1,)), ((), ())), preferred_element_type=F32)


def iota(shape, dim):
    return lax.broadcasted_iota(I32, shape, dim)


def one_hot(mask):
    return jnp.where(mask, 1.0, 0.0).astype(BF)


def params():
    return pltpu.CompilerParams(vmem_limit_bytes=48 * 1024 * 1024)


def cost(flops, size):
    return pl.CostEstimate(flops=int(flops), bytes_accessed=int(size), transcendentals=0)


def split(serve):
    high = lax.shift_right_logical(serve, 8)
    low = jnp.bitwise_and(serve, 255)
    return high.astype(F32).astype(BF), low.astype(F32).astype(BF)


def column(serve, start, count):
    peers, cap = serve.shape
    high, low = split(serve)
    pick = one_hot((iota((count, peers), 0) + start) // cap == iota((count, peers), 1))
    every = 256.0 * dot(pick, high) + dot(pick, low)
    mine = (iota((count, cap), 0) + start) % cap == iota((count, cap), 1)
    return jnp.sum(jnp.where(mine, every, 0.0), axis=1, keepdims=True)


def row(serve):
    peers, cap = serve.shape
    slots = peers * cap
    high, low = split(serve)
    pick = one_hot(iota((cap, slots), 1) % cap == iota((cap, slots), 0))
    every = 256.0 * dot(high, pick) + dot(low, pick)
    mine = iota((peers, slots), 1) // cap == iota((peers, slots), 0)
    return jnp.sum(jnp.where(mine, every, 0.0), axis=0, keepdims=True)


def rows_at(col, count):
    at = iota((col.shape[0], count), 1).astype(F32)
    return one_hot(at == col)


def half_of(core, half):
    return pl.ds(pl.multiple_of(core * half, half), half)


def serve_kernel(packed, rows_ref, self_ref, mem_ref, *outs):
    core = lax.axis_index("mp")
    count, width = mem_ref.shape
    half = width // 2
    mem = mem_ref[:, half_of(core, half)]
    done = 0
    for table, (ref, out) in enumerate(((rows_ref, outs[0]), (self_ref, outs[-1]))):
        serve = ref[0]
        peers, cap = serve.shape
        slots = peers * cap
        step = min(256, slots)
        for start in range(0, slots, step):
            picked = dot(rows_at(column(serve, start, step), count), mem).astype(BF)
            if packed:
                out[start // cap : (start + step) // cap, done : done + cap, :] = picked.reshape(
                    step // cap, cap, half
                )
            else:
                out[start : start + step, :] = picked
        done += cap


def encode_turns(x):
    turns = x * (1.0 / TURN)
    u = turns - jnp.round(turns)
    square = u * u
    total = jnp.full_like(square, COS[0])
    for factor in COS[1:]:
        total = total * square + factor
    return total


def grouped_column(block):
    return jnp.concatenate([block[:, k : k + 1] for k in range(block.shape[1])], axis=0)


def time_kernel(delta_ref, freq_ref, phase_ref, te_ref, msg_ref):
    ends, neigh = delta_ref.shape
    size = GROUP * neigh
    freq = freq_ref[...]
    phase = phase_ref[...]

    def body(g, carry):
        at = pl.ds(pl.multiple_of(g * GROUP, GROUP), GROUP)
        col = grouped_column(delta_ref[at, :])
        enc = encode_turns(col * freq + phase).astype(BF)
        te_ref[pl.ds(pl.multiple_of(g * size, size), size), :] = enc
        msg_ref[at, :] = enc[:GROUP, :]
        return carry

    lax.fori_loop(0, ends // GROUP, body, 0)


def slot_kernel(
    peers,
    slot_ref,
    slot_t_ref,
    te_ref,
    edge_ref,
    edge_x_ref,
    wt_ref,
    we_ref,
    wx_ref,
    pairs_ref,
    count_ref,
    sent_ref,
    pre_ref,
):
    core = lax.axis_index("mp")
    events = slot_ref.shape[0]
    slots, half = pre_ref.shape
    cap = slots // peers
    part = wt_ref.shape[0]
    tall = [one_hot(iota((slots, events), 0) == slot_t_ref[j : j + 1, :]) for j in range(2)]
    wide = [one_hot(iota((events, slots), 1) == slot_ref[:, j : j + 1]) for j in range(2)]
    pairs_ref[...] = (dot(tall[0], wide[1]) + dot(tall[1], wide[0])).astype(BF)
    ones = jnp.ones((events, 128), BF)
    count_ref[...] = dot(tall[0], ones) + dot(tall[1], ones)
    lane = iota((slots, 128), 1)
    place = one_hot(iota((slots, 128), 0) % cap == lane)
    spread = (count_ref[...] * place.astype(F32)).astype(BF)
    owner = one_hot(iota((peers, slots), 1) // cap == iota((peers, slots), 0))
    sent_ref[...] = dot(owner, spread)
    cols = half_of(core, half)
    wx = wx_ref[wx_ref.shape[0] - 2 * part :, cols]
    mine, theirs = wt_ref[:, cols], wx[:part]
    first = core == 0
    w_time = jnp.concatenate(
        [jnp.where(first, mine, theirs), jnp.where(first, theirs, mine)], axis=0
    )
    edge = dot(edge_ref[...], we_ref[:, cols]) + dot(edge_x_ref[...], wx[part:])
    total = jnp.zeros((slots, half), F32)
    for j in range(2):
        value = dot(te_ref[j * events : (j + 1) * events, :], w_time) + edge
        high = value.astype(BF)
        low = (value - high.astype(F32)).astype(BF)
        total = total + dot(tall[j], high) + dot(tall[j], low)
    pre_ref[...] = total


def owner_kernel(self_ref, mem_ref, whid_ref, gh_ref, same_ref, put_ref, base_ref):
    core = lax.axis_index("mp")
    count, width = mem_ref.shape
    half = width // 2
    serve = self_ref[0]
    slots = serve.size
    for start in range(0, slots, 256):
        picked = dot(rows_at(column(serve, start, 256), count), mem_ref[...]).astype(BF)
        gh_ref[start : start + 256, :] = dot(picked, whid_ref[...])
    col = column(serve, 0, slots)
    line = row(serve)
    same = col == line
    same_ref[...] = one_hot(same)
    earlier = same & (iota((slots, slots), 0) < iota((slots, slots), 1))
    again = jnp.sum(jnp.where(earlier, 1.0, 0.0), axis=0, keepdims=True)
    line = jnp.where(again > 0, -1.0, line)
    step = 256
    for start in range(0, count, step):
        at = (iota((step, slots), 0) + start).astype(F32)
        hit = jnp.where(at == line, 1.0, 0.0)
        put_ref[start : start + step, :] = hit.astype(BF)
        free = 1.0 - jnp.sum(hit, axis=1, keepdims=True)
        old = mem_ref[start : start + step, half_of(core, half)].astype(F32)
        base_ref[start : start + step, :] = (old * free).astype(BF)


def part_of(ref, packed, start, size):
    if packed:
        return ref[:, start : start + size, :].reshape(-1, ref.shape[2])
    return ref[...]


def message_kernel(
    packed,
    cap,
    cap_self,
    own_ref,
    oth_ref,
    ws_ref,
    wo_ref,
    wx_ref,
    pairs_ref,
    count_ref,
    sent_ref,
    pre_ref,
    out_ref,
):
    core = lax.axis_index("mp")
    half = ws_ref.shape[0]
    cols = half_of(core, half)
    own = part_of(own_ref, packed, cap, cap_self)
    oth = part_of(oth_ref, packed, cap, cap_self)
    other = dot(own, wo_ref[:, cols]) + dot(oth, wx_ref[half : 2 * half, cols])
    mine = dot(own, ws_ref[:, cols]) + dot(oth, wx_ref[:half, cols])
    count = jnp.concatenate([count_ref[...]] * (half // 128), axis=1)
    total = dot(pairs_ref[...], other.astype(BF)) + count * mine + pre_ref[...]
    out = total.astype(BF)
    if not packed:
        out_ref[...] = out
        return
    peers = out.shape[0] // cap_self
    tiles = half // 128
    for tile in range(tiles):
        out_ref[:, tile * cap_self : (tile + 1) * cap_self, :] = out[
            :, tile * 128 : (tile + 1) * 128
        ].reshape(peers, cap_self, 128)
    sent = sent_ref[...]
    out_ref[:, tiles * cap_self :, :] = jnp.broadcast_to(sent[:, None, :], (peers, 16, 128)).astype(
        BF
    )


def attention_kernel(
    packed,
    cap,
    cap_self,
    nown_ref,
    noth_ref,
    sown_ref,
    soth_ref,
    slot_ref,
    nslot_ref,
    te_ref,
    phase_ref,
    wq_ref,
    wk_ref,
    wv_ref,
    wout_ref,
    wself_ref,
    emb_ref,
    kv_w,
    att_ref,
):
    core = lax.axis_index("mp")
    half = wout_ref.shape[0]
    width = 2 * half
    mine, theirs = half_of(core, half), half_of(1 - core, half)
    fown = part_of(nown_ref, packed, 0, cap)
    foth = part_of(noth_ref, packed, 0, cap)
    slots = fown.shape[0]
    for place, ref in enumerate((wk_ref, wv_ref)):
        cols = slice(place * half, (place + 1) * half)
        kv_w[:slots, cols] = (dot(fown, ref[mine, :]) + dot(foth, ref[theirs, :])).astype(BF)
        kv_w[slots:, cols] = ref[width:, :]
    xown = part_of(sown_ref, packed, cap, cap_self)
    xoth = part_of(soth_ref, packed, cap, cap_self)
    te_self = encode_turns(phase_ref[...]).astype(BF)
    te_self = jnp.broadcast_to(te_self, (16, te_self.shape[1]))
    query = dot(xown, wq_ref[mine, :]) + dot(xoth, wq_ref[theirs, :])
    query = (query + dot(te_self, wq_ref[width:, :])[:1]).astype(BF)
    ends, neigh = nslot_ref.shape
    events = ends // 2
    at = iota((events, xown.shape[0]), 1)
    find = jnp.concatenate([one_hot(at == slot_ref[:, j : j + 1]) for j in range(2)], axis=0)
    q = (dot(find, query) * (1.0 / (width // HEADS) ** 0.5)).astype(BF)
    heads = HEADS // 2
    size = width // HEADS
    tall = heads * GROUP
    pick = iota((tall, half), 1) // size == iota((tall, half), 0) // GROUP
    pairs = GROUP * neigh
    member = iota((tall, pairs), 1) % GROUP == iota((tall, pairs), 0) % GROUP
    lanes = iota((pairs, slots), 1)
    att_ref[...] = q

    def body(g, carry):
        at = pl.ds(pl.multiple_of(g * GROUP, GROUP), GROUP)
        col = grouped_column(nslot_ref[at, :])
        te = te_ref[pl.ds(pl.multiple_of(g * pairs, pairs), pairs), :]
        left = jnp.concatenate([one_hot(lanes == col), te], axis=1)
        kv = dot(left, kv_w[...]).astype(BF)
        q4 = jnp.concatenate([att_ref[at, :]] * heads, axis=0)
        q4 = jnp.where(pick, q4, jnp.zeros_like(q4))
        score = dot_nt(q4, kv[:, :half])
        expo = jnp.where(member, jnp.exp(score), 0.0)
        weights = (expo / jnp.sum(expo, axis=1, keepdims=True)).astype(BF)
        mixed = jnp.where(pick, dot(weights, kv[:, half:]), 0.0)
        att = sum(mixed[h * GROUP : (h + 1) * GROUP] for h in range(heads))
        att_ref[at, :] = att.astype(BF)
        return carry

    lax.fori_loop(0, ends // GROUP, body, 0)
    self_own = dot(find, xown).astype(BF)
    emb_ref[...] = dot(att_ref[...], wout_ref[...]) + dot(self_own, wself_ref[...])


def update_kernel(
    packed,
    cap_self,
    own_ref,
    oth_ref,
    cnt_ref,
    same_ref,
    win_ref,
    gh_ref,
    old_ref,
    put_ref,
    base_ref,
    out_ref,
):
    core = lax.axis_index("mp")
    half = base_ref.shape[1]
    slots = same_ref.shape[0]
    tiles = half // 128

    def messages(ref):
        if not packed:
            return ref[...]
        return jnp.concatenate(
            [
                ref[:, tile * cap_self : (tile + 1) * cap_self, :].reshape(slots, 128)
                for tile in range(tiles)
            ],
            axis=1,
        )

    peers = slots // cap_self
    counts = cnt_ref[:, tiles * cap_self :, :][:, 0, :] if packed else cnt_ref[...]
    spread = dot(one_hot(iota((slots, peers), 0) // cap_self == iota((slots, peers), 1)), counts)
    lane = iota((slots, 128), 1)
    spread = jnp.where(iota((slots, 128), 0) % cap_self == lane, spread, 0.0).astype(BF)
    same = same_ref[...]
    count = jnp.sum(dot(same, spread), axis=1, keepdims=True)
    inverse = 1.0 / jnp.maximum(count, 1.0)
    own = (dot(same, messages(own_ref)) * inverse).astype(BF)
    oth = (dot(same, messages(oth_ref)) * inverse).astype(BF)
    gi = dot(own, win_ref[half_of(core, half), :]) + dot(oth, win_ref[half_of(1 - core, half), :])
    gh = gh_ref[...]
    reset = jax.nn.sigmoid(gi[:, :half] + gh[:, :half])
    gate = jax.nn.sigmoid(gi[:, half : 2 * half] + gh[:, half : 2 * half])
    cand = jnp.tanh(gi[:, 2 * half :] + reset * gh[:, 2 * half :])
    old = old_ref[:, old_ref.shape[1] - cap_self :, :].reshape(slots, half) if packed else old_ref[...]
    old = old.astype(F32)
    fresh = jnp.where(count > 0, (1.0 - gate) * cand + gate * old, old).astype(BF)
    step = 256
    for start in range(0, base_ref.shape[0], step):
        at = slice(start, start + step)
        put = dot(put_ref[at, :], fresh)
        out_ref[at, :] = (base_ref[at, :].astype(F32) + put).astype(BF)


def per_device(
    memory,
    ev_time,
    nbr_time,
    edge_feat,
    self_slot,
    nbr_slot,
    serve_self,
    serve_rows,
    freq,
    phase,
    w_query,
    w_key,
    w_value,
    w_out,
    w_self,
    w_msg_self,
    w_msg_other,
    w_msg_time,
    w_msg_edge,
    w_in,
    w_hid,
):
    owned, width = memory.shape
    half = w_out.shape[0]
    peers, cap = serve_rows.shape[1:]
    cap_self = serve_self.shape[2]
    events, _, neigh = nbr_slot.shape
    ends = 2 * events
    tdim = freq.shape[0]
    slots_n, slots_s = peers * cap, peers * cap_self
    packed = cap % 16 == 0 and cap_self % 16 == 0
    shape = jax.ShapeDtypeStruct

    def call(kernel, out_shape, args, flops=0, scratch=()):
        outs = out_shape if isinstance(out_shape, (list, tuple)) else [out_shape]
        size = sum(a.size * a.dtype.itemsize for a in (*args, *outs))
        return pl.pallas_call(
            kernel,
            out_shape=out_shape,
            in_specs=[VMEM] * len(args),
            out_specs=jax.tree.map(lambda _: VMEM, out_shape),
            scratch_shapes=list(scratch),
            compiler_params=params(),
            cost_estimate=cost(flops, size),
        )(*args)

    def swap(x):
        return lax.ppermute(x, "mp", [(0, 1), (1, 0)])

    def exchange(x):
        return lax.all_to_all(x, "nodes", split_axis=0, concat_axis=0, tiled=True)

    flops_serve = 2 * (slots_n + slots_s) * owned * half
    if packed:
        served = call(
            functools.partial(serve_kernel, True),
            shape((peers, cap + cap_self, half), BF),
            (serve_rows, serve_self, memory),
            flops_serve,
        )
        old = served
    else:
        served_n, old = call(
            functools.partial(serve_kernel, False),
            [shape((slots_n, half), BF), shape((slots_s, half), BF)],
            (serve_rows, serve_self, memory),
            flops_serve,
        )
        served = jnp.concatenate(
            [served_n.reshape(peers, cap, half), old.reshape(peers, cap_self, half)], axis=1
        )
    fetched = exchange(served)

    w_swap = swap(jnp.concatenate([w_msg_self, w_msg_other, w_msg_time, w_msg_edge], axis=0))
    edge_swap = swap(edge_feat)
    slot_t = self_slot.T
    delta = (ev_time[:, None, None] - nbr_time).astype(F32).transpose(1, 0, 2).reshape(ends, neigh)
    nslot = nbr_slot.transpose(1, 0, 2).reshape(ends, neigh)
    te, te_msg = call(
        time_kernel,
        [shape((ends * neigh, tdim), BF), shape((ends, tdim), BF)],
        (delta, freq[None], phase[None]),
        ends * neigh * tdim * 40,
    )
    pairs, count, sent, pre = call(
        functools.partial(slot_kernel, peers),
        [
            shape((slots_s, slots_s), BF),
            shape((slots_s, 128), F32),
            shape((peers, 128), F32),
            shape((slots_s, half), F32),
        ],
        (
            self_slot,
            slot_t,
            te_msg,
            edge_feat,
            edge_swap,
            w_msg_time,
            w_msg_edge,
            w_swap,
        ),
        4 * slots_s * events * (slots_s + half),
    )
    gh, same, put, base = call(
        owner_kernel,
        [
            shape((slots_s, 3 * half), F32),
            shape((slots_s, slots_s), BF),
            shape((owned, slots_s), BF),
            shape((owned, half), BF),
        ],
        (serve_self, memory, w_hid.reshape(width, 3 * half)),
        2 * slots_s * (owned * width + width * 3 * half),
    )

    fetched_x = swap(fetched)
    if packed:
        nown = sown = fetched
        noth = soth = fetched_x
        back_shape = shape((peers, (half // 128) * cap_self + 16, 128), BF)
    else:
        nown, noth = (f[:, :cap].reshape(slots_n, half) for f in (fetched, fetched_x))
        sown, soth = (f[:, cap:].reshape(slots_s, half) for f in (fetched, fetched_x))
        back_shape = shape((slots_s, half), BF)
    message = call(
        functools.partial(message_kernel, packed, cap, cap_self),
        back_shape,
        (sown, soth, w_msg_self, w_msg_other, w_swap, pairs, count, sent, pre),
        2 * slots_s * half * (2 * width + slots_s),
    )
    if packed:
        back = exchange(message)
        counts = back
        back_x = swap(back)
    else:
        message = jnp.concatenate(
            [
                message.reshape(peers, cap_self, half),
                jnp.pad(sent.astype(BF), ((0, 0), (0, half - 128)))[:, None],
            ],
            axis=1,
        )
        back = exchange(message)
        back_x = swap(back)[:, :cap_self].reshape(slots_s, half)
        counts = back[:, cap_self, :128]
        back = back[:, :cap_self].reshape(slots_s, half)

    part = call(
        functools.partial(attention_kernel, packed, cap, cap_self),
        shape((ends, width), F32),
        (
            nown,
            noth,
            sown,
            soth,
            self_slot,
            nslot,
            te,
            phase[None],
            w_query,
            w_key,
            w_value,
            w_out,
            w_self,
        ),
        2 * ends * neigh * (slots_n + tdim) * width,
        [pltpu.VMEM((slots_n + tdim, 2 * half), BF), pltpu.VMEM((ends, half), BF)],
    )
    embedding = (part + swap(part)).astype(BF).reshape(2, events, width).transpose(1, 0, 2)

    memory_out = call(
        functools.partial(update_kernel, packed, cap_self),
        shape((owned, half), BF),
        (back, back_x, counts, same, w_in.reshape(width, 3 * half), gh, old, put, base),
        2 * slots_s * (slots_s * width + width * 3 * half + owned * half),
    )
    return (embedding, memory_out)


def solution(mesh):
    return jax.shard_map(
        per_device,
        mesh=mesh,
        in_specs=(
            P("nodes", None),
            P("nodes"),
            P("nodes", None, None),
            P("nodes", "mp"),
            P("nodes", None),
            P("nodes", None, None),
            P("nodes", None, None),
            P("nodes", None, None),
            P(),
            P(),
            P(None, "mp"),
            P(None, "mp"),
            P(None, "mp"),
            P("mp", None),
            P("mp", None),
            P("mp", None),
            P("mp", None),
            P("mp", None),
            P("mp", None),
            P(None, None, "mp"),
            P(None, None, "mp"),
        ),
        out_specs=(P("nodes", None, None), P("nodes", "mp")),
        check_vma=False,
    )
```

time: 209 us -> 79.3 us (0.38)
  matrix products: 52.7 us -> 0 us
  local copies, waits for them, and re-layouts: 57 us -> 14.1 us
  other arithmetic: 41.4 us -> 2 us
  Pallas kernels: 0 us -> 33.7 us
  between operations: 14.4 us -> 0.92 us
  starting transfers between devices: 23.2 us -> 13.6 us
  blocking collectives: 5.32 us -> 0 us
    dot_general x14 -> x0, matrix products: 52.7 us -> none  [the longest x1 10.7 us: per_device(): jnp.dot(te_nbr, w_value[width:], preferred_element_type=jnp.float32)]
    pallas_call x0 -> x7, Pallas kernels: none -> 33.7 us  [call(): pl.pallas_call(kernel, out_shape=out_shape, in_specs=[VMEM] * len(args),...]
    gather x5 -> x0, local copies, waits for them, and re-layouts: 25.5 us -> none  [the longest x1 17.3 us: per_device(): nbrs = flat[nbr_slot].reshape(-1, width)]
    unnamed x2 -> x0, other arithmetic: 15.9 us -> none
    reshape x5 -> x3, local copies, waits for them, and re-layouts: 16.1 us -> 1.52 us  [the longest x1 0.97 us: per_device(): (part + swap(part)).astype(BF).reshape(2, events, width).transpose(1, 0, 2)]
    scatter-add x4 -> x0, other arithmetic: 14.5 us -> none  [the longest x1 6.03 us: per_device(): total = jnp.zeros((owned, msg_width), jnp.float32).at[local_rows].add(bac...]
    all_to_all x4 -> x2, starting transfers between devices: 23 us -> 12.4 us  [exchange(): return lax.all_to_all(x, 'nodes', split_axis=0, concat_axis=0, tiled=True)]
    convert_element_type x6 -> x1, other arithmetic: 6.62 us -> 1.11 us  [per_device(): (part + swap(part)).astype(BF).reshape(2, events, width).transpose(1, 0, 2)]
  transfers between devices with their start and end apart: 5 -> 7, of which waited for: 3 -> 1; matrix products, arithmetic and copies ran while one was open for 62% -> 7% of each run, Pallas kernels for 0% -> 32%
where the time goes in v1:
time: 79.3 us; the launch traced here: 78.6 us
  Pallas kernels  33.7 us (42%)
  waiting for transfers between devices  14.2 us (18%)
  local copies, waits for them, and re-layouts  14.1 us (18%)
  starting transfers between devices  13.6 us (17%)
  other arithmetic  2 us (3%)
  between operations  0.92 us (1%)
    pallas_call x7, Pallas kernels, call(): pl.pallas_call(kernel, out_shape=out_shape, in_specs=[VMEM] * len(args),...  33.7 us
    all_to_all x2, waiting for transfers between devices, exchange(): return lax.all_to_all(x, 'nodes', split_axis=0, concat_axis=0, tiled=True)  14.2 us
    unnamed x52, local copies, waits for them, and re-layouts  12.4 us
    all_to_all x2, starting transfers between devices, exchange(): return lax.all_to_all(x, 'nodes', split_axis=0, concat_axis=0, tiled=True)  12.4 us
  transfers between devices with their start and end apart: 7, of which 1 were waited for; matrix products, arithmetic and copies ran while one was open for 7% of the time, Pallas kernels for 32%

profile of v1, /device:TPU:0, one launch (start us, length us, event | category | flops | bytes accessed | tf_op | source)
XLA Modules:
  0.0 78.6 jit_solution(10629122055166748718)
XLA Ops:
  0.7 0.0 copy-start.8
  0.7 1.6 %copy-done.8 = bf16[2048,512]{1,0:T(8,128)(2,1)S(1)} copy-done((bf16[2048,512]{1,0:T(8,128)(2,1)S(1)}, bf16[2048,512]{1,0:T(8,128)(2,1)}, u32[]{:S(2)}) %copy-start.8) | copy-done | bytes 2097176
  2.3 0.7 copy-done.16
  3.0 0.7 copy-done.17
  3.7 2.6 %shard_map.212.old_ref = bf16[16,64,256]{2,1,0:T(8,128)(2,1)} custom-call(s32[1,16,32]{2,1,0:T(8,128)S(1)} %copy-done.16, s32[1,16,32]{2,1,0:T(8,128)S(1)} %copy-done.17, bf16[2048,512]{1,0:T(8,128)(2,1)S(1)} %copy-done.8), custom_call_target="tpu_custom_call" | custom-call | flops 1073741824 | bytes 2625536 | tf_op jit(solution)/shard_map/pallas_call | solution.py:423
  6.3 0.0 copy-start.21
  6.3 0.0 copy-start.6
  6.3 0.0 copy-start.7
  6.3 8.5 %all-to-all-start = ((bf16[16,64,256]{2,1,0:T(8,128)(2,1)}), bf16[16,64,256]{2,1,0:T(8,128)(2,1)S(1)}, u32[]{:S(2)}, u32[]{:S(2)}) async-start(bf16[16,64,256]{2,1,0:T(8,128)(2,1)} %shard_map.212.old_ref), calls=%async_computation | async-start | bytes 1048576 | tf_op jit(solution)/shard_map/all_to_all | solution.py:437
  14.8 0.9 %pad_maximum_fusion = bf16[640,512]{1,0:T(8,128)(2,1)} fusion(bf16[64,512]{1,0:T(8,128)(2,1)S(1)} %copy-done.3, bf16[64,512]{1,0:T(8,128)(2,1)S(1)} %copy-done.4, bf16[256,512]{1,0:T(8,128)(2,1)S(1)} %copy-done.2, bf16[256,512]{1,0:T(8,128)(2,1)S(1)} %copy-done.1), kind=kLoop, calls=%fused_computation | loop fusion | flops 2621440 | bytes 1310720 | tf_op jit(solution)/shard_map/concatenate | solution.py:460
  15.7 0.0 collective-permute-start.2
  15.7 14.2 %all-to-all-done.nown_ref.sown_ref.own_ref = bf16[16,64,256]{2,1,0:T(8,128)(2,1)S(1)} async-done(((bf16[16,64,256]{2,1,0:T(8,128)(2,1)}), bf16[16,64,256]{2,1,0:T(8,128)(2,1)S(1)}, u32[]{:S(2)}, u32[]{:S(2)}) %all-to-all-start) | async-done | bytes 524320 | tf_op jit(solution)/shard_map/all_to_all | solution.py:437
  29.9 0.0 collective-permute-start
  29.9 0.1 copy.38.edge_ref
  30.1 0.6 collective-permute-start.3
  30.6 0.1 copy.34.slot_ref
  30.8 0.1 copy.33
  30.9 0.1 copy.32
  31.0 3.5 %shard_map.213 = (bf16[4096,128]{1,0:T(8,128)(2,1)S(1)}, bf16[256,128]{1,0:T(8,128)(2,1)S(1)}) custom-call(f32[256,16]{1,0:T(8,128)S(1)} %bitcast.14, f32[1,128]{1,0:T(1,128)S(1)} %bitcast.17, f32[1,128]{1,0:T(1,128)S(1)} %bitcast.18), custom_call_target="tpu_custom_call" | custom-call | flops 20971520 | bytes 1131520 | tf_op jit(solution)/shard_map/pallas_call | solution.py:423
  34.5 0.0 copy-start.9
  34.5 1.0 %copy-done.9 = bf16[4096,128]{1,0:T(8,128)(2,1)} copy-done((bf16[4096,128]{1,0:T(8,128)(2,1)}, bf16[4096,128]{1,0:T(8,128)(2,1)S(1)}, u32[]{:S(2)}) %copy-start.9) | copy-done | bytes 1048600
  35.5 0.0 collective-permute-done.3.edge_x_ref
  35.5 0.0 collective-permute-done.2.wx_ref
  35.5 1.8 %shard_map.215 = (bf16[512,512]{1,0:T(8,128)(2,1)S(1)}, f32[512,128]{1,0:T(8,128)S(1)}, f32[16,128]{1,0:T(8,128)S(1)}, f32[512,256]{1,0:T(8,128)S(1)}) custom-call(s32[128,2]{1,0:T(8,128)S(1)} %copy.34.slot_ref, s32[2,128]{1,0:T(2,128)S(1)} %bitcast.16, bf16[256,128]{1,0:T(8,128)(2,1)S(1)} %get-tuple-element.13.te_ref, bf16[128,64]{1,0:T(8,128)(2,1)S(1)} %copy.38.edge_ref, ...), custom_call_target="tpu_custom_call" | custom-call | flops 201326592 | bytes 2205696 | tf_op jit(solution)/shard_map/pallas_call | solution.py:423
  37.2 0.0 collective-permute-done.noth_ref.soth_ref.oth_ref
  37.3 0.0 copy-start.11
  37.3 1.4 %shard_map.216 = bf16[16,80,128]{2,1,0:T(8,128)(2,1)} custom-call(bf16[16,64,256]{2,1,0:T(8,128)(2,1)S(1)} %all-to-all-done.nown_ref.sown_ref.own_ref, bf16[16,64,256]{2,1,0:T(8,128)(2,1)S(1)} %collective-permute-done.noth_ref.soth_ref.oth_ref, bf16[256,512]{1,0:T(8,128)(2,1)S(1)} %copy-done.1, bf16[256,512]{1,0:T(8,128)(2,1)S(1)} %copy-done.2, ...), custom_call_target="tpu_custom_call" | custom-call | flops 402653184 | bytes 3874816 | tf_op jit(solution)/shard_map/pallas_call | solution.py:423
  38.6 3.9 %all-to-all-start.1 = ((bf16[16,80,128]{2,1,0:T(8,128)(2,1)}), bf16[16,80,128]{2,1,0:T(8,128)(2,1)S(1)}, u32[]{:S(2)}, u32[]{:S(2)}) async-start(bf16[16,80,128]{2,1,0:T(8,128)(2,1)} %shard_map.216), calls=%async_computation.1 | async-start | bytes 655360 | tf_op jit(solution)/shard_map/all_to_all | solution.py:437
  42.6 0.0 copy-start.10
  42.6 1.2 %copy-done.10 = bf16[4096,128]{1,0:T(8,128)(2,1)S(1)} copy-done((bf16[4096,128]{1,0:T(8,128)(2,1)S(1)}, bf16[4096,128]{1,0:T(8,128)(2,1)}, u32[]{:S(2)}) %copy-start.10) | copy-done | bytes 1048600
  43.8 1.0 %copy-done.12 = bf16[640,256]{1,0:T(8,128)(2,1)S(1)} copy-done((bf16[640,256]{1,0:T(8,128)(2,1)S(1)}, bf16[640,256]{1,0:T(8,128)(2,1)}, u32[]{:S(2)}) %copy-start.12) | copy-done | bytes 327704
  44.8 1.0 %copy-done.13 = bf16[640,256]{1,0:T(8,128)(2,1)S(1)} copy-done((bf16[640,256]{1,0:T(8,128)(2,1)S(1)}, bf16[640,256]{1,0:T(8,128)(2,1)}, u32[]{:S(2)}) %copy-start.13) | copy-done | bytes 327704
  45.7 0.9 %copy-done.14 = bf16[256,512]{1,0:T(8,128)(2,1)S(1)} copy-done((bf16[256,512]{1,0:T(8,128)(2,1)S(1)}, bf16[256,512]{1,0:T(8,128)(2,1)}, u32[]{:S(2)}) %copy-start.14) | copy-done | bytes 262168
  46.7 0.9 %copy-done.15 = bf16[256,512]{1,0:T(8,128)(2,1)S(1)} copy-done((bf16[256,512]{1,0:T(8,128)(2,1)S(1)}, bf16[256,512]{1,0:T(8,128)(2,1)}, u32[]{:S(2)}) %copy-start.15) | copy-done | bytes 262168
  47.6 14.9 %shard_map.214 = f32[256,512]{1,0:T(8,128)S(1)} custom-call(bf16[16,64,256]{2,1,0:T(8,128)(2,1)S(1)} %all-to-all-done.nown_ref.sown_ref.own_ref, bf16[16,64,256]{2,1,0:T(8,128)(2,1)S(1)} %collective-permute-done.noth_ref.soth_ref.oth_ref, bf16[16,64,256]{2,1,0:T(8,128)(2,1)S(1)} %all-to-all-done.nown_ref.sown_ref.own_ref, ...), custom_call_target="tpu_custom_call" | custom-call | flops 2684354560 | bytes 5195264 | tf_op jit(solution)/shard_map/pallas_call | solution.py:423
  62.6 0.1 collective-permute-start.1
  62.7 0.3 copy.41
  63.0 0.3 copy.42.win_ref
  63.2 0.0 copy-start.18
  63.3 1.4 %copy.39 = bf16[512,3,256]{0,2,1:T(8,128)(2,1)S(1)} copy(bf16[512,3,256]{2,0,1:T(8,128)(2,1)} %param.41) | data formatting | bytes 1572864 | tf_op args[20]
  64.7 0.3 copy.40.whid_ref
  65.0 0.6 collective-permute-start.4
  65.5 4.8 %shard_map.217 = (f32[512,768]{1,0:T(8,128)S(1)}, bf16[512,512]{1,0:T(8,128)(2,1)S(1)}, bf16[2048,512]{1,0:T(8,128)(2,1)S(1)}, bf16[2048,256]{1,0:T(8,128)(2,1)S(1)}) custom-call(s32[1,16,32]{2,1,0:T(8,128)S(1)} %copy-done.18, bf16[2048,512]{1,0:T(8,128)(2,1)} %mem_ref.3, bf16[512,768]{1,0:T(8,128)(2,1)S(1)} %copy.40.whid_ref), custom_call_target="tpu_custom_call" | custom-call | flops 1476395008 | bytes 8128512 | tf_op jit(solution)/shard_map/pallas_call | solution.py:423
  70.3 1.3 %copy-done = bf16[2048,512]{1,0:T(8,128)(2,1)} copy-done((bf16[2048,512]{1,0:T(8,128)(2,1)}, bf16[2048,512]{1,0:T(8,128)(2,1)S(1)}, u32[]{:S(2)}) %copy-start) | copy-done | bytes 2097176
  71.6 0.0 collective-permute-done.1
  71.6 1.1 %add_convert_fusion = bf16[256,512]{1,0:T(8,128)(2,1)S(1)} fusion(f32[256,512]{1,0:T(8,128)S(1)} %shard_map.214, f32[256,512]{1,0:T(8,128)} %collective-permute-done.1), kind=kLoop, calls=%fused_computation.1 | loop fusion | flops 262144 | bytes 1310720 | tf_op jit(solution)/shard_map/convert_element_type | solution.py:556
  72.8 1.0 %copy.44 = bf16[2,128,512]{2,0,1:T(2,128)(2,1)} copy(bf16[2,128,512]{2,1,0:T(8,128)(2,1)S(1)} %bitcast.22) | data formatting | bytes 524288 | tf_op jit(solution)/shard_map/reshape | solution.py:556
  73.7 4.8 %shard_map.218 = bf16[2048,256]{1,0:T(8,128)(2,1)} custom-call(bf16[16,80,128]{2,1,0:T(8,128)(2,1)S(1)} %all-to-all-done.1.own_ref.cnt_ref, bf16[16,80,128]{2,1,0:T(8,128)(2,1)S(1)} %collective-permute-done.4.oth_ref, bf16[16,80,128]{2,1,0:T(8,128)(2,1)S(1)} %all-to-all-done.1.own_ref.cnt_ref, bf16[512,512]{1,0:T(8,128)(2,1)S(1)} %get-tuple-element.18.same_ref, ...), custom_call_target="tpu_custom_call" | custom-call | flops 1207959552 | bytes 8585216 | tf_op jit(solution)/shard_map/pallas_call | solution.py:423
  (33 shorter events, 0.1 us)
Async XLA Ops:
  0.6 14.2 %copy-start.3 = (bf16[64,512]{1,0:T(8,128)(2,1)S(1)}, bf16[64,512]{1,0:T(8,128)(2,1)}, u32[]{:S(2)}) copy-start(bf16[64,512]{1,0:T(8,128)(2,1)} %we_ref.1) | copy-start | bytes 196612
  0.6 14.2 %copy-start.4 = (bf16[64,512]{1,0:T(8,128)(2,1)S(1)}, bf16[64,512]{1,0:T(8,128)(2,1)}, u32[]{:S(2)}) copy-start(bf16[64,512]{1,0:T(8,128)(2,1)} %wt_ref.1) | copy-start | bytes 196612
  0.7 14.2 %copy-start.2 = (bf16[256,512]{1,0:T(8,128)(2,1)S(1)}, bf16[256,512]{1,0:T(8,128)(2,1)}, u32[]{:S(2)}) copy-start(bf16[256,512]{1,0:T(8,128)(2,1)} %wo_ref.1) | copy-start | bytes 786436
  0.7 14.2 %copy-start.1 = (bf16[256,512]{1,0:T(8,128)(2,1)S(1)}, bf16[256,512]{1,0:T(8,128)(2,1)}, u32[]{:S(2)}) copy-start(bf16[256,512]{1,0:T(8,128)(2,1)} %ws_ref.1) | copy-start | bytes 786436
  0.7 1.7 %copy-start.8 = (bf16[2048,512]{1,0:T(8,128)(2,1)S(1)}, bf16[2048,512]{1,0:T(8,128)(2,1)}, u32[]{:S(2)}) copy-start(bf16[2048,512]{1,0:T(8,128)(2,1)} %mem_ref.3) | copy-start | bytes 6291460
  2.3 0.7 copy-start.16
  3.0 0.7 copy-start.17
  6.3 23.6 %copy-start.20 = (bf16[128,64]{0,1:T(8,128)(2,1)S(1)}, bf16[128,64]{0,1:T(8,128)(2,1)}, u32[]{:S(2)}) copy-start(bf16[128,64]{0,1:T(8,128)(2,1)} %param.24) | copy-start | bytes 49156
  6.3 24.3 %copy-start.22 = (s32[128,2,16]{0,2,1:T(8,128)S(1)}, s32[128,2,16]{0,2,1:T(8,128)}, u32[]{:S(2)}) copy-start(s32[128,2,16]{0,2,1:T(8,128)} %param.23) | copy-start | bytes 49156
  6.3 24.3 %copy-start.23 = (s32[128]{0:T(128)S(1)}, s32[128]{0:T(128)}, u32[]{:S(2)}) copy-start(s32[128]{0:T(128)} %param.22) | copy-start | bytes 1540
  6.3 24.3 %copy-start.5 = (s32[128,2]{0,1:T(2,128)S(1)}, s32[128,2]{0,1:T(2,128)}, u32[]{:S(2)}) copy-start(s32[128,2]{0,1:T(2,128)} %param.25) | copy-start | bytes 3076
  6.3 24.6 %copy-start.21 = (s32[128,2,16]{0,2,1:T(8,128)S(1)}, s32[128,2,16]{0,2,1:T(8,128)}, u32[]{:S(2)}) copy-start(s32[128,2,16]{0,2,1:T(8,128)} %param.26) | copy-start | bytes 49156
  6.3 24.7 %copy-start.6 = (f32[128]{0:T(128)S(1)}, f32[128]{0:T(128)}, u32[]{:S(2)}) copy-start(f32[128]{0:T(128)} %param.29) | copy-start | bytes 1540
  6.3 24.7 %copy-start.7 = (f32[128]{0:T(128)S(1)}, f32[128]{0:T(128)}, u32[]{:S(2)}) copy-start(f32[128]{0:T(128)} %param.30) | copy-start | bytes 1540
  6.3 23.6 %all-to-all-start = ((bf16[16,64,256]{2,1,0:T(8,128)(2,1)}), bf16[16,64,256]{2,1,0:T(8,128)(2,1)S(1)}, u32[]{:S(2)}, u32[]{:S(2)}) async-start(bf16[16,64,256]{2,1,0:T(8,128)(2,1)} %shard_map.212.old_ref), calls=%async_computation | async-start | bytes 1048576 | tf_op jit(solution)/shard_map/all_to_all | solution.py:437
  15.7 19.8 %collective-permute-start.2 = (bf16[640,512]{1,0:T(8,128)(2,1)}, bf16[640,512]{1,0:T(8,128)(2,1)S(1)}, u32[]{:S(2)}, u32[]{:S(2)}) collective-permute-start(bf16[640,512]{1,0:T(8,128)(2,1)} %pad_maximum_fusion), channel_id=1, source_target_pairs={{0,1},{1,0},{2,3},{3,2},{4,5},{5,4},{6,7},{7,6},{8,9},{9,8},{10,11... | collective-permute-start | bytes 1966088 | tf_op jit(solution)/shard_map/ppermute | solution.py:434
  29.9 7.3 %collective-permute-start = (bf16[16,64,256]{2,1,0:T(8,128)(2,1)S(1)}, bf16[16,64,256]{2,1,0:T(8,128)(2,1)S(1)}, u32[]{:S(2)}, u32[]{:S(2)}) collective-permute-start(bf16[16,64,256]{2,1,0:T(8,128)(2,1)S(1)} %all-to-all-done.nown_ref.sown_ref.own_ref), channel_id=1, source_target_pairs={{0,1},{1,0},{2,3},{3,2},{4,5},{5,4},{6,7},{7,6},{8,9},{9,8},{10,11... | collective-permute-start | bytes 1572872 | tf_op jit(solution)/shard_map/ppermute | solution.py:434
  30.1 5.4 %collective-permute-start.3 = (bf16[128,64]{1,0:T(8,128)(2,1)S(1)}, bf16[128,64]{1,0:T(8,128)(2,1)S(1)}, u32[]{:S(2)}, u32[]{:S(2)}) collective-permute-start(bf16[128,64]{1,0:T(8,128)(2,1)S(1)} %copy.38.edge_ref), channel_id=1, source_target_pairs={{0,1},{1,0},{2,3},{3,2},{4,5},{5,4},{6,7},{7,6},{8,9},{9,8},{10,11... | collective-permute-start | bytes 49160 | tf_op jit(solution)/shard_map/ppermute | solution.py:434
  34.5 1.0 %copy-start.9 = (bf16[4096,128]{1,0:T(8,128)(2,1)}, bf16[4096,128]{1,0:T(8,128)(2,1)S(1)}, u32[]{:S(2)}) copy-start(bf16[4096,128]{1,0:T(8,128)(2,1)S(1)} %get-tuple-element.12.te_ref) | copy-start | bytes 3145732
  37.3 5.3 %copy-start.11 = (bf16[640,256]{1,0:T(8,128)(2,1)S(1)}, bf16[640,256]{1,0:T(8,128)(2,1)}, u32[]{:S(2)}) copy-start(bf16[640,256]{1,0:T(8,128)(2,1)} %wq_ref.1) | copy-start | bytes 983044
  38.6 26.3 %all-to-all-start.1 = ((bf16[16,80,128]{2,1,0:T(8,128)(2,1)}), bf16[16,80,128]{2,1,0:T(8,128)(2,1)S(1)}, u32[]{:S(2)}, u32[]{:S(2)}) async-start(bf16[16,80,128]{2,1,0:T(8,128)(2,1)} %shard_map.216), calls=%async_computation.1 | async-start | bytes 655360 | tf_op jit(solution)/shard_map/all_to_all | solution.py:437
  42.6 1.2 %copy-start.10 = (bf16[4096,128]{1,0:T(8,128)(2,1)S(1)}, bf16[4096,128]{1,0:T(8,128)(2,1)}, u32[]{:S(2)}) copy-start(bf16[4096,128]{1,0:T(8,128)(2,1)} %copy-done.9) | copy-start | bytes 3145732
  43.8 1.0 %copy-start.12 = (bf16[640,256]{1,0:T(8,128)(2,1)S(1)}, bf16[640,256]{1,0:T(8,128)(2,1)}, u32[]{:S(2)}) copy-start(bf16[640,256]{1,0:T(8,128)(2,1)} %wk_ref.1) | copy-start | bytes 983044
  44.8 1.0 %copy-start.13 = (bf16[640,256]{1,0:T(8,128)(2,1)S(1)}, bf16[640,256]{1,0:T(8,128)(2,1)}, u32[]{:S(2)}) copy-start(bf16[640,256]{1,0:T(8,128)(2,1)} %wv_ref.1) | copy-start | bytes 983044
  45.7 0.9 %copy-start.14 = (bf16[256,512]{1,0:T(8,128)(2,1)S(1)}, bf16[256,512]{1,0:T(8,128)(2,1)}, u32[]{:S(2)}) copy-start(bf16[256,512]{1,0:T(8,128)(2,1)} %wout_ref.1) | copy-start | bytes 786436
  46.7 0.9 %copy-start.15 = (bf16[256,512]{1,0:T(8,128)(2,1)S(1)}, bf16[256,512]{1,0:T(8,128)(2,1)}, u32[]{:S(2)}) copy-start(bf16[256,512]{1,0:T(8,128)(2,1)} %wself_ref.1) | copy-start | bytes 786436
  47.6 15.0 %copy-start.19 = (bf16[512,3,256]{2,0,1:T(8,128)(2,1)S(1)}, bf16[512,3,256]{2,0,1:T(8,128)(2,1)}, u32[]{:S(2)}) copy-start(bf16[512,3,256]{2,0,1:T(8,128)(2,1)} %param.40) | copy-start | bytes 2359300
  62.6 9.1 %collective-permute-start.1 = (f32[256,512]{1,0:T(8,128)S(1)}, f32[256,512]{1,0:T(8,128)}, u32[]{:S(2)}, u32[]{:S(2)}) collective-permute-start(f32[256,512]{1,0:T(8,128)S(1)} %shard_map.214), channel_id=1, source_target_pairs={{0,1},{1,0},{2,3},{3,2},{4,5},{5,4},{6,7},{7,6},{8,9},{9,8},{10,11... | collective-permute-start | bytes 1572872 | tf_op jit(solution)/shard_map/ppermute | solution.py:434
  63.2 2.3 %copy-start.18 = (s32[1,16,32]{2,1,0:T(8,128)S(1)}, s32[1,16,32]{2,1,0:T(8,128)}, u32[]{:S(2)}) copy-start(s32[1,16,32]{2,1,0:T(8,128)} %self_ref.3) | copy-start | bytes 6148
  65.0 8.8 %collective-permute-start.4 = (bf16[16,80,128]{2,1,0:T(8,128)(2,1)S(1)}, bf16[16,80,128]{2,1,0:T(8,128)(2,1)S(1)}, u32[]{:S(2)}, u32[]{:S(2)}) collective-permute-start(bf16[16,80,128]{2,1,0:T(8,128)(2,1)S(1)} %all-to-all-done.1.own_ref.cnt_ref), channel_id=1, source_target_pairs={{0,1},{1,0},{2,3},{3,2},{4,5},{5,4},{6,7},{7,6},{8,9},{9,8},{10,11... | collective-permute-start | bytes 983048 | tf_op jit(solution)/shard_map/ppermute | solution.py:434
  70.3 1.3 %copy-start = (bf16[2048,512]{1,0:T(8,128)(2,1)}, bf16[2048,512]{1,0:T(8,128)(2,1)S(1)}, u32[]{:S(2)}) copy-start(bf16[2048,512]{1,0:T(8,128)(2,1)S(1)} %get-tuple-element.20.put_ref) | copy-start | bytes 6291460

commit v2 on v1

v2 whole, which is shorter than its diff:
```python
import functools

import jax
import jax.numpy as jnp
from jax import lax
from jax.experimental import pallas as pl
from jax.experimental.pallas import tpu as pltpu
from jax.sharding import PartitionSpec as P

HEADS = 8
BF = jnp.bfloat16
F32 = jnp.float32
I32 = jnp.int32
VMEM = pl.BlockSpec(memory_space=pltpu.VMEM)
HBM = pl.BlockSpec(memory_space=pltpu.HBM)
TURN = 6.283185307179586
COS = (
    6.52861337,
    -25.9675685,
    60.1676231,
    -85.4501386,
    64.9391174,
    -19.7392045,
    0.999999989,
)


def dot(a, b):
    return jnp.dot(a, b, preferred_element_type=F32)


def dot_nt(a, b):
    return lax.dot_general(a, b, (((1,), (1,)), ((), ())), preferred_element_type=F32)


def iota(shape, dim):
    return lax.broadcasted_iota(I32, shape, dim)


class Operand:
    def __init__(self, copy, ref):
        self.copy, self.ref, self.shape = copy, ref, ref.shape
        copy.start()

    def wait(self):
        if self.copy is not None:
            self.copy.wait()
            self.copy = None

    def __getitem__(self, at):
        self.wait()
        return self.ref[at]


class Result:
    def __init__(self, room, ref, sems, parts):
        self.room, self.ref, self.sems, self.parts = room, ref, sems, parts
        self.shape, self.sent = room.shape, []

    def __setitem__(self, at, value):
        self.room[at] = value

    def __getitem__(self, at):
        return self.room[at]

    def send(self, part):
        size = self.shape[0] // self.parts
        at = pl.ds(part * size, size)
        copy = pltpu.make_async_copy(self.room.at[at], self.ref.at[at], self.sems.at[part])
        copy.start()
        self.sent.append((part, copy))

    def finish(self):
        done = [part for part, _ in self.sent]
        for part in range(self.parts):
            if part not in done:
                self.send(part)
        for _, copy in self.sent:
            copy.wait()


def staged(kernel, views, parts, *refs):
    count, outs = len(views), len(parts)
    ins, results, rest = refs[:count], refs[count : count + outs], list(refs[count + outs :])
    in_sems, out_sems = rest[-2:]
    rest = rest[:-2]
    operands = []
    for n, (ref, view) in enumerate(zip(ins, views)):
        if view is None:
            operands.append(ref)
        else:
            room = rest.pop(0)
            operands.append(Operand(pltpu.make_async_copy(view(ref), room, in_sems.at[n]), room))
    held = [
        Result(rest.pop(0), ref, out_sems.at[n], part)
        for n, (ref, part) in enumerate(zip(results, parts))
    ]
    kernel(*operands, *held, *rest)
    for operand in operands:
        if isinstance(operand, Operand):
            operand.wait()
    for result in held:
        result.finish()


def one_hot(mask):
    return jnp.where(mask, 1.0, 0.0).astype(BF)


def split(serve):
    high = lax.shift_right_logical(serve, 8)
    low = jnp.bitwise_and(serve, 255)
    return high.astype(F32).astype(BF), low.astype(F32).astype(BF)


def column(serve, start, count):
    peers, cap = serve.shape
    high, low = split(serve)
    pick = one_hot((iota((count, peers), 0) + start) // cap == iota((count, peers), 1))
    every = 256.0 * dot(pick, high) + dot(pick, low)
    mine = (iota((count, cap), 0) + start) % cap == iota((count, cap), 1)
    return jnp.sum(jnp.where(mine, every, 0.0), axis=1, keepdims=True)


def row(serve):
    peers, cap = serve.shape
    slots = peers * cap
    high, low = split(serve)
    pick = one_hot(iota((cap, slots), 1) % cap == iota((cap, slots), 0))
    every = 256.0 * dot(high, pick) + dot(low, pick)
    mine = iota((peers, slots), 1) // cap == iota((peers, slots), 0)
    return jnp.sum(jnp.where(mine, every, 0.0), axis=0, keepdims=True)


def rows_at(col, count):
    at = iota((col.shape[0], count), 1).astype(F32)
    return one_hot(at == col)


def half_of(core, half):
    return pl.ds(pl.multiple_of(core * half, half), half)


def serve_kernel(packed, rows_ref, self_ref, *refs):
    mems, outs, hot = refs[:4], refs[4:-1], refs[-1]
    depth, half = mems[0].shape
    count = len(mems) * depth
    step = 256
    rows, own = rows_ref[0], self_ref[0]
    jobs = []
    for table, serve in enumerate((rows, own)):
        jobs += [(start, table, serve) for start in range(0, serve.size, step)]
    jobs.sort(key=lambda job: (job[0], job[1]))
    early = hot.shape[0] // step
    for n, (start, table, serve) in enumerate(jobs[:early]):
        hot[n * step : (n + 1) * step, :] = rows_at(column(serve, start, step), count)
    for n, (start, table, serve) in enumerate(jobs):
        if n < early:
            at = hot[n * step : (n + 1) * step, :]
        else:
            at = rows_at(column(serve, start, step), count)
        picked = dot(at[:, :depth], mems[0][...])
        for part in range(1, len(mems)):
            picked = picked + dot(at[:, part * depth : (part + 1) * depth], mems[part][...])
        picked = picked.astype(BF)
        if packed:
            cap = serve.shape[1]
            first = table * rows.shape[1]
            outs[0][start // cap : (start + step) // cap, first : first + cap, :] = picked.reshape(
                step // cap, cap, half
            )
            if outs[0].parts > 1 and table == 1:
                outs[0].send(start // step)
        else:
            outs[table][start : start + step, :] = picked


def encode_turns(x):
    turns = x * (1.0 / TURN)
    u = turns - jnp.round(turns)
    square = u * u
    total = jnp.full_like(square, COS[0])
    for factor in COS[1:]:
        total = total * square + factor
    return total


def down(line, count):
    return jnp.broadcast_to(line, (count, line.shape[1])).T


def time_kernel(ev_ref, nbr_ref, freq_ref, phase_ref, wq_ref, wk_ref, wv_ref, te_ref, wqt_ref, wkvt_ref):
    neigh, tdim, ends = te_ref.shape
    events = ends // 2
    freq = down(freq_ref[...], events)
    phase = down(phase_ref[...], events)
    time = ev_ref[...]
    for k in range(neigh):
        for j in range(2):
            delta = (time - nbr_ref[j, k : k + 1, :]).astype(F32)
            enc = encode_turns(delta * freq + phase)
            te_ref[k, :, j * events : (j + 1) * events] = enc.astype(BF)
    half = wq_ref.shape[1]
    wqt_ref[...] = wq_ref[...].T
    wkvt_ref[:half, :] = wk_ref[...].T
    wkvt_ref[half:, :] = wv_ref[...].T


def tall_one_hot(slot_t_ref, slots):
    events = slot_t_ref.shape[1]
    at = iota((slots, events), 0)
    return [one_hot(at == slot_t_ref[j : j + 1, :]) for j in range(2)]


def pack_places(slots, half):
    at_pre = slots + 128
    at_weight = at_pre + 2 * half
    at_sent = at_weight + 2 * half
    return slots, at_pre, at_weight, at_sent, at_sent + 128


def slot_kernel(
    peers,
    slot_t_ref,
    te_ref,
    edge_ref,
    edge_x_ref,
    wt_ref,
    we_ref,
    ws_ref,
    wo_ref,
    wx_ref,
    pack_ref,
):
    core = lax.axis_index("mp")
    slots = pack_ref.shape[0]
    part, half = wt_ref.shape
    tall = tall_one_hot(slot_t_ref, slots)
    events = tall[0].shape[1]
    both = tall[0] + tall[1]
    at_count, at_pre, at_weight, at_sent = pack_places(slots, half)[:4]
    pack_ref[:, :at_count] = (dot_nt(tall[0], tall[1]) + dot_nt(tall[1], tall[0])).astype(BF)
    count = dot_nt(both, jnp.ones((128, events), BF))
    pack_ref[:, at_count:at_pre] = count.astype(BF)
    cap = slots // peers
    place = iota((slots, 128), 0) % cap == iota((slots, 128), 1)
    owner = one_hot(iota((peers, slots), 1) // cap == iota((peers, slots), 0))
    pack_ref[:peers, at_sent:] = dot(owner, jnp.where(place, count, 0.0).astype(BF)).astype(BF)
    pack_ref[peers:, at_sent:] = jnp.zeros((slots - peers, 128), BF)
    pack_ref[:half, at_weight : at_weight + half] = wo_ref[...]
    pack_ref[:half, at_weight + half : at_sent] = ws_ref[...]
    pack_ref[half : 2 * half, at_weight : at_weight + half] = wx_ref[half : 2 * half, :]
    pack_ref[half : 2 * half, at_weight + half : at_sent] = wx_ref[:half, :]
    mine, theirs = wt_ref[...], wx_ref[2 * half : 2 * half + part, :]
    first = core == 0
    weight = jnp.concatenate(
        [
            jnp.where(first, mine, theirs),
            jnp.where(first, theirs, mine),
            we_ref[...],
            wx_ref[2 * half + part :, :],
        ],
        axis=0,
    )
    edge = jnp.concatenate([edge_ref[...], edge_x_ref[...]], axis=0)
    value = jnp.concatenate(
        [dot_nt(jnp.concatenate(tall, axis=1), te_ref[0]), dot_nt(both, edge)], axis=1
    )
    high = value.astype(BF)
    low = (value - high.astype(F32)).astype(BF)
    pre = dot(high, weight) + dot(low, weight)
    high = pre.astype(BF)
    pack_ref[:, at_pre : at_pre + half] = high
    pack_ref[:, at_pre + half : at_weight] = (pre - high.astype(F32)).astype(BF)


def prepare_kernel(
    self_ref,
    ev_ref,
    nbr_ref,
    freq_ref,
    phase_ref,
    mem_ref,
    whid_ref,
    wq_ref,
    wk_ref,
    wv_ref,
    gh_ref,
    te_ref,
    wqt_ref,
    wkvt_ref,
):
    time_kernel(ev_ref, nbr_ref, freq_ref, phase_ref, wq_ref, wk_ref, wv_ref, te_ref, wqt_ref, wkvt_ref)
    te_ref.send(0)
    wqt_ref.send(0)
    wkvt_ref.send(0)
    count, width = mem_ref.shape
    serve = self_ref[0]
    slots = serve.size
    col = column(serve, 0, slots)
    for start in range(0, slots, 256):
        at = slice(start, start + 256)
        picked = dot(rows_at(col[at], count), mem_ref[...]).astype(BF)
        for g in range(3):
            gh_ref[g, at, :] = dot(picked, whid_ref[g])


def place_kernel(self_ref, mem_ref, base_ref):
    count, half = mem_ref.shape
    serve = self_ref[0]
    line = row(serve)
    step = count // base_ref.parts
    for part in range(base_ref.parts):
        at = slice(part * step, (part + 1) * step)
        hit = (iota((step, serve.size), 0) + part * step).astype(F32) == line
        served = jnp.max(jnp.where(hit, 1.0, 0.0), axis=1, keepdims=True)
        base_ref[at, :] = (mem_ref[at, :].astype(F32) * (1.0 - served)).astype(BF)
        base_ref.send(part)


def part_of(ref, packed, start, size):
    if packed:
        return ref[:, start : start + size, :].reshape(-1, ref.shape[2])
    return ref[...]


def message_kernel(packed, peers, cap, cap_self, own_ref, oth_ref, pack_ref, out_ref):
    slots = pack_ref.shape[0]
    half = own_ref.shape[-1]
    at_count, at_pre, at_weight, at_sent, _ = pack_places(slots, half)
    own = part_of(own_ref, packed, cap, cap_self)
    oth = part_of(oth_ref, packed, cap, cap_self)
    weight = slice(at_weight, at_sent)
    both = dot(own, pack_ref[:half, weight]) + dot(oth, pack_ref[half : 2 * half, weight])
    count = pack_ref[:, at_count:at_pre].astype(F32)
    count = jnp.concatenate([count] * (half // 128), axis=1)
    pre = pack_ref[:, at_pre : at_pre + half].astype(F32)
    pre = pre + pack_ref[:, at_pre + half : at_weight].astype(F32)
    total = dot(pack_ref[:, :at_count], both[:, :half].astype(BF)) + count * both[:, half:] + pre
    out = total.astype(BF)
    if not packed:
        out_ref[...] = out
        return
    tiles = half // 128
    for tile in range(tiles):
        out_ref[:, tile * cap_self : (tile + 1) * cap_self, :] = out[
            :, tile * 128 : (tile + 1) * 128
        ].reshape(peers, cap_self, 128)
    sent = pack_ref[:peers, at_sent:].astype(F32)
    out_ref[:, tiles * cap_self :, :] = jnp.broadcast_to(sent[:, None, :], (peers, 16, 128)).astype(
        BF
    )


def attention_kernel(
    packed,
    cap,
    cap_self,
    *refs,
):
    own_refs, oth_refs, refs = (refs[:1], refs[1:2], refs[2:]) if packed else (
        refs[:2], refs[2:4], refs[4:]
    )
    wkvt_ref, nslot_ref, te_ref, wqt_ref, slot_t_ref, phase_ref, wout_ref, wself_ref = refs[:8]
    emb_ref, kv_w, value_ref = refs[8:]
    nown_ref, sown_ref = own_refs[0], own_refs[-1]
    noth_ref, soth_ref = oth_refs[0], oth_refs[-1]
    core = lax.axis_index("mp")
    half = wout_ref.shape[0]
    width = 2 * half
    size = width // HEADS
    heads = HEADS // 2
    mine, theirs = half_of(core, half), half_of(1 - core, half)
    fown = part_of(nown_ref, packed, 0, cap)
    foth = part_of(noth_ref, packed, 0, cap)
    slots = fown.shape[0]
    kv_w[:, :slots] = (dot_nt(wkvt_ref[:, mine], fown) + dot_nt(wkvt_ref[:, theirs], foth)).astype(BF)
    kv_w[:, slots:] = wkvt_ref[:, width:]
    xown = part_of(sown_ref, packed, cap, cap_self)
    xoth = part_of(soth_ref, packed, cap, cap_self)
    slots_s = xown.shape[0]
    te_self = encode_turns(phase_ref[...]).astype(BF)
    te_self = jnp.broadcast_to(te_self, (128, te_self.shape[1]))
    query = dot_nt(wqt_ref[:, mine], xown) + dot_nt(wqt_ref[:, theirs], xoth)
    query_te = dot_nt(wqt_ref[:, width:], te_self)
    query = (query + jnp.concatenate([query_te] * (slots_s // 128), axis=1)).astype(BF)
    find = jnp.concatenate(tall_one_hot(slot_t_ref, slots_s), axis=1)
    q = dot(query, find) * (1.0 / size**0.5)
    neigh, _, ends = te_ref.shape
    at = iota((slots, ends), 0)
    weights = []
    for k in range(neigh):
        line = jnp.concatenate([nslot_ref[j, k : k + 1, :] for j in range(2)], axis=1)
        right = jnp.concatenate([one_hot(at == line), te_ref[k]], axis=0)
        kv = dot(kv_w[...], right)
        value_ref[k] = kv[half:].astype(BF)
        score = q * kv[:half].astype(BF).astype(F32)
        score = [
            jnp.sum(score[h * size : (h + 1) * size], axis=0, keepdims=True) for h in range(heads)
        ]
        weights.append(jnp.exp(jnp.concatenate(score, axis=0)))
    total = weights[0]
    for k in range(1, neigh):
        total = total + weights[k]
    weights = [(w / total).astype(BF).astype(F32) for w in weights]
    att = []
    for h in range(heads):
        part = jnp.zeros((size, ends), F32)
        for k in range(neigh):
            value = value_ref[k, h * size : (h + 1) * size, :].astype(F32)
            part = part + weights[k][h : h + 1] * value
        att.append(part)
    att = jnp.concatenate(att, axis=0).T.astype(BF)
    events = ends // 2
    at = iota((events, slots_s), 1)
    find = [
        one_hot(at == down(slot_t_ref[j : j + 1, :].astype(F32), slots_s).astype(I32))
        for j in range(2)
    ]
    self_own = dot(jnp.concatenate(find, axis=0), xown).astype(BF)
    emb_ref[...] = (dot(att, wout_ref[...]) + dot(self_own, wself_ref[...])).astype(BF)


def sum_kernel(own_ref, oth_ref, out_ref):
    total = own_ref[...].astype(F32) + oth_ref[...].astype(F32)
    events = out_ref.shape[0]
    out_ref[...] = jnp.stack([total[:events], total[events:]], axis=1).astype(BF)


def update_kernel(
    packed,
    cap_self,
    own_ref,
    oth_ref,
    count_ref,
    serve_ref,
    win_ref,
    gh_ref,
    old_ref,
    base_ref,
    out_ref,
    put,
):
    core = lax.axis_index("mp")
    rows, half = base_ref.shape
    serve = serve_ref[0]
    slots = serve.size
    tiles = half // 128

    def messages(ref):
        if not packed:
            return ref[...]
        return jnp.concatenate(
            [
                ref[:, tile * cap_self : (tile + 1) * cap_self, :].reshape(slots, 128)
                for tile in range(tiles)
            ],
            axis=1,
        )

    line = row(serve)
    match = column(serve, 0, slots) == line
    same = one_hot(match)
    earlier = match & (iota((slots, slots), 0) < iota((slots, slots), 1))
    again = jnp.sum(jnp.where(earlier, 1.0, 0.0), axis=0, keepdims=True)
    line = jnp.where(again > 0, -1.0, line)
    step = rows // out_ref.parts
    for part in range(out_ref.parts):
        at = (iota((step, slots), 0) + part * step).astype(F32)
        put[part * step : (part + 1) * step, :] = one_hot(at == line)
    peers = slots // cap_self
    counts = count_ref[:, tiles * cap_self :, :][:, 0, :] if packed else count_ref[...]
    spread = dot(one_hot(iota((slots, peers), 0) // cap_self == iota((slots, peers), 1)), counts)
    lane = iota((slots, 128), 1)
    spread = jnp.where(iota((slots, 128), 0) % cap_self == lane, spread, 0.0).astype(BF)
    count = jnp.sum(dot(same, spread), axis=1, keepdims=True)
    inverse = 1.0 / jnp.maximum(count, 1.0)
    own = (dot(same, messages(own_ref)) * inverse).astype(BF)
    oth = (dot(same, messages(oth_ref)) * inverse).astype(BF)
    mine, theirs = half_of(core, half), half_of(1 - core, half)
    gi = [dot(own, win_ref[g, mine, :]) + dot(oth, win_ref[g, theirs, :]) for g in range(3)]
    reset = jax.nn.sigmoid(gi[0] + gh_ref[0])
    gate = jax.nn.sigmoid(gi[1] + gh_ref[1])
    cand = jnp.tanh(gi[2] + reset * gh_ref[2])
    old = old_ref[...].reshape(slots, half).astype(F32)
    fresh = jnp.where(count > 0, (1.0 - gate) * cand + gate * old, old).astype(BF)
    for part in range(out_ref.parts):
        at = slice(part * step, (part + 1) * step)
        moved = dot(put[at, :], fresh)
        out_ref[at, :] = (base_ref[at, :].astype(F32) + moved).astype(BF)
        out_ref.send(part)


def per_device(
    memory,
    ev_time,
    nbr_time,
    edge_feat,
    self_slot,
    nbr_slot,
    serve_self,
    serve_rows,
    freq,
    phase,
    w_query,
    w_key,
    w_value,
    w_out,
    w_self,
    w_msg_self,
    w_msg_other,
    w_msg_time,
    w_msg_edge,
    w_in,
    w_hid,
):
    owned, width = memory.shape
    half = w_out.shape[0]
    peers, cap = serve_rows.shape[1:]
    cap_self = serve_self.shape[2]
    events, _, neigh = nbr_slot.shape
    ends = 2 * events
    tdim = freq.shape[0]
    slots_n, slots_s = peers * cap, peers * cap_self
    packed = cap % 16 == 0 and cap_self % 16 == 0
    shape = jax.ShapeDtypeStruct

    core = lax.axis_index("mp")

    def call(kernel, out_shape, args, flops=0, scratch=(), limit=62, direct=(), views={}, parts=(), small=False):
        single = not isinstance(out_shape, (list, tuple))
        outs = [out_shape] if single else list(out_shape)
        parts = [*parts, *[1] * (len(outs) - len(parts))]
        size = sum(a.size * a.dtype.itemsize for a in (*args, *outs))
        whole, rooms = [], []
        for n, arg in enumerate(args):
            if n in direct:
                whole.append(None)
                continue
            view, room = views.get(n, (lambda ref: ref, arg.shape))
            whole.append(view)
            rooms.append(pltpu.VMEM(room, arg.dtype))
        rooms += [pltpu.VMEM(o.shape, o.dtype) for o in outs]
        return pl.pallas_call(
            functools.partial(staged, kernel, whole, parts),
            out_shape=out_shape,
            in_specs=[HBM if view else VMEM for view in whole],
            out_specs=HBM if single else [HBM] * len(outs),
            scratch_shapes=[
                *rooms,
                *scratch,
                pltpu.SemaphoreType.DMA((len(args),)),
                pltpu.SemaphoreType.DMA((len(outs), max(parts))),
            ],
            compiler_params=pltpu.CompilerParams(vmem_limit_bytes=limit * 1024 * 1024),
            cost_estimate=pl.CostEstimate(
                flops=int(flops), bytes_accessed=1 if small else int(size), transcendentals=0
            ),
        )(*args)

    def columns(rows):
        return (lambda ref: ref.at[:, half_of(lax.axis_index("mp"), half)], (rows, half))

    def stripe(part, size):
        return (
            lambda ref: ref.at[pl.ds(part * size, size), half_of(lax.axis_index("mp"), half)],
            (size, half),
        )

    def swap(x):
        return lax.ppermute(x, "mp", [(0, 1), (1, 0)])

    def exchange(x):
        return lax.all_to_all(x, "nodes", split_axis=0, concat_axis=0, tiled=True)

    flops_serve = 2 * (slots_n + slots_s) * owned * half
    if packed:
        served_shape = shape((peers, cap + cap_self, half), BF)
    else:
        served_shape = [shape((slots_n, half), BF), shape((slots_s, half), BF)]
    quarter = owned // 4
    served = call(
        functools.partial(serve_kernel, packed),
        served_shape,
        (serve_rows, serve_self, *[memory] * 4),
        flops_serve,
        [pltpu.VMEM((512, owned), BF)],
        views={2 + n: stripe(n, quarter) for n in range(4)},
        parts=[slots_s // 256] if packed and cap == cap_self else (),
    )
    if packed:
        old = served
        old_view = (lambda ref: ref.at[:, pl.ds(cap, cap_self), :], (peers, cap_self, half))
    else:
        served_n, old = served
        old_view = (lambda ref: ref, old.shape)
        served = jnp.concatenate(
            [served_n.reshape(peers, cap, half), old.reshape(peers, cap_self, half)], axis=1
        )
    fetched = exchange(served)

    away = lax.dynamic_slice_in_dim(
        jnp.concatenate([w_msg_self, w_msg_other, w_msg_time, w_msg_edge], axis=0),
        (1 - core) * half,
        half,
        1,
    )
    w_swap = swap(away)
    edge_t = edge_feat.T
    edge_swap = swap(edge_t)
    nslot = nbr_slot.transpose(1, 2, 0)
    slot_t = self_slot.T
    gh, te, wq_t, wkv_t = call(
        prepare_kernel,
        [
            shape((3, slots_s, half), F32),
            shape((neigh, tdim, ends), BF),
            shape((half, width + tdim), BF),
            shape((2 * half, width + tdim), BF),
        ],
        (
            serve_self,
            ev_time[None],
            nbr_time.transpose(1, 2, 0),
            freq[None],
            phase[None],
            memory,
            w_hid.transpose(1, 0, 2),
            w_query,
            w_key,
            w_value,
        ),
        2 * slots_s * (owned * width + width * 3 * half),
    )
    tpart = w_msg_time.shape[0]
    pack = call(
        functools.partial(slot_kernel, peers),
        shape((slots_s, pack_places(slots_s, half)[-1]), BF),
        (
            slot_t,
            te,
            edge_t,
            edge_swap,
            w_msg_time,
            w_msg_edge,
            w_msg_self,
            w_msg_other,
            w_swap,
        ),
        4 * slots_s * events * (slots_s + half),
        views={
            1: (lambda ref: ref.at[pl.ds(0, 1)], (1, tdim, ends)),
            4: columns(tpart),
            5: columns(w_msg_edge.shape[0]),
            6: columns(half),
            7: columns(half),
        },
    )
    base = call(
        place_kernel,
        shape((owned, half), BF),
        (serve_self, memory),
        0,
        views={1: columns(owned)},
        parts=[8],
    )

    fetched, te, pack, gh, base = lax.optimization_barrier((fetched, te, pack, gh, base))
    fetched_x = swap(fetched)
    if packed:
        both = (fetched, fetched_x)
        mine = (fetched, fetched_x)
        back_shape = shape((peers, (half // 128) * cap_self + 16, 128), BF)
    else:
        nbr = [f[:, :cap].reshape(slots_n, half) for f in (fetched, fetched_x)]
        mine = [f[:, cap:].reshape(slots_s, half) for f in (fetched, fetched_x)]
        both = (nbr[0], mine[0], nbr[1], mine[1])
        back_shape = shape((slots_s, half), BF)
    message = call(
        functools.partial(message_kernel, packed, peers, cap, cap_self),
        back_shape,
        (*mine, pack),
        2 * slots_s * half * (2 * width + slots_s),
        direct=(0, 1, 2),
        limit=50,
    )
    message, slot_t2 = lax.optimization_barrier((message, slot_t))
    part = call(
        functools.partial(attention_kernel, packed, cap, cap_self),
        shape((ends, width), BF),
        (*both, wkv_t, nslot, te, wq_t, slot_t2, phase[None], w_out, w_self),
        2 * ends * neigh * (slots_n + tdim) * width,
        [pltpu.VMEM((2 * half, slots_n + tdim), BF), pltpu.VMEM((neigh, half, ends), BF)],
        direct=range(len(both)),
        limit=52,
    )
    embedding = call(
        sum_kernel, shape((events, 2, width), BF), (part, swap(part)), direct=(0, 1), small=True
    )
    if not packed:
        message = jnp.concatenate(
            [
                message.reshape(peers, cap_self, half),
                jnp.pad(pack[:peers, -128:], ((0, 0), (0, half - 128)))[:, None],
            ],
            axis=1,
        )
    back = exchange(message)
    back, embedding = lax.optimization_barrier((back, embedding))
    back_x = swap(back)
    counts = back
    if not packed:
        back_x = back_x[:, :cap_self].reshape(slots_s, half)
        counts = back[:, cap_self, :128]
        back = back[:, :cap_self].reshape(slots_s, half)
    memory_out = call(
        functools.partial(update_kernel, packed, cap_self),
        shape((owned, half), BF),
        (back, back_x, counts, serve_self, w_in.transpose(1, 0, 2), gh, old, base),
        2 * slots_s * (slots_s * width + width * 3 * half + owned * half),
        [pltpu.VMEM((owned, slots_s), BF)],
        direct=(0, 1, 2),
        views={6: old_view},
        parts=[8],
        limit=50,
    )
    return (embedding, memory_out)


def solution(mesh):
    return jax.shard_map(
        per_device,
        mesh=mesh,
        in_specs=(
            P("nodes", None),
            P("nodes"),
            P("nodes", None, None),
            P("nodes", "mp"),
            P("nodes", None),
            P("nodes", None, None),
            P("nodes", None, None),
            P("nodes", None, None),
            P(),
            P(),
            P(None, "mp"),
            P(None, "mp"),
            P(None, "mp"),
            P("mp", None),
            P("mp", None),
            P("mp", None),
            P("mp", None),
            P("mp", None),
            P("mp", None),
            P(None, None, "mp"),
            P(None, None, "mp"),
        ),
        out_specs=(P("nodes", None, None), P("nodes", "mp")),
        check_vma=False,
    )
```

time: 79.3 us -> 59.7 us (0.75)
  local copies, waits for them, and re-layouts: 14.1 us -> 5.15 us
  waiting for transfers between devices: 14.2 us -> 6.78 us
  Pallas kernels: 33.7 us -> 31.6 us
  other arithmetic: 2 us -> 0.03 us
  starting transfers between devices: 13.6 us -> 14.4 us
    all_to_all x2, waiting for transfers between devices: 14.2 us -> 1.72 us  [exchange(): return lax.all_to_all(x, 'nodes', split_axis=0, concat_axis=0, tiled=True)]
    unnamed x52 -> x44, local copies, waits for them, and re-layouts: 12.4 us -> 5.15 us
    ppermute x5, waiting for transfers between devices: 0.01 us -> 5.06 us  [swap(): return lax.ppermute(x, 'mp', [(0, 1), (1, 0)])]
    pallas_call x7 -> x8, Pallas kernels: 33.7 us -> 31.6 us  [call(): pl.pallas_call(functools.partial(staged, kernel, whole, parts), out_shape...]
    reshape x3 -> x0, local copies, waits for them, and re-layouts: 1.52 us -> none  [the longest x1 0.97 us: per_device(): (part + swap(part)).astype(BF).reshape(2, events, width).transpose(1, 0, 2)]
    all_to_all x2, starting transfers between devices: 12.4 us -> 13.6 us  [exchange(): return lax.all_to_all(x, 'nodes', split_axis=0, concat_axis=0, tiled=True)]
    convert_element_type x1 -> x0, other arithmetic: 1.11 us -> none  [per_device(): (part + swap(part)).astype(BF).reshape(2, events, width).transpose(1, 0, 2)]
    concatenate x1, other arithmetic: 0.88 us -> 0.03 us  [per_device(): jnp.concatenate([w_msg_self, w_msg_other, w_msg_time, w_msg_edge], axis=0)]
  transfers between devices with their start and end apart: 7 -> 7, of which waited for: 1 -> 4; matrix products, arithmetic and copies ran while one was open for 7% -> 0% of each run, Pallas kernels for 32% -> 38%
where the time goes in v2:
time: 59.7 us; the launch traced here: 59.1 us
  Pallas kernels  31.6 us (53%)
  starting transfers between devices  14.4 us (24%)
  waiting for transfers between devices  6.78 us (11%)
  local copies, waits for them, and re-layouts  5.15 us (9%)
  between operations  1.12 us (2%)
    pallas_call x8, Pallas kernels, call(): pl.pallas_call(functools.partial(staged, kernel, whole, parts), out_shape...  31.6 us
    all_to_all x2, starting transfers between devices, exchange(): return lax.all_to_all(x, 'nodes', split_axis=0, concat_axis=0, tiled=True)  13.6 us
    unnamed x44, local copies, waits for them, and re-layouts  5.15 us
    ppermute x5, waiting for transfers between devices, swap(): return lax.ppermute(x, 'mp', [(0, 1), (1, 0)])  5.06 us
    all_to_all x2, waiting for transfers between devices, exchange(): return lax.all_to_all(x, 'nodes', split_axis=0, concat_axis=0, tiled=True)  1.72 us
  transfers between devices with their start and end apart: 7, of which 4 were waited for; matrix products, arithmetic and copies ran while one was open for 0% of the time, Pallas kernels for 38%

profile of v2, /device:TPU:0, one launch (start us, length us, event | category | flops | bytes accessed | tf_op | source)
XLA Modules:
  0.0 59.1 jit_solution(16481656910621606024)
XLA Ops:
  0.6 0.0 copy-start.19
  0.6 0.0 copy-start.18
  0.7 0.0 copy-start.16
  0.7 0.0 copy-start.15
  0.7 3.9 %shard_map.212.refs_6_ = bf16[16,64,256]{2,1,0:T(8,128)(2,1)} custom-call(s32[1,16,32]{2,1,0:T(8,128)} %refs_0_.3, s32[1,16,32]{2,1,0:T(8,128)} %refs_3_.3, bf16[2048,512]{1,0:T(8,128)(2,1)} %refs_1_.3, bf16[2048,512]{1,0:T(8,128)(2,1)} %refs_1_.3, bf16[2048,512]{1,0:T(8,128)(2,1)} %refs_1_.3, bf16[2048,512]{1,0:T(8,128)(2,1)} %refs_1_.3), custom_call_target="tpu_custom_call" | custom-call | flops 1073741824 | bytes 8916992 | tf_op jit(solution)/shard_map/pallas_call | solution.py:544
  4.6 0.0 copy-start.20
  4.6 8.3 %all-to-all-start = ((bf16[16,64,256]{2,1,0:T(8,128)(2,1)}), bf16[16,64,256]{2,1,0:T(8,128)(2,1)S(1)}, u32[]{:S(2)}, u32[]{:S(2)}) async-start(bf16[16,64,256]{2,1,0:T(8,128)(2,1)} %shard_map.212.refs_6_), calls=%async_computation | async-start | bytes 1048576 | tf_op jit(solution)/shard_map/all_to_all | solution.py:574
  12.9 0.0 copy-done.19
  12.9 0.0 copy-done.18
  12.9 0.0 copy-done.16
  12.9 0.0 copy-done.15
  13.0 0.1 collective-permute-start.1
  13.1 0.0 copy-done.20
  13.1 0.5 collective-permute-start
  13.6 6.2 %shard_map.213 = (f32[3,512,256]{2,1,0:T(8,128)}, bf16[16,128,256]{2,1,0:T(8,128)(2,1)}, bf16[256,640]{1,0:T(8,128)(2,1)}, bf16[512,640]{1,0:T(8,128)(2,1)}) custom-call(s32[1,16,32]{2,1,0:T(8,128)} %refs_3_.3, s32[1,128]{1,0:T(1,128)} %bitcast.19, s32[2,16,128]{2,1,0:T(8,128)} %bitcast.18, f32[1,128]{1,0:T(1,128)} %bitcast.20, f32[1,128]{1,0:T(1,128)} %bitcast.13, ...), custom_call_target="tpu_custom_call" | custom-call | flops 1476395008 | bytes 7491072 | tf_op jit(solution)/shard_map/pallas_call | solution.py:544
  19.8 2.7 %shard_map.215.refs_7_ = bf16[2048,256]{1,0:T(8,128)(2,1)} custom-call(s32[1,16,32]{2,1,0:T(8,128)} %refs_3_.3, bf16[2048,512]{1,0:T(8,128)(2,1)} %refs_1_.3), custom_call_target="tpu_custom_call" | custom-call | bytes 3147776 | tf_op jit(solution)/shard_map/pallas_call | solution.py:544
  22.4 0.0 collective-permute-done.refs_3_
  22.4 0.0 copy-start.21
  22.4 0.0 collective-permute-done.1.refs_8_
  22.4 0.0 copy-start.17
  22.5 0.6 copy-done.21
  23.0 0.1 copy-done.17
  23.2 3.2 %shard_map.214.refs_2_ = bf16[512,1792]{1,0:T(8,128)(2,1)} custom-call(s32[2,128]{1,0:T(2,128)} %bitcast.10, bf16[16,128,256]{2,1,0:T(8,128)(2,1)} %get-tuple-element.21.refs_1_.refs_4_, bf16[64,128]{1,0:T(8,128)(2,1)} %bitcast.15, bf16[64,128]{1,0:T(8,128)(2,1)} %copy-done.21, bf16[64,512]{1,0:T(8,128)(2,1)} %refs_4_.3, bf16[64,512]{1,0:T(8,128)(2,1)} %refs_5_.5, ...), custom_call_target="tpu_custom_call" | custom-call | flops 201326592 | bytes 3900416 | tf_op jit(solution)/shard_map/pallas_call | solution.py:544
  26.3 1.7 %all-to-all-done.refs_0_ = bf16[16,64,256]{2,1,0:T(8,128)(2,1)S(1)} async-done(((bf16[16,64,256]{2,1,0:T(8,128)(2,1)}), bf16[16,64,256]{2,1,0:T(8,128)(2,1)S(1)}, u32[]{:S(2)}, u32[]{:S(2)}) %all-to-all-start) | async-done | bytes 524320 | tf_op jit(solution)/shard_map/all_to_all | solution.py:574
  28.1 0.0 collective-permute-start.2
  28.1 1.9 %collective-permute-done.2.refs_1_ = bf16[16,64,256]{2,1,0:T(8,128)(2,1)S(1)} collective-permute-done((bf16[16,64,256]{2,1,0:T(8,128)(2,1)S(1)}, bf16[16,64,256]{2,1,0:T(8,128)(2,1)S(1)}, u32[]{:S(2)}, u32[]{:S(2)}) %collective-permute-start.2) | collective-permute-done | bytes 524320 | tf_op jit(solution)/shard_map/ppermute | solution.py:571
  30.0 1.5 %copy-done = bf16[512,1792]{1,0:T(8,128)(2,1)S(1)} copy-done((bf16[512,1792]{1,0:T(8,128)(2,1)S(1)}, bf16[512,1792]{1,0:T(8,128)(2,1)}, u32[]{:S(2)}) %copy-start) | copy-done | bytes 1835032
  31.5 0.0 copy-start.14
  31.5 1.4 %shard_map.216 = bf16[16,80,128]{2,1,0:T(8,128)(2,1)} custom-call(bf16[16,64,256]{2,1,0:T(8,128)(2,1)S(1)} %all-to-all-done.refs_0_, bf16[16,64,256]{2,1,0:T(8,128)(2,1)S(1)} %collective-permute-done.2.refs_1_, bf16[512,1792]{1,0:T(8,128)(2,1)S(1)} %copy-done), custom_call_target="tpu_custom_call" | custom-call | flops 402653184 | bytes 3211264 | tf_op jit(solution)/shard_map/pallas_call | solution.py:544
  32.9 0.0 copy-done.3
  32.9 0.0 copy-done.6
  32.9 5.3 %all-to-all-start.1 = ((bf16[16,80,128]{2,1,0:T(8,128)(2,1)}), bf16[16,80,128]{2,1,0:T(8,128)(2,1)S(1)}, u32[]{:S(2)}, u32[]{:S(2)}) async-start(bf16[16,80,128]{2,1,0:T(8,128)(2,1)} %shard_map.216), calls=%async_computation.1 | async-start | bytes 655360 | tf_op jit(solution)/shard_map/all_to_all | solution.py:574
  38.2 0.0 copy-done.9
  38.3 0.0 copy-done.13
  38.3 1.0 %copy-done.4 = bf16[16,64,256]{2,1,0:T(8,128)(2,1)S(1)} copy-done((bf16[16,64,256]{2,1,0:T(8,128)(2,1)S(1)}, bf16[16,64,256]{2,1,0:T(8,128)(2,1)}, u32[]{:S(2)}) %copy-start.4) | copy-done | bytes 524312
  39.4 8.1 %shard_map.217.refs_0_ = bf16[256,512]{1,0:T(8,128)(2,1)S(1)} custom-call(bf16[16,64,256]{2,1,0:T(8,128)(2,1)S(1)} %copy-done.4, bf16[16,64,256]{2,1,0:T(8,128)(2,1)} %copy-done.6, bf16[512,640]{1,0:T(8,128)(2,1)} %get-tuple-element.20.refs_2_, s32[2,16,128]{2,1,0:T(8,128)S(1)} %bitcast.12, bf16[16,128,256]{2,1,0:T(8,128)(2,1)} %get-tuple-element.21.refs_1_.refs_4_, ...), custom_call_target="tpu_custom_call" | custom-call | flops 2684354560 | bytes 3884544 | tf_op jit(solution)/shard_map/pallas_call | solution.py:544
  47.5 0.0 copy-start.7
  47.5 0.7 %copy-done.7 = bf16[256,512]{1,0:T(8,128)(2,1)} copy-done((bf16[256,512]{1,0:T(8,128)(2,1)}, bf16[256,512]{1,0:T(8,128)(2,1)S(1)}, u32[]{:S(2)}) %copy-start.7) | copy-done | bytes 262168
  48.2 0.0 collective-permute-start.3
  48.2 1.7 %collective-permute-done.3.refs_1_ = bf16[256,512]{1,0:T(8,128)(2,1)} collective-permute-done((bf16[256,512]{1,0:T(8,128)(2,1)S(1)}, bf16[256,512]{1,0:T(8,128)(2,1)}, u32[]{:S(2)}, u32[]{:S(2)}) %collective-permute-start.3) | collective-permute-done | bytes 262176 | tf_op jit(solution)/shard_map/ppermute | solution.py:571
  49.9 2.2 %shard_map.218 = bf16[128,2,512]{2,1,0:T(2,128)(2,1)} custom-call(bf16[256,512]{1,0:T(8,128)(2,1)} %copy-done.7, bf16[256,512]{1,0:T(8,128)(2,1)} %collective-permute-done.3.refs_1_), custom_call_target="tpu_custom_call" | custom-call | bytes 1 | tf_op jit(solution)/shard_map/pallas_call | solution.py:544
  52.1 0.0 all-to-all-done.1.refs_0_.refs_2_
  52.1 0.2 collective-permute-start.4
  52.3 1.5 %collective-permute-done.4.refs_1_ = bf16[16,80,128]{2,1,0:T(8,128)(2,1)S(1)} collective-permute-done((bf16[16,80,128]{2,1,0:T(8,128)(2,1)S(1)}, bf16[16,80,128]{2,1,0:T(8,128)(2,1)S(1)}, u32[]{:S(2)}, u32[]{:S(2)}) %collective-permute-start.4) | collective-permute-done | bytes 327712 | tf_op jit(solution)/shard_map/ppermute | solution.py:571
  53.8 0.0 copy-done.2
  53.8 0.0 copy-start.5
  53.8 1.1 %copy-done.5 = bf16[512,3,256]{2,0,1:T(8,128)(2,1)S(1)} copy-done((bf16[512,3,256]{2,0,1:T(8,128)(2,1)S(1)}, bf16[512,3,256]{2,0,1:T(8,128)(2,1)}, u32[]{:S(2)}) %copy-start.5) | copy-done | bytes 786456
  54.9 4.0 %shard_map.219 = bf16[2048,256]{1,0:T(8,128)(2,1)} custom-call(bf16[16,80,128]{2,1,0:T(8,128)(2,1)S(1)} %all-to-all-done.1.refs_0_.refs_2_, bf16[16,80,128]{2,1,0:T(8,128)(2,1)S(1)} %collective-permute-done.4.refs_1_, bf16[16,80,128]{2,1,0:T(8,128)(2,1)S(1)} %all-to-all-done.1.refs_0_.refs_2_, s32[1,16,32]{2,1,0:T(8,128)S(1)} %copy-done.8, ...), custom_call_target="tpu_custom_call" | custom-call | flops 1207959552 | bytes 5965824 | tf_op jit(solution)/shard_map/pallas_call | solution.py:544
  (19 shorter events, 0.1 us)
Async XLA Ops:
  0.6 12.3 %copy-start.19 = (bf16[64,512]{1,0:T(8,128)(2,1)S(1)}, bf16[64,512]{1,0:T(8,128)(2,1)}, u32[]{:S(2)}) copy-start(bf16[64,512]{1,0:T(8,128)(2,1)} %refs_5_.5) | copy-start | bytes 196612
  0.6 12.3 %copy-start.18 = (bf16[64,512]{1,0:T(8,128)(2,1)S(1)}, bf16[64,512]{1,0:T(8,128)(2,1)}, u32[]{:S(2)}) copy-start(bf16[64,512]{1,0:T(8,128)(2,1)} %refs_4_.3) | copy-start | bytes 196612
  0.7 12.3 %copy-start.16 = (bf16[256,512]{1,0:T(8,128)(2,1)S(1)}, bf16[256,512]{1,0:T(8,128)(2,1)}, u32[]{:S(2)}) copy-start(bf16[256,512]{1,0:T(8,128)(2,1)} %refs_7_.3) | copy-start | bytes 786436
  0.7 12.3 %copy-start.15 = (bf16[256,512]{1,0:T(8,128)(2,1)S(1)}, bf16[256,512]{1,0:T(8,128)(2,1)}, u32[]{:S(2)}) copy-start(bf16[256,512]{1,0:T(8,128)(2,1)} %refs_6_.1) | copy-start | bytes 786436
  4.6 8.5 %copy-start.20 = (bf16[128,64]{0,1:T(8,128)(2,1)S(1)}, bf16[128,64]{0,1:T(8,128)(2,1)}, u32[]{:S(2)}) copy-start(bf16[128,64]{0,1:T(8,128)(2,1)} %param.24) | copy-start | bytes 49156
  4.6 23.5 %all-to-all-start = ((bf16[16,64,256]{2,1,0:T(8,128)(2,1)}), bf16[16,64,256]{2,1,0:T(8,128)(2,1)S(1)}, u32[]{:S(2)}, u32[]{:S(2)}) async-start(bf16[16,64,256]{2,1,0:T(8,128)(2,1)} %shard_map.212.refs_6_), calls=%async_computation | async-start | bytes 1048576 | tf_op jit(solution)/shard_map/all_to_all | solution.py:574
  13.0 9.4 %collective-permute-start.1 = (bf16[640,256]{1,0:T(8,128)(2,1)S(1)}, bf16[640,256]{1,0:T(8,128)(2,1)S(1)}, u32[]{:S(2)}, u32[]{:S(2)}) collective-permute-start(bf16[640,256]{1,0:T(8,128)(2,1)S(1)} %fusion.2), channel_id=1, source_target_pairs={{0,1},{1,0},{2,3},{3,2},{4,5},{5,4},{6,7},{7,6},{8,9},{9,8},{10,11... | collective-permute-start | bytes 983048 | tf_op jit(solution)/shard_map/ppermute | solution.py:571
  13.1 9.3 %collective-permute-start = (bf16[64,128]{1,0:T(8,128)(2,1)S(1)}, bf16[64,128]{1,0:T(8,128)(2,1)S(1)}, u32[]{:S(2)}, u32[]{:S(2)}) collective-permute-start(bf16[64,128]{1,0:T(8,128)(2,1)S(1)} %bitcast.16), channel_id=1, source_target_pairs={{0,1},{1,0},{2,3},{3,2},{4,5},{5,4},{6,7},{7,6},{8,9},{9,8},{10,11... | collective-permute-start | bytes 49160 | tf_op jit(solution)/shard_map/ppermute | solution.py:571
  22.4 0.6 %copy-start.21 = (bf16[64,128]{1,0:T(8,128)(2,1)}, bf16[64,128]{1,0:T(8,128)(2,1)S(1)}, u32[]{:S(2)}) copy-start(bf16[64,128]{1,0:T(8,128)(2,1)S(1)} %collective-permute-done.refs_3_) | copy-start | bytes 49156
  22.4 0.7 %copy-start.17 = (bf16[640,256]{1,0:T(8,128)(2,1)}, bf16[640,256]{1,0:T(8,128)(2,1)S(1)}, u32[]{:S(2)}) copy-start(bf16[640,256]{1,0:T(8,128)(2,1)S(1)} %collective-permute-done.1.refs_8_) | copy-start | bytes 983044
  28.1 4.9 %copy-start.3 = (bf16[16,64,256]{2,1,0:T(8,128)(2,1)}, bf16[16,64,256]{2,1,0:T(8,128)(2,1)S(1)}, u32[]{:S(2)}) copy-start(bf16[16,64,256]{2,1,0:T(8,128)(2,1)S(1)} %all-to-all-done.refs_0_) | copy-start | bytes 1572868
  28.1 10.2 %copy-start.9 = (s32[128,2]{0,1:T(2,128)S(1)}, s32[128,2]{0,1:T(2,128)}, u32[]{:S(2)}) copy-start(s32[128,2]{0,1:T(2,128)} %param.25) | copy-start | bytes 3076
  28.1 10.2 %copy-start.13 = (f32[128]{0:T(128)S(1)}, f32[128]{0:T(128)}, u32[]{:S(2)}) copy-start(f32[128]{0:T(128)} %param.30) | copy-start | bytes 1540
  28.1 1.9 %collective-permute-start.2 = (bf16[16,64,256]{2,1,0:T(8,128)(2,1)S(1)}, bf16[16,64,256]{2,1,0:T(8,128)(2,1)S(1)}, u32[]{:S(2)}, u32[]{:S(2)}) collective-permute-start(bf16[16,64,256]{2,1,0:T(8,128)(2,1)S(1)} %all-to-all-done.refs_0_), channel_id=1, source_target_pairs={{0,1},{1,0},{2,3},{3,2},{4,5},{5,4},{6,7},{7,6},{8,9},{9,8},{10,11... | collective-permute-start | bytes 1572872 | tf_op jit(solution)/shard_map/ppermute | solution.py:571
  30.0 1.5 %copy-start = (bf16[512,1792]{1,0:T(8,128)(2,1)S(1)}, bf16[512,1792]{1,0:T(8,128)(2,1)}, u32[]{:S(2)}) copy-start(bf16[512,1792]{1,0:T(8,128)(2,1)} %shard_map.214.refs_2_) | copy-start | bytes 5505028
  31.5 1.4 %copy-start.6 = (bf16[16,64,256]{2,1,0:T(8,128)(2,1)}, bf16[16,64,256]{2,1,0:T(8,128)(2,1)S(1)}, u32[]{:S(2)}) copy-start(bf16[16,64,256]{2,1,0:T(8,128)(2,1)S(1)} %collective-permute-done.2.refs_1_) | copy-start | bytes 1572868
  31.5 6.8 %copy-start.10 = (bf16[256,512]{1,0:T(8,128)(2,1)S(1)}, bf16[256,512]{1,0:T(8,128)(2,1)}, u32[]{:S(2)}) copy-start(bf16[256,512]{1,0:T(8,128)(2,1)} %refs_8_.3) | copy-start | bytes 786436
  31.5 6.8 %copy-start.11 = (bf16[256,512]{1,0:T(8,128)(2,1)S(1)}, bf16[256,512]{1,0:T(8,128)(2,1)}, u32[]{:S(2)}) copy-start(bf16[256,512]{1,0:T(8,128)(2,1)} %refs_9_.3) | copy-start | bytes 786436
  31.5 6.8 %copy-start.12 = (s32[128,2,16]{0,2,1:T(8,128)S(1)}, s32[128,2,16]{0,2,1:T(8,128)}, u32[]{:S(2)}) copy-start(s32[128,2,16]{0,2,1:T(8,128)} %param.26) | copy-start | bytes 49156
  31.5 6.8 %copy-start.14 = (bf16[256,640]{1,0:T(8,128)(2,1)S(1)}, bf16[256,640]{1,0:T(8,128)(2,1)}, u32[]{:S(2)}) copy-start(bf16[256,640]{1,0:T(8,128)(2,1)} %get-tuple-element.22.refs_5_) | copy-start | bytes 983044
  32.9 19.1 %all-to-all-start.1 = ((bf16[16,80,128]{2,1,0:T(8,128)(2,1)}), bf16[16,80,128]{2,1,0:T(8,128)(2,1)S(1)}, u32[]{:S(2)}, u32[]{:S(2)}) async-start(bf16[16,80,128]{2,1,0:T(8,128)(2,1)} %shard_map.216), calls=%async_computation.1 | async-start | bytes 655360 | tf_op jit(solution)/shard_map/all_to_all | solution.py:574
  38.3 1.0 %copy-start.4 = (bf16[16,64,256]{2,1,0:T(8,128)(2,1)S(1)}, bf16[16,64,256]{2,1,0:T(8,128)(2,1)}, u32[]{:S(2)}) copy-start(bf16[16,64,256]{2,1,0:T(8,128)(2,1)} %copy-done.3) | copy-start | bytes 1572868
  39.3 14.4 %copy-start.1 = (bf16[16,64,256]{2,1,0:T(8,128)(2,1)S(1)}, bf16[16,64,256]{2,1,0:T(8,128)(2,1)}, u32[]{:S(2)}) copy-start(bf16[16,64,256]{2,1,0:T(8,128)(2,1)} %shard_map.212.refs_6_) | copy-start | bytes 1572868
  39.4 14.4 %copy-start.2 = (bf16[2048,256]{1,0:T(8,128)(2,1)S(1)}, bf16[2048,256]{1,0:T(8,128)(2,1)}, u32[]{:S(2)}) copy-start(bf16[2048,256]{1,0:T(8,128)(2,1)} %shard_map.215.refs_7_) | copy-start | bytes 3145732
  39.4 14.4 %copy-start.8 = (s32[1,16,32]{2,1,0:T(8,128)S(1)}, s32[1,16,32]{2,1,0:T(8,128)}, u32[]{:S(2)}) copy-start(s32[1,16,32]{2,1,0:T(8,128)} %refs_3_.3) | copy-start | bytes 6148
  47.5 0.7 %copy-start.7 = (bf16[256,512]{1,0:T(8,128)(2,1)}, bf16[256,512]{1,0:T(8,128)(2,1)S(1)}, u32[]{:S(2)}) copy-start(bf16[256,512]{1,0:T(8,128)(2,1)S(1)} %shard_map.217.refs_0_) | copy-start | bytes 786436
  48.2 1.7 %collective-permute-start.3 = (bf16[256,512]{1,0:T(8,128)(2,1)S(1)}, bf16[256,512]{1,0:T(8,128)(2,1)}, u32[]{:S(2)}, u32[]{:S(2)}) collective-permute-start(bf16[256,512]{1,0:T(8,128)(2,1)S(1)} %shard_map.217.refs_0_), channel_id=1, source_target_pairs={{0,1},{1,0},{2,3},{3,2},{4,5},{5,4},{6,7},{7,6},{8,9},{9,8},{10,11... | collective-permute-start | bytes 786440 | tf_op jit(solution)/shard_map/ppermute | solution.py:571
  52.1 1.7 %collective-permute-start.4 = (bf16[16,80,128]{2,1,0:T(8,128)(2,1)S(1)}, bf16[16,80,128]{2,1,0:T(8,128)(2,1)S(1)}, u32[]{:S(2)}, u32[]{:S(2)}) collective-permute-start(bf16[16,80,128]{2,1,0:T(8,128)(2,1)S(1)} %all-to-all-done.1.refs_0_.refs_2_), channel_id=1, source_target_pairs={{0,1},{1,0},{2,3},{3,2},{4,5},{5,4},{6,7},{7,6},{8,9},{9,8},{10,11... | collective-permute-start | bytes 983048 | tf_op jit(solution)/shard_map/ppermute | solution.py:571
  53.8 1.1 %copy-start.5 = (bf16[512,3,256]{2,0,1:T(8,128)(2,1)S(1)}, bf16[512,3,256]{2,0,1:T(8,128)(2,1)}, u32[]{:S(2)}) copy-start(bf16[512,3,256]{2,0,1:T(8,128)(2,1)} %param.40) | copy-start | bytes 2359300

commit v3 on v2

--- a/solution.py
+++ b/solution.py
@@ -324,20 +324,29 @@
     return ref[...]
 
 
-def message_kernel(packed, peers, cap, cap_self, own_ref, oth_ref, pack_ref, out_ref):
+def message_part(own, pack_ref, first, half):
     slots = pack_ref.shape[0]
-    half = own_ref.shape[-1]
     at_count, at_pre, at_weight, at_sent, _ = pack_places(slots, half)
-    own = part_of(own_ref, packed, cap, cap_self)
-    oth = part_of(oth_ref, packed, cap, cap_self)
-    weight = slice(at_weight, at_sent)
-    both = dot(own, pack_ref[:half, weight]) + dot(oth, pack_ref[half : 2 * half, weight])
+    both = dot(own, pack_ref[first : first + half, at_weight:at_sent])
     count = pack_ref[:, at_count:at_pre].astype(F32)
     count = jnp.concatenate([count] * (half // 128), axis=1)
+    return dot(pack_ref[:, :at_count], both[:, :half].astype(BF)) + count * both[:, half:]
+
+
+def own_message_kernel(packed, cap, cap_self, own_ref, pack_ref, total_ref):
+    half = own_ref.shape[-1]
+    _, at_pre, at_weight, _, _ = pack_places(pack_ref.shape[0], half)
     pre = pack_ref[:, at_pre : at_pre + half].astype(F32)
     pre = pre + pack_ref[:, at_pre + half : at_weight].astype(F32)
-    total = dot(pack_ref[:, :at_count], both[:, :half].astype(BF)) + count * both[:, half:] + pre
-    out = total.astype(BF)
+    own = part_of(own_ref, packed, cap, cap_self)
+    total_ref[...] = message_part(own, pack_ref, 0, half) + pre
+
+
+def message_kernel(packed, peers, cap, cap_self, oth_ref, pack_ref, total_ref, out_ref):
+    half = oth_ref.shape[-1]
+    at_sent = pack_places(pack_ref.shape[0], half)[3]
+    oth = part_of(oth_ref, packed, cap, cap_self)
+    out = (total_ref[...] + message_part(oth, pack_ref, half, half)).astype(BF)
     if not packed:
         out_ref[...] = out
         return
@@ -558,6 +567,19 @@
             ),
         )(*args)
 
+    def plain(kernel, out_shape, args, flops, limit):
+        size = sum(a.size * a.dtype.itemsize for a in (*args, out_shape))
+        return pl.pallas_call(
+            kernel,
+            out_shape=out_shape,
+            in_specs=[VMEM] * len(args),
+            out_specs=VMEM,
+            compiler_params=pltpu.CompilerParams(vmem_limit_bytes=limit * 1024 * 1024),
+            cost_estimate=pl.CostEstimate(
+                flops=int(flops), bytes_accessed=int(size), transcendentals=0
+            ),
+        )(*args)
+
     def columns(rows):
         return (lambda ref: ref.at[:, half_of(lax.axis_index("mp"), half)], (rows, half))
 
@@ -676,13 +698,19 @@
         mine = [f[:, cap:].reshape(slots_s, half) for f in (fetched, fetched_x)]
         both = (nbr[0], mine[0], nbr[1], mine[1])
         back_shape = shape((slots_s, half), BF)
-    message = call(
+    total = plain(
+        functools.partial(own_message_kernel, packed, cap, cap_self),
+        shape((slots_s, half), F32),
+        (mine[0], pack),
+        slots_s * half * (2 * width + slots_s),
+        50,
+    )
+    message = plain(
         functools.partial(message_kernel, packed, peers, cap, cap_self),
         back_shape,
-        (*mine, pack),
-        2 * slots_s * half * (2 * width + slots_s),
-        direct=(0, 1, 2),
-        limit=50,
+        (mine[1], pack, total),
+        slots_s * half * (2 * width + slots_s),
+        50,
     )
     message, slot_t2 = lax.optimization_barrier((message, slot_t))
     part = call(
@@ -692,10 +720,10 @@
         2 * ends * neigh * (slots_n + tdim) * width,
         [pltpu.VMEM((2 * half, slots_n + tdim), BF), pltpu.VMEM((neigh, half, ends), BF)],
         direct=range(len(both)),
-        limit=52,
+        limit=62,
     )
     embedding = call(
-        sum_kernel, shape((events, 2, width), BF), (part, swap(part)), direct=(0, 1), small=True
+        sum_kernel, shape((events, 2, width), BF), (part, swap(part)), direct=(0, 1), small=True, limit=52
     )
     if not packed:
         message = jnp.concatenate(
@@ -722,7 +750,7 @@
         direct=(0, 1, 2),
         views={6: old_view},
         parts=[8],
-        limit=50,
+        limit=53,
     )
     return (embedding, memory_out)
 

time: 59.7 us -> 56.2 us (0.941)
  waiting for transfers between devices: 6.78 us -> 4.85 us
  local copies, waits for them, and re-layouts: 5.15 us -> 3.42 us
    pallas_call x0 -> x2, Pallas kernels: none -> 1.94 us  [plain(): pl.pallas_call(kernel, out_shape=out_shape, in_specs=[VMEM] * len(args),...]
    ppermute x5, waiting for transfers between devices: 5.06 us -> 3.17 us  [swap(): return lax.ppermute(x, 'mp', [(0, 1), (1, 0)])]
    pallas_call x8 -> x7, Pallas kernels: 31.6 us -> 29.9 us  [call(): pl.pallas_call(functools.partial(staged, kernel, whole, parts), out_shape...]
    unnamed x44 -> x24, local copies, waits for them, and re-layouts: 5.15 us -> 3.42 us
  transfers between devices with their start and end apart: 7 -> 7, of which waited for: 4 -> 3; matrix products, arithmetic and copies ran while one was open for 0% -> 0% of each run, Pallas kernels for 38% -> 41%
where the time goes in v3:
time: 56.2 us; the launch traced here: 55.6 us
  Pallas kernels  31.8 us (57%)
  starting transfers between devices  14.5 us (26%)
  waiting for transfers between devices  4.85 us (9%)
  local copies, waits for them, and re-layouts  3.42 us (6%)
  between operations  1.03 us (2%)
    pallas_call x7, Pallas kernels, call(): pl.pallas_call(functools.partial(staged, kernel, whole, parts), out_shape...  29.9 us
    all_to_all x2, starting transfers between devices, exchange(): return lax.all_to_all(x, 'nodes', split_axis=0, concat_axis=0, tiled=True)  13.6 us
    unnamed x24, local copies, waits for them, and re-layouts  3.42 us
    ppermute x5, waiting for transfers between devices, swap(): return lax.ppermute(x, 'mp', [(0, 1), (1, 0)])  3.17 us
    pallas_call x2, Pallas kernels, plain(): pl.pallas_call(kernel, out_shape=out_shape, in_specs=[VMEM] * len(args),...  1.94 us
    all_to_all x2, waiting for transfers between devices, exchange(): return lax.all_to_all(x, 'nodes', split_axis=0, concat_axis=0, tiled=True)  1.68 us
  transfers between devices with their start and end apart: 7, of which 3 were waited for; matrix products, arithmetic and copies ran while one was open for 0% of the time, Pallas kernels for 41%

profile of v3, /device:TPU:0, one launch (start us, length us, event | category | flops | bytes accessed | tf_op | source)
XLA Modules:
  0.0 55.6 jit_solution(9986324674124662331)
XLA Ops:
  0.6 0.0 copy-start.9
  0.6 0.0 copy-start.8
  0.7 0.0 copy-start.6
  0.7 0.0 copy-start.5
  0.7 3.9 %shard_map.212.refs_6_ = bf16[16,64,256]{2,1,0:T(8,128)(2,1)} custom-call(s32[1,16,32]{2,1,0:T(8,128)} %refs_0_.3, s32[1,16,32]{2,1,0:T(8,128)} %refs_3_.3, bf16[2048,512]{1,0:T(8,128)(2,1)} %refs_1_.3, bf16[2048,512]{1,0:T(8,128)(2,1)} %refs_1_.3, bf16[2048,512]{1,0:T(8,128)(2,1)} %refs_1_.3, bf16[2048,512]{1,0:T(8,128)(2,1)} %refs_1_.3), custom_call_target="tpu_custom_call" | custom-call | flops 1073741824 | bytes 8916992 | tf_op jit(solution)/shard_map/pallas_call | solution.py:553
  4.6 0.0 copy-start.10
  4.6 8.3 %all-to-all-start = ((bf16[16,64,256]{2,1,0:T(8,128)(2,1)}), bf16[16,64,256]{2,1,0:T(8,128)(2,1)S(1)}, u32[]{:S(2)}, u32[]{:S(2)}) async-start(bf16[16,64,256]{2,1,0:T(8,128)(2,1)} %shard_map.212.refs_6_), calls=%async_computation | async-start | bytes 1048576 | tf_op jit(solution)/shard_map/all_to_all | solution.py:596
  12.9 0.0 copy-done.9
  12.9 0.0 copy-done.8
  13.0 0.0 copy-done.6
  13.0 0.0 copy-done.5
  13.0 0.1 collective-permute-start.1
  13.1 0.0 copy-done.10
  13.1 0.5 collective-permute-start
  13.6 6.2 %shard_map.213 = (f32[3,512,256]{2,1,0:T(8,128)}, bf16[16,128,256]{2,1,0:T(8,128)(2,1)}, bf16[256,640]{1,0:T(8,128)(2,1)}, bf16[512,640]{1,0:T(8,128)(2,1)}) custom-call(s32[1,16,32]{2,1,0:T(8,128)} %refs_3_.3, s32[1,128]{1,0:T(1,128)} %bitcast.17, s32[2,16,128]{2,1,0:T(8,128)} %bitcast.15, f32[1,128]{1,0:T(1,128)} %bitcast.18, f32[1,128]{1,0:T(1,128)} %bitcast.19, ...), custom_call_target="tpu_custom_call" | custom-call | flops 1476395008 | bytes 7491072 | tf_op jit(solution)/shard_map/pallas_call | solution.py:553
  19.8 2.7 %shard_map.215.refs_7_ = bf16[2048,256]{1,0:T(8,128)(2,1)} custom-call(s32[1,16,32]{2,1,0:T(8,128)} %refs_3_.3, bf16[2048,512]{1,0:T(8,128)(2,1)} %refs_1_.3), custom_call_target="tpu_custom_call" | custom-call | bytes 3147776 | tf_op jit(solution)/shard_map/pallas_call | solution.py:553
  22.4 0.0 collective-permute-done.refs_3_
  22.5 0.0 copy-start.11
  22.5 0.0 collective-permute-done.1.refs_8_
  22.5 0.0 copy-start.7
  22.5 0.6 %copy-done.11 = bf16[64,128]{1,0:T(8,128)(2,1)} copy-done((bf16[64,128]{1,0:T(8,128)(2,1)}, bf16[64,128]{1,0:T(8,128)(2,1)S(1)}, u32[]{:S(2)}) %copy-start.11) | copy-done | bytes 16408
  23.1 0.2 copy-done.7
  23.2 3.2 %shard_map.214.pack_ref = bf16[512,1792]{1,0:T(8,128)(2,1)} custom-call(s32[2,128]{1,0:T(2,128)} %bitcast.12, bf16[16,128,256]{2,1,0:T(8,128)(2,1)} %get-tuple-element.21.refs_1_.refs_4_, bf16[64,128]{1,0:T(8,128)(2,1)} %bitcast.10, bf16[64,128]{1,0:T(8,128)(2,1)} %copy-done.11, bf16[64,512]{1,0:T(8,128)(2,1)} %refs_4_.3, bf16[64,512]{1,0:T(8,128)(2,1)} %refs_5_.5, ...), custom_call_target="tpu_custom_call" | custom-call | flops 201326592 | bytes 3900416 | tf_op jit(solution)/shard_map/pallas_call | solution.py:553
  26.4 1.7 %all-to-all-done.own_ref.refs_0_ = bf16[16,64,256]{2,1,0:T(8,128)(2,1)S(1)} async-done(((bf16[16,64,256]{2,1,0:T(8,128)(2,1)}), bf16[16,64,256]{2,1,0:T(8,128)(2,1)S(1)}, u32[]{:S(2)}, u32[]{:S(2)}) %all-to-all-start) | async-done | bytes 524320 | tf_op jit(solution)/shard_map/all_to_all | solution.py:596
  28.1 0.0 copy-start.1
  28.1 0.0 collective-permute-start.2
  28.1 0.0 copy-start
  28.1 1.7 %copy-done = bf16[512,1792]{1,0:T(8,128)(2,1)S(1)} copy-done((bf16[512,1792]{1,0:T(8,128)(2,1)S(1)}, bf16[512,1792]{1,0:T(8,128)(2,1)}, u32[]{:S(2)}) %copy-start) | copy-done | bytes 1835032
  29.8 0.6 %shard_map.216.total_ref = f32[512,256]{1,0:T(8,128)S(1)} custom-call(bf16[16,64,256]{2,1,0:T(8,128)(2,1)S(1)} %all-to-all-done.own_ref.refs_0_, bf16[512,1792]{1,0:T(8,128)(2,1)S(1)} %copy-done), custom_call_target="tpu_custom_call" | custom-call | flops 201326592 | bytes 2883584 | tf_op jit(solution)/shard_map/pallas_call | solution.py:572
  30.4 0.0 collective-permute-done.2.oth_ref.refs_1_
  30.4 0.0 copy-start.2
  30.4 1.3 %shard_map.217 = bf16[16,80,128]{2,1,0:T(8,128)(2,1)} custom-call(bf16[16,64,256]{2,1,0:T(8,128)(2,1)S(1)} %collective-permute-done.2.oth_ref.refs_1_, bf16[512,1792]{1,0:T(8,128)(2,1)S(1)} %copy-done, f32[512,256]{1,0:T(8,128)S(1)} %shard_map.216.total_ref), custom_call_target="tpu_custom_call" | custom-call | flops 201326592 | bytes 3211264 | tf_op jit(solution)/shard_map/pallas_call | solution.py:572
  31.7 0.0 copy-done.1
  31.7 0.0 copy-done.2
  31.7 5.3 %all-to-all-start.1 = ((bf16[16,80,128]{2,1,0:T(8,128)(2,1)}), bf16[16,80,128]{2,1,0:T(8,128)(2,1)S(1)}, u32[]{:S(2)}, u32[]{:S(2)}) async-start(bf16[16,80,128]{2,1,0:T(8,128)(2,1)} %shard_map.217), calls=%async_computation.1 | async-start | bytes 655360 | tf_op jit(solution)/shard_map/all_to_all | solution.py:596
  37.0 0.0 copy-start.4
  37.0 8.9 %shard_map.218.refs_0_ = bf16[256,512]{1,0:T(8,128)(2,1)} custom-call(bf16[16,64,256]{2,1,0:T(8,128)(2,1)} %copy-done.1, bf16[16,64,256]{2,1,0:T(8,128)(2,1)} %copy-done.2, bf16[512,640]{1,0:T(8,128)(2,1)} %get-tuple-element.20.refs_2_, s32[2,16,128]{2,1,0:T(8,128)} %bitcast.16, bf16[16,128,256]{2,1,0:T(8,128)(2,1)} %get-tuple-element.21.refs_1_.refs_4_, ...), custom_call_target="tpu_custom_call" | custom-call | flops 2684354560 | bytes 3884544 | tf_op jit(solution)/shard_map/pallas_call | solution.py:553
  45.9 0.1 collective-permute-start.3
  46.1 1.7 %collective-permute-done.3.refs_1_ = bf16[256,512]{1,0:T(8,128)(2,1)S(1)} collective-permute-done((bf16[256,512]{1,0:T(8,128)(2,1)}, bf16[256,512]{1,0:T(8,128)(2,1)S(1)}, u32[]{:S(2)}, u32[]{:S(2)}) %collective-permute-start.3) | collective-permute-done | bytes 262176 | tf_op jit(solution)/shard_map/ppermute | solution.py:593
  47.7 0.0 copy-start.3
  47.7 0.9 %copy-done.3 = bf16[256,512]{1,0:T(8,128)(2,1)S(1)} copy-done((bf16[256,512]{1,0:T(8,128)(2,1)S(1)}, bf16[256,512]{1,0:T(8,128)(2,1)}, u32[]{:S(2)}) %copy-start.3) | copy-done | bytes 262168
  48.7 1.2 %shard_map.219 = bf16[128,2,512]{2,1,0:T(2,128)(2,1)} custom-call(bf16[256,512]{1,0:T(8,128)(2,1)S(1)} %copy-done.3, bf16[256,512]{1,0:T(8,128)(2,1)S(1)} %collective-permute-done.3.refs_1_), custom_call_target="tpu_custom_call" | custom-call | bytes 1 | tf_op jit(solution)/shard_map/pallas_call | solution.py:553
  49.8 0.0 all-to-all-done.1.refs_0_.refs_2_
  49.8 0.2 collective-permute-start.4
  50.0 1.5 %collective-permute-done.4.refs_1_ = bf16[16,80,128]{2,1,0:T(8,128)(2,1)S(1)} collective-permute-done((bf16[16,80,128]{2,1,0:T(8,128)(2,1)S(1)}, bf16[16,80,128]{2,1,0:T(8,128)(2,1)S(1)}, u32[]{:S(2)}, u32[]{:S(2)}) %collective-permute-start.4) | collective-permute-done | bytes 327712 | tf_op jit(solution)/shard_map/ppermute | solution.py:593
  51.5 0.0 copy-done.4
  51.5 3.9 %shard_map.220 = bf16[2048,256]{1,0:T(8,128)(2,1)} custom-call(bf16[16,80,128]{2,1,0:T(8,128)(2,1)S(1)} %all-to-all-done.1.refs_0_.refs_2_, bf16[16,80,128]{2,1,0:T(8,128)(2,1)S(1)} %collective-permute-done.4.refs_1_, bf16[16,80,128]{2,1,0:T(8,128)(2,1)S(1)} %all-to-all-done.1.refs_0_.refs_2_, s32[1,16,32]{2,1,0:T(8,128)S(1)} %copy-done.4, ...), custom_call_target="tpu_custom_call" | custom-call | flops 1207959552 | bytes 5965824 | tf_op jit(solution)/shard_map/pallas_call | solution.py:553
  (1 shorter events, 0.0 us)
Async XLA Ops:
  0.6 12.3 %copy-start.9 = (bf16[64,512]{1,0:T(8,128)(2,1)S(1)}, bf16[64,512]{1,0:T(8,128)(2,1)}, u32[]{:S(2)}) copy-start(bf16[64,512]{1,0:T(8,128)(2,1)} %refs_5_.5) | copy-start | bytes 196612
  0.6 12.3 %copy-start.8 = (bf16[64,512]{1,0:T(8,128)(2,1)S(1)}, bf16[64,512]{1,0:T(8,128)(2,1)}, u32[]{:S(2)}) copy-start(bf16[64,512]{1,0:T(8,128)(2,1)} %refs_4_.3) | copy-start | bytes 196612
  0.7 12.3 %copy-start.6 = (bf16[256,512]{1,0:T(8,128)(2,1)S(1)}, bf16[256,512]{1,0:T(8,128)(2,1)}, u32[]{:S(2)}) copy-start(bf16[256,512]{1,0:T(8,128)(2,1)} %refs_7_.3) | copy-start | bytes 786436
  0.7 12.3 %copy-start.5 = (bf16[256,512]{1,0:T(8,128)(2,1)S(1)}, bf16[256,512]{1,0:T(8,128)(2,1)}, u32[]{:S(2)}) copy-start(bf16[256,512]{1,0:T(8,128)(2,1)} %refs_6_.1) | copy-start | bytes 786436
  4.6 8.5 %copy-start.10 = (bf16[128,64]{0,1:T(8,128)(2,1)S(1)}, bf16[128,64]{0,1:T(8,128)(2,1)}, u32[]{:S(2)}) copy-start(bf16[128,64]{0,1:T(8,128)(2,1)} %param.24) | copy-start | bytes 49156
  4.6 23.5 %all-to-all-start = ((bf16[16,64,256]{2,1,0:T(8,128)(2,1)}), bf16[16,64,256]{2,1,0:T(8,128)(2,1)S(1)}, u32[]{:S(2)}, u32[]{:S(2)}) async-start(bf16[16,64,256]{2,1,0:T(8,128)(2,1)} %shard_map.212.refs_6_), calls=%async_computation | async-start | bytes 1048576 | tf_op jit(solution)/shard_map/all_to_all | solution.py:596
  13.0 9.5 %collective-permute-start.1 = (bf16[640,256]{1,0:T(8,128)(2,1)S(1)}, bf16[640,256]{1,0:T(8,128)(2,1)S(1)}, u32[]{:S(2)}, u32[]{:S(2)}) collective-permute-start(bf16[640,256]{1,0:T(8,128)(2,1)S(1)} %fusion.2), channel_id=1, source_target_pairs={{0,1},{1,0},{2,3},{3,2},{4,5},{5,4},{6,7},{7,6},{8,9},{9,8},{10,11... | collective-permute-start | bytes 983048 | tf_op jit(solution)/shard_map/ppermute | solution.py:593
  13.1 9.3 %collective-permute-start = (bf16[64,128]{1,0:T(8,128)(2,1)S(1)}, bf16[64,128]{1,0:T(8,128)(2,1)S(1)}, u32[]{:S(2)}, u32[]{:S(2)}) collective-permute-start(bf16[64,128]{1,0:T(8,128)(2,1)S(1)} %bitcast.11), channel_id=1, source_target_pairs={{0,1},{1,0},{2,3},{3,2},{4,5},{5,4},{6,7},{7,6},{8,9},{9,8},{10,11... | collective-permute-start | bytes 49160 | tf_op jit(solution)/shard_map/ppermute | solution.py:593
  22.5 0.6 %copy-start.11 = (bf16[64,128]{1,0:T(8,128)(2,1)}, bf16[64,128]{1,0:T(8,128)(2,1)S(1)}, u32[]{:S(2)}) copy-start(bf16[64,128]{1,0:T(8,128)(2,1)S(1)} %collective-permute-done.refs_3_) | copy-start | bytes 49156
  22.5 0.7 %copy-start.7 = (bf16[640,256]{1,0:T(8,128)(2,1)}, bf16[640,256]{1,0:T(8,128)(2,1)S(1)}, u32[]{:S(2)}) copy-start(bf16[640,256]{1,0:T(8,128)(2,1)S(1)} %collective-permute-done.1.refs_8_) | copy-start | bytes 983044
  28.1 3.7 %copy-start.1 = (bf16[16,64,256]{2,1,0:T(8,128)(2,1)}, bf16[16,64,256]{2,1,0:T(8,128)(2,1)S(1)}, u32[]{:S(2)}) copy-start(bf16[16,64,256]{2,1,0:T(8,128)(2,1)S(1)} %all-to-all-done.own_ref.refs_0_) | copy-start | bytes 1572868
  28.1 2.3 %collective-permute-start.2 = (bf16[16,64,256]{2,1,0:T(8,128)(2,1)S(1)}, bf16[16,64,256]{2,1,0:T(8,128)(2,1)S(1)}, u32[]{:S(2)}, u32[]{:S(2)}) collective-permute-start(bf16[16,64,256]{2,1,0:T(8,128)(2,1)S(1)} %all-to-all-done.own_ref.refs_0_), channel_id=1, source_target_pairs={{0,1},{1,0},{2,3},{3,2},{4,5},{5,4},{6,7},{7,6},{8,9},{9,8},{10,11... | collective-permute-start | bytes 1572872 | tf_op jit(solution)/shard_map/ppermute | solution.py:593
  28.1 1.7 %copy-start = (bf16[512,1792]{1,0:T(8,128)(2,1)S(1)}, bf16[512,1792]{1,0:T(8,128)(2,1)}, u32[]{:S(2)}) copy-start(bf16[512,1792]{1,0:T(8,128)(2,1)} %shard_map.214.pack_ref) | copy-start | bytes 5505028
  30.4 1.3 %copy-start.2 = (bf16[16,64,256]{2,1,0:T(8,128)(2,1)}, bf16[16,64,256]{2,1,0:T(8,128)(2,1)S(1)}, u32[]{:S(2)}) copy-start(bf16[16,64,256]{2,1,0:T(8,128)(2,1)S(1)} %collective-permute-done.2.oth_ref.refs_1_) | copy-start | bytes 1572868
  31.7 18.1 %all-to-all-start.1 = ((bf16[16,80,128]{2,1,0:T(8,128)(2,1)}), bf16[16,80,128]{2,1,0:T(8,128)(2,1)S(1)}, u32[]{:S(2)}, u32[]{:S(2)}) async-start(bf16[16,80,128]{2,1,0:T(8,128)(2,1)} %shard_map.217), calls=%async_computation.1 | async-start | bytes 655360 | tf_op jit(solution)/shard_map/all_to_all | solution.py:596
  37.0 14.5 %copy-start.4 = (s32[1,16,32]{2,1,0:T(8,128)S(1)}, s32[1,16,32]{2,1,0:T(8,128)}, u32[]{:S(2)}) copy-start(s32[1,16,32]{2,1,0:T(8,128)} %refs_3_.3) | copy-start | bytes 6148
  45.9 1.8 %collective-permute-start.3 = (bf16[256,512]{1,0:T(8,128)(2,1)}, bf16[256,512]{1,0:T(8,128)(2,1)S(1)}, u32[]{:S(2)}, u32[]{:S(2)}) collective-permute-start(bf16[256,512]{1,0:T(8,128)(2,1)} %shard_map.218.refs_0_), channel_id=1, source_target_pairs={{0,1},{1,0},{2,3},{3,2},{4,5},{5,4},{6,7},{7,6},{8,9},{9,8},{10,11... | collective-permute-start | bytes 786440 | tf_op jit(solution)/shard_map/ppermute | solution.py:593
  47.7 1.0 %copy-start.3 = (bf16[256,512]{1,0:T(8,128)(2,1)S(1)}, bf16[256,512]{1,0:T(8,128)(2,1)}, u32[]{:S(2)}) copy-start(bf16[256,512]{1,0:T(8,128)(2,1)} %shard_map.218.refs_0_) | copy-start | bytes 786436
  49.8 1.7 %collective-permute-start.4 = (bf16[16,80,128]{2,1,0:T(8,128)(2,1)S(1)}, bf16[16,80,128]{2,1,0:T(8,128)(2,1)S(1)}, u32[]{:S(2)}, u32[]{:S(2)}) collective-permute-start(bf16[16,80,128]{2,1,0:T(8,128)(2,1)S(1)} %all-to-all-done.1.refs_0_.refs_2_), channel_id=1, source_target_pairs={{0,1},{1,0},{2,3},{3,2},{4,5},{5,4},{6,7},{7,6},{8,9},{9,8},{10,11... | collective-permute-start | bytes 983048 | tf_op jit(solution)/shard_map/ppermute | solution.py:593

commit v4 on v3

--- a/solution.py
+++ b/solution.py
@@ -40,10 +40,16 @@
 class Operand:
     def __init__(self, copy, ref):
         self.copy, self.ref, self.shape = copy, ref, ref.shape
-        copy.start()
+        self.started = False
+
+    def start(self):
+        if not self.started:
+            self.copy.start()
+            self.started = True
 
     def wait(self):
         if self.copy is not None:
+            self.start()
             self.copy.wait()
             self.copy = None
 
@@ -79,7 +85,7 @@
             copy.wait()
 
 
-def staged(kernel, views, parts, *refs):
+def staged(kernel, views, parts, late, *refs):
     count, outs = len(views), len(parts)
     ins, results, rest = refs[:count], refs[count : count + outs], list(refs[count + outs :])
     in_sems, out_sems = rest[-2:]
@@ -91,6 +97,9 @@
         else:
             room = rest.pop(0)
             operands.append(Operand(pltpu.make_async_copy(view(ref), room, in_sems.at[n]), room))
+    for n, operand in enumerate(operands):
+        if isinstance(operand, Operand) and n not in late:
+            operand.start()
     held = [
         Result(rest.pop(0), ref, out_sems.at[n], part)
         for n, (ref, part) in enumerate(zip(results, parts))
@@ -132,9 +141,21 @@
     return jnp.sum(jnp.where(mine, every, 0.0), axis=0, keepdims=True)
 
 
+def hot_rows(line, start, count):
+    width = line.shape[1]
+    near = (line - start).astype(I32)
+    near = jnp.where((near >= 0) & (near < count), near, -1)
+    near = jnp.broadcast_to(near, (16, width)).astype(jnp.int16)
+    near = jnp.concatenate([near] * (count // 16), axis=0)
+    at = lax.broadcasted_iota(jnp.int16, (count, width), 0)
+    return jnp.where(at == near, jnp.ones((), BF), jnp.zeros((), BF))
+
+
 def rows_at(col, count):
-    at = iota((col.shape[0], count), 1).astype(F32)
-    return one_hot(at == col)
+    near = jnp.broadcast_to(col, (col.shape[0], 128)).astype(I32).astype(jnp.int16)
+    near = jnp.concatenate([near] * (count // 128), axis=1)
+    at = lax.broadcasted_iota(jnp.int16, near.shape, 1)
+    return jnp.where(at == near, jnp.ones((), BF), jnp.zeros((), BF))
 
 
 def half_of(core, half):
@@ -142,7 +163,7 @@
 
 
 def serve_kernel(packed, rows_ref, self_ref, *refs):
-    mems, outs, hot = refs[:4], refs[4:-1], refs[-1]
+    mems, outs, hot = refs[:1], refs[1:-1], refs[-1]
     depth, half = mems[0].shape
     count = len(mems) * depth
     step = 256
@@ -289,6 +310,7 @@
     te_ref,
     wqt_ref,
     wkvt_ref,
+    base_ref,
 ):
     time_kernel(ev_ref, nbr_ref, freq_ref, phase_ref, wq_ref, wk_ref, wv_ref, te_ref, wqt_ref, wkvt_ref)
     te_ref.send(0)
@@ -303,18 +325,16 @@
         picked = dot(rows_at(col[at], count), mem_ref[...]).astype(BF)
         for g in range(3):
             gh_ref[g, at, :] = dot(picked, whid_ref[g])
-
-
-def place_kernel(self_ref, mem_ref, base_ref):
-    count, half = mem_ref.shape
-    serve = self_ref[0]
+    gh_ref.send(0)
     line = row(serve)
+    cols = half_of(lax.axis_index("mp"), width // 2)
     step = count // base_ref.parts
     for part in range(base_ref.parts):
         at = slice(part * step, (part + 1) * step)
-        hit = (iota((step, serve.size), 0) + part * step).astype(F32) == line
-        served = jnp.max(jnp.where(hit, 1.0, 0.0), axis=1, keepdims=True)
-        base_ref[at, :] = (mem_ref[at, :].astype(F32) * (1.0 - served)).astype(BF)
+        hit = hot_rows(line, part * step, step)
+        served = dot(hit, jnp.ones((slots, 128), BF))
+        free = jnp.concatenate([jnp.where(served > 0, 0.0, 1.0)] * (width // 256), axis=1)
+        base_ref[at, :] = (mem_ref[at, cols].astype(F32) * free).astype(BF)
         base_ref.send(part)
 
 
@@ -346,19 +366,14 @@
     half = oth_ref.shape[-1]
     at_sent = pack_places(pack_ref.shape[0], half)[3]
     oth = part_of(oth_ref, packed, cap, cap_self)
-    out = (total_ref[...] + message_part(oth, pack_ref, half, half)).astype(BF)
+    out = total_ref[...] + message_part(oth, pack_ref, half, half)
     if not packed:
-        out_ref[...] = out
+        out_ref[...] = out.astype(BF)
         return
-    tiles = half // 128
-    for tile in range(tiles):
-        out_ref[:, tile * cap_self : (tile + 1) * cap_self, :] = out[
-            :, tile * 128 : (tile + 1) * 128
-        ].reshape(peers, cap_self, 128)
-    sent = pack_ref[:peers, at_sent:].astype(F32)
-    out_ref[:, tiles * cap_self :, :] = jnp.broadcast_to(sent[:, None, :], (peers, 16, 128)).astype(
-        BF
-    )
+    parts = out.reshape(peers, cap_self // 8, 8, half)
+    parts = [parts[:, n] for n in range(cap_self // 8)]
+    parts.append(jnp.broadcast_to(pack_ref[:peers, at_sent:].astype(F32)[:, None, :], (peers, 8, 128)))
+    out_ref[...] = jnp.concatenate(parts, axis=2).astype(BF)
 
 
 def attention_kernel(
@@ -382,6 +397,8 @@
     mine, theirs = half_of(core, half), half_of(1 - core, half)
     fown = part_of(nown_ref, packed, 0, cap)
     foth = part_of(noth_ref, packed, 0, cap)
+    for ref in (te_ref, wout_ref, wself_ref):
+        ref.start()
     slots = fown.shape[0]
     kv_w[:, :slots] = (dot_nt(wkvt_ref[:, mine], fown) + dot_nt(wkvt_ref[:, theirs], foth)).astype(BF)
     kv_w[:, slots:] = wkvt_ref[:, width:]
@@ -396,14 +413,18 @@
     find = jnp.concatenate(tall_one_hot(slot_t_ref, slots_s), axis=1)
     q = dot(query, find) * (1.0 / size**0.5)
     neigh, _, ends = te_ref.shape
-    at = iota((slots, ends), 0)
+    at = lax.broadcasted_iota(jnp.int16, (slots, ends), 0)
+    one, zero = jnp.ones((), BF), jnp.zeros((), BF)
     weights = []
     for k in range(neigh):
         line = jnp.concatenate([nslot_ref[j, k : k + 1, :] for j in range(2)], axis=1)
-        right = jnp.concatenate([one_hot(at == line), te_ref[k]], axis=0)
+        line = jnp.broadcast_to(line, (16, ends)).astype(jnp.int16)
+        line = jnp.concatenate([line] * (slots // 16), axis=0)
+        hot = jnp.where(at == line, one, zero)
+        right = jnp.concatenate([hot, te_ref[k]], axis=0)
         kv = dot(kv_w[...], right)
         value_ref[k] = kv[half:].astype(BF)
-        score = q * kv[:half].astype(BF).astype(F32)
+        score = q * kv[:half]
         score = [
             jnp.sum(score[h * size : (h + 1) * size], axis=0, keepdims=True) for h in range(heads)
         ]
@@ -454,18 +475,15 @@
     rows, half = base_ref.shape
     serve = serve_ref[0]
     slots = serve.size
-    tiles = half // 128
 
     def messages(ref):
         if not packed:
             return ref[...]
-        return jnp.concatenate(
-            [
-                ref[:, tile * cap_self : (tile + 1) * cap_self, :].reshape(slots, 128)
-                for tile in range(tiles)
-            ],
-            axis=1,
-        )
+        values = ref[...].astype(F32)
+        parts = [
+            values[:, None, :, n * half : (n + 1) * half] for n in range(cap_self // 8)
+        ]
+        return jnp.concatenate(parts, axis=1).reshape(slots, half).astype(BF)
 
     line = row(serve)
     match = column(serve, 0, slots) == line
@@ -475,10 +493,11 @@
     line = jnp.where(again > 0, -1.0, line)
     step = rows // out_ref.parts
     for part in range(out_ref.parts):
-        at = (iota((step, slots), 0) + part * step).astype(F32)
-        put[part * step : (part + 1) * step, :] = one_hot(at == line)
+        put[part * step : (part + 1) * step, :] = hot_rows(line, part * step, step)
     peers = slots // cap_self
-    counts = count_ref[:, tiles * cap_self :, :][:, 0, :] if packed else count_ref[...]
+    counts = count_ref[...]
+    if packed:
+        counts = counts.astype(F32)[:, 0, counts.shape[2] - 128 :].astype(BF)
     spread = dot(one_hot(iota((slots, peers), 0) // cap_self == iota((slots, peers), 1)), counts)
     lane = iota((slots, 128), 1)
     spread = jnp.where(iota((slots, 128), 0) % cap_self == lane, spread, 0.0).astype(BF)
@@ -536,7 +555,7 @@
 
     core = lax.axis_index("mp")
 
-    def call(kernel, out_shape, args, flops=0, scratch=(), limit=62, direct=(), views={}, parts=(), small=False):
+    def call(kernel, out_shape, args, flops=0, scratch=(), limit=62, direct=(), views={}, parts=(), small=False, late=()):
         single = not isinstance(out_shape, (list, tuple))
         outs = [out_shape] if single else list(out_shape)
         parts = [*parts, *[1] * (len(outs) - len(parts))]
@@ -551,7 +570,7 @@
             rooms.append(pltpu.VMEM(room, arg.dtype))
         rooms += [pltpu.VMEM(o.shape, o.dtype) for o in outs]
         return pl.pallas_call(
-            functools.partial(staged, kernel, whole, parts),
+            functools.partial(staged, kernel, whole, parts, late),
             out_shape=out_shape,
             in_specs=[HBM if view else VMEM for view in whole],
             out_specs=HBM if single else [HBM] * len(outs),
@@ -600,14 +619,14 @@
         served_shape = shape((peers, cap + cap_self, half), BF)
     else:
         served_shape = [shape((slots_n, half), BF), shape((slots_s, half), BF)]
-    quarter = owned // 4
+    quarter = owned
     served = call(
         functools.partial(serve_kernel, packed),
         served_shape,
-        (serve_rows, serve_self, *[memory] * 4),
+        (serve_rows, serve_self, memory),
         flops_serve,
-        [pltpu.VMEM((512, owned), BF)],
-        views={2 + n: stripe(n, quarter) for n in range(4)},
+        [pltpu.VMEM((1024, owned), BF)],
+        views={2 + n: stripe(n, quarter) for n in range(1)},
         parts=[slots_s // 256] if packed and cap == cap_self else (),
     )
     if packed:
@@ -632,13 +651,14 @@
     edge_swap = swap(edge_t)
     nslot = nbr_slot.transpose(1, 2, 0)
     slot_t = self_slot.T
-    gh, te, wq_t, wkv_t = call(
+    gh, te, wq_t, wkv_t, base = call(
         prepare_kernel,
         [
             shape((3, slots_s, half), F32),
             shape((neigh, tdim, ends), BF),
             shape((half, width + tdim), BF),
             shape((2 * half, width + tdim), BF),
+            shape((owned, half), BF),
         ],
         (
             serve_self,
@@ -653,6 +673,7 @@
             w_value,
         ),
         2 * slots_s * (owned * width + width * 3 * half),
+        parts=[1, 1, 1, 1, 8],
     )
     tpart = w_msg_time.shape[0]
     pack = call(
@@ -670,6 +691,7 @@
             w_swap,
         ),
         4 * slots_s * events * (slots_s + half),
+        limit=50,
         views={
             1: (lambda ref: ref.at[pl.ds(0, 1)], (1, tdim, ends)),
             4: columns(tpart),
@@ -678,21 +700,12 @@
             7: columns(half),
         },
     )
-    base = call(
-        place_kernel,
-        shape((owned, half), BF),
-        (serve_self, memory),
-        0,
-        views={1: columns(owned)},
-        parts=[8],
-    )
-
     fetched, te, pack, gh, base = lax.optimization_barrier((fetched, te, pack, gh, base))
     fetched_x = swap(fetched)
     if packed:
         both = (fetched, fetched_x)
         mine = (fetched, fetched_x)
-        back_shape = shape((peers, (half // 128) * cap_self + 16, 128), BF)
+        back_shape = shape((peers, 8, cap_self // 8 * half + 128), BF)
     else:
         nbr = [f[:, :cap].reshape(slots_n, half) for f in (fetched, fetched_x)]
         mine = [f[:, cap:].reshape(slots_s, half) for f in (fetched, fetched_x)]
@@ -720,7 +733,8 @@
         2 * ends * neigh * (slots_n + tdim) * width,
         [pltpu.VMEM((2 * half, slots_n + tdim), BF), pltpu.VMEM((neigh, half, ends), BF)],
         direct=range(len(both)),
-        limit=62,
+        late=[len(both) + n for n in (2, 6, 7)],
+        limit=53,
     )
     embedding = call(
         sum_kernel, shape((events, 2, width), BF), (part, swap(part)), direct=(0, 1), small=True, limit=52

time: 56.2 us -> 52.6 us (0.936)
  Pallas kernels: 31.8 us -> 26.7 us
  waiting for transfers between devices: 4.85 us -> 8.32 us
  starting transfers between devices: 14.5 us -> 13 us
  local copies, waits for them, and re-layouts: 3.42 us -> 2.22 us
  other arithmetic: 0.03 us -> 0.75 us
    pallas_call x7 -> x6, Pallas kernels: 29.9 us -> 24.8 us  [call(): pl.pallas_call(functools.partial(staged, kernel, whole, parts, late), out...]
    all_to_all x2, waiting for transfers between devices: 1.68 us -> 4.09 us  [exchange(): return lax.all_to_all(x, 'nodes', split_axis=0, concat_axis=0, tiled=True)]
    all_to_all x2, starting transfers between devices: 13.6 us -> 12.2 us  [exchange(): return lax.all_to_all(x, 'nodes', split_axis=0, concat_axis=0, tiled=True)]
    unnamed x24 -> x28, local copies, waits for them, and re-layouts: 3.42 us -> 2.22 us
    ppermute x5, waiting for transfers between devices: 3.17 us -> 4.23 us  [swap(): return lax.ppermute(x, 'mp', [(0, 1), (1, 0)])]
    concatenate x1, other arithmetic: 0.03 us -> 0.75 us  [per_device(): jnp.concatenate([w_msg_self, w_msg_other, w_msg_time, w_msg_edge], axis=0)]
  transfers between devices with their start and end apart: 7 -> 7, of which waited for: 3 -> 4; matrix products, arithmetic and copies ran while one was open for 0% -> 1% of each run, Pallas kernels for 41% -> 35%
where the time goes in v4:
time: 52.6 us; the launch traced here: 52.1 us
  Pallas kernels  26.7 us (51%)
  starting transfers between devices  13 us (25%)
  waiting for transfers between devices  8.32 us (16%)
  local copies, waits for them, and re-layouts  2.22 us (4%)
  between operations  1.04 us (2%)
  other arithmetic  0.75 us (1%)
    pallas_call x6, Pallas kernels, call(): pl.pallas_call(functools.partial(staged, kernel, whole, parts, late), out...  24.8 us
    all_to_all x2, starting transfers between devices, exchange(): return lax.all_to_all(x, 'nodes', split_axis=0, concat_axis=0, tiled=True)  12.2 us
    ppermute x5, waiting for transfers between devices, swap(): return lax.ppermute(x, 'mp', [(0, 1), (1, 0)])  4.23 us
    all_to_all x2, waiting for transfers between devices, exchange(): return lax.all_to_all(x, 'nodes', split_axis=0, concat_axis=0, tiled=True)  4.09 us
    unnamed x28, local copies, waits for them, and re-layouts  2.22 us
    pallas_call x2, Pallas kernels, plain(): pl.pallas_call(kernel, out_shape=out_shape, in_specs=[VMEM] * len(args),...  1.95 us
  transfers between devices with their start and end apart: 7, of which 4 were waited for; matrix products, arithmetic and copies ran while one was open for 1% of the time, Pallas kernels for 35%

profile of v4, /device:TPU:0, one launch (start us, length us, event | category | flops | bytes accessed | tf_op | source)
XLA Modules:
  0.0 52.1 jit_solution(10447306546543072586)
XLA Ops:
  0.6 0.0 copy-start.6
  0.6 0.0 copy-start.5
  0.7 0.0 copy-start.3
  0.7 0.0 copy-start.2
  0.7 3.3 %shard_map.212.refs_6_ = bf16[16,64,256]{2,1,0:T(8,128)(2,1)} custom-call(s32[1,16,32]{2,1,0:T(8,128)} %refs_0_.2, s32[1,16,32]{2,1,0:T(8,128)} %refs_3_.1, bf16[2048,512]{1,0:T(8,128)(2,1)} %refs_5_.2), custom_call_target="tpu_custom_call" | custom-call | flops 1073741824 | bytes 2625536 | tf_op jit(solution)/shard_map/pallas_call | solution.py:572
  4.0 0.0 copy-start.7
  4.0 8.3 %all-to-all-start = ((bf16[16,64,256]{2,1,0:T(8,128)(2,1)}), bf16[16,64,256]{2,1,0:T(8,128)(2,1)S(1)}, u32[]{:S(2)}, u32[]{:S(2)}) async-start(bf16[16,64,256]{2,1,0:T(8,128)(2,1)} %shard_map.212.refs_6_), calls=%async_computation | async-start | bytes 1048576 | tf_op jit(solution)/shard_map/all_to_all | solution.py:615
  12.3 0.0 copy-done.6
  12.4 0.0 copy-done.5
  12.4 0.0 copy-done.3
  12.4 0.0 copy-done.2
  12.4 0.7 %fusion.2 = bf16[640,256]{1,0:T(8,128)(2,1)} fusion(s32[]{:T(128)S(6)} %select_n.3, bf16[256,512]{1,0:T(8,128)(2,1)S(1)} %copy-done.2, bf16[256,512]{1,0:T(8,128)(2,1)S(1)} %copy-done.3, bf16[64,512]{1,0:T(8,128)(2,1)S(1)} %copy-done.5, bf16[64,512]{1,0:T(8,128)(2,1)S(1)} %copy-done.6), kind=kLoop, calls=%fused_computation.6 | loop fusion | flops 1310720 | bytes 983044 | tf_op jit(solution)/shard_map/concatenate | solution.py:644
  13.1 0.0 collective-permute-start.1
  13.1 0.0 copy-done.7
  13.1 0.5 collective-permute-start
  13.7 0.0 copy-start.9
  13.7 6.8 %shard_map.213 = (f32[3,512,256]{2,1,0:T(8,128)}, bf16[16,128,256]{2,1,0:T(8,128)(2,1)}, bf16[256,640]{1,0:T(8,128)(2,1)}, bf16[512,640]{1,0:T(8,128)(2,1)}, bf16[2048,256]{1,0:T(8,128)(2,1)}) custom-call(s32[1,16,32]{2,1,0:T(8,128)} %refs_3_.1, s32[1,128]{1,0:T(1,128)} %bitcast.19, s32[2,16,128]{2,1,0:T(8,128)} %bitcast.18, f32[1,128]{1,0:T(1,128)} %bitcast.20, ...), custom_call_target="tpu_custom_call" | custom-call | flops 1476395008 | bytes 8539648 | tf_op jit(solution)/shard_map/pallas_call | solution.py:572
  20.5 0.0 collective-permute-done.refs_3_
  20.5 0.0 collective-permute-done.1.refs_8_
  20.5 0.0 copy-done.9
  20.5 0.0 copy-start.1
  20.5 1.2 %copy-done.1 = bf16[16,128,256]{2,1,0:T(8,128)(2,1)S(1)} copy-done((bf16[16,128,256]{2,1,0:T(8,128)(2,1)S(1)}, bf16[16,128,256]{2,1,0:T(8,128)(2,1)}, u32[]{:S(2)}) %copy-start.1) | copy-done | bytes 1048600
  21.8 1.6 %shard_map.214.pack_ref = bf16[512,1792]{1,0:T(8,128)(2,1)S(1)} custom-call(s32[2,128]{1,0:T(2,128)S(1)} %bitcast.11, bf16[16,128,256]{2,1,0:T(8,128)(2,1)S(1)} %copy-done.1, bf16[64,128]{1,0:T(8,128)(2,1)S(1)} %bitcast.10, bf16[64,128]{1,0:T(8,128)(2,1)S(1)} %collective-permute-done.refs_3_, bf16[64,512]{1,0:T(8,128)(2,1)S(1)} %copy-done.5, ...), custom_call_target="tpu_custom_call" | custom-call | flops 201326592 | bytes 3900416 | tf_op jit(solution)/shard_map/pallas_call | solution.py:572
  23.4 4.1 %all-to-all-done.own_ref.refs_0_ = bf16[16,64,256]{2,1,0:T(8,128)(2,1)S(1)} async-done(((bf16[16,64,256]{2,1,0:T(8,128)(2,1)}), bf16[16,64,256]{2,1,0:T(8,128)(2,1)S(1)}, u32[]{:S(2)}, u32[]{:S(2)}) %all-to-all-start) | async-done | bytes 524320 | tf_op jit(solution)/shard_map/all_to_all | solution.py:615
  27.5 0.0 collective-permute-start.2
  27.5 0.6 %shard_map.215.total_ref = f32[512,256]{1,0:T(8,128)S(1)} custom-call(bf16[16,64,256]{2,1,0:T(8,128)(2,1)S(1)} %all-to-all-done.own_ref.refs_0_, bf16[512,1792]{1,0:T(8,128)(2,1)S(1)} %shard_map.214.pack_ref), custom_call_target="tpu_custom_call" | custom-call | flops 201326592 | bytes 2883584 | tf_op jit(solution)/shard_map/pallas_call | solution.py:591
  28.1 0.0 copy-start.10
  28.1 0.0 copy-start.12
  28.1 0.0 copy-start.13
  28.1 1.3 %collective-permute-done.2.oth_ref.refs_1_ = bf16[16,64,256]{2,1,0:T(8,128)(2,1)S(1)} collective-permute-done((bf16[16,64,256]{2,1,0:T(8,128)(2,1)S(1)}, bf16[16,64,256]{2,1,0:T(8,128)(2,1)S(1)}, u32[]{:S(2)}, u32[]{:S(2)}) %collective-permute-start.2) | collective-permute-done | bytes 524320 | tf_op jit(solution)/shard_map/ppermute | solution.py:612
  29.4 1.3 %shard_map.216 = bf16[16,8,1152]{2,1,0:T(8,128)(2,1)} custom-call(bf16[16,64,256]{2,1,0:T(8,128)(2,1)S(1)} %collective-permute-done.2.oth_ref.refs_1_, bf16[512,1792]{1,0:T(8,128)(2,1)S(1)} %shard_map.214.pack_ref, f32[512,256]{1,0:T(8,128)S(1)} %shard_map.215.total_ref), custom_call_target="tpu_custom_call" | custom-call | flops 201326592 | bytes 3178496 | tf_op jit(solution)/shard_map/pallas_call | solution.py:591
  30.7 0.0 copy-done
  30.7 0.0 copy-done.4
  30.7 3.9 %all-to-all-start.1 = ((bf16[16,8,1152]{2,1,0:T(8,128)(2,1)}), bf16[16,8,1152]{2,1,0:T(8,128)(2,1)S(1)}, u32[]{:S(2)}, u32[]{:S(2)}) async-start(bf16[16,8,1152]{2,1,0:T(8,128)(2,1)} %shard_map.216), calls=%async_computation.1 | async-start | bytes 589824 | tf_op jit(solution)/shard_map/all_to_all | solution.py:615
  34.7 0.0 copy-done.10
  34.7 0.0 copy-done.12
  34.7 0.0 copy-done.13
  34.7 0.0 copy-start.11
  34.7 0.9 %copy-done.11 = bf16[256,512]{1,0:T(8,128)(2,1)S(1)} copy-done((bf16[256,512]{1,0:T(8,128)(2,1)S(1)}, bf16[256,512]{1,0:T(8,128)(2,1)}, u32[]{:S(2)}) %copy-start.11) | copy-done | bytes 262168
  35.6 7.9 %shard_map.217.refs_0_ = bf16[256,512]{1,0:T(8,128)(2,1)S(1)} custom-call(bf16[16,64,256]{2,1,0:T(8,128)(2,1)} %copy-done, bf16[16,64,256]{2,1,0:T(8,128)(2,1)} %copy-done.4, bf16[512,640]{1,0:T(8,128)(2,1)} %get-tuple-element.22.refs_2_, s32[2,16,128]{2,1,0:T(8,128)S(1)} %bitcast.13, bf16[16,128,256]{2,1,0:T(8,128)(2,1)} %get-tuple-element.23.refs_1_.refs_4_, ...), custom_call_target="tpu_custom_call" | custom-call | flops 2684354560 | bytes 3884544 | tf_op jit(solution)/shard_map/pallas_call | solution.py:572
  43.6 0.1 collective-permute-start.3
  43.7 1.5 %collective-permute-done.3.refs_1_ = bf16[256,512]{1,0:T(8,128)(2,1)S(1)} collective-permute-done((bf16[256,512]{1,0:T(8,128)(2,1)S(1)}, bf16[256,512]{1,0:T(8,128)(2,1)S(1)}, u32[]{:S(2)}, u32[]{:S(2)}) %collective-permute-start.3) | collective-permute-done | bytes 262176 | tf_op jit(solution)/shard_map/ppermute | solution.py:612
  45.2 1.2 %shard_map.218 = bf16[128,2,512]{2,1,0:T(2,128)(2,1)} custom-call(bf16[256,512]{1,0:T(8,128)(2,1)S(1)} %shard_map.217.refs_0_, bf16[256,512]{1,0:T(8,128)(2,1)S(1)} %collective-permute-done.3.refs_1_), custom_call_target="tpu_custom_call" | custom-call | bytes 1 | tf_op jit(solution)/shard_map/pallas_call | solution.py:572
  46.3 0.0 all-to-all-done.1.refs_0_.refs_2_
  46.4 0.2 collective-permute-start.4
  46.6 1.4 %collective-permute-done.4.refs_1_ = bf16[16,8,1152]{2,1,0:T(8,128)(2,1)S(1)} collective-permute-done((bf16[16,8,1152]{2,1,0:T(8,128)(2,1)S(1)}, bf16[16,8,1152]{2,1,0:T(8,128)(2,1)S(1)}, u32[]{:S(2)}, u32[]{:S(2)}) %collective-permute-start.4) | collective-permute-done | bytes 294944 | tf_op jit(solution)/shard_map/ppermute | solution.py:612
  48.0 0.0 copy-done.8
  48.0 3.9 %shard_map.219 = bf16[2048,256]{1,0:T(8,128)(2,1)} custom-call(bf16[16,8,1152]{2,1,0:T(8,128)(2,1)S(1)} %all-to-all-done.1.refs_0_.refs_2_, bf16[16,8,1152]{2,1,0:T(8,128)(2,1)S(1)} %collective-permute-done.4.refs_1_, bf16[16,8,1152]{2,1,0:T(8,128)(2,1)S(1)} %all-to-all-done.1.refs_0_.refs_2_, s32[1,16,32]{2,1,0:T(8,128)S(1)} %copy-done.8, ...), custom_call_target="tpu_custom_call" | custom-call | flops 1207959552 | bytes 5867520 | tf_op jit(solution)/shard_map/pallas_call | solution.py:572
  (3 shorter events, 0.0 us)
Async XLA Ops:
  0.6 11.7 %copy-start.6 = (bf16[64,512]{1,0:T(8,128)(2,1)S(1)}, bf16[64,512]{1,0:T(8,128)(2,1)}, u32[]{:S(2)}) copy-start(bf16[64,512]{1,0:T(8,128)(2,1)} %refs_5_.3) | copy-start | bytes 196612
  0.6 11.7 %copy-start.5 = (bf16[64,512]{1,0:T(8,128)(2,1)S(1)}, bf16[64,512]{1,0:T(8,128)(2,1)}, u32[]{:S(2)}) copy-start(bf16[64,512]{1,0:T(8,128)(2,1)} %refs_4_.1) | copy-start | bytes 196612
  0.7 11.7 %copy-start.3 = (bf16[256,512]{1,0:T(8,128)(2,1)S(1)}, bf16[256,512]{1,0:T(8,128)(2,1)}, u32[]{:S(2)}) copy-start(bf16[256,512]{1,0:T(8,128)(2,1)} %refs_7_.3) | copy-start | bytes 786436
  0.7 11.7 %copy-start.2 = (bf16[256,512]{1,0:T(8,128)(2,1)S(1)}, bf16[256,512]{1,0:T(8,128)(2,1)}, u32[]{:S(2)}) copy-start(bf16[256,512]{1,0:T(8,128)(2,1)} %refs_6_.1) | copy-start | bytes 786436
  4.0 9.1 %copy-start.7 = (bf16[128,64]{0,1:T(8,128)(2,1)S(1)}, bf16[128,64]{0,1:T(8,128)(2,1)}, u32[]{:S(2)}) copy-start(bf16[128,64]{0,1:T(8,128)(2,1)} %param.24) | copy-start | bytes 49156
  4.0 23.5 %all-to-all-start = ((bf16[16,64,256]{2,1,0:T(8,128)(2,1)}), bf16[16,64,256]{2,1,0:T(8,128)(2,1)S(1)}, u32[]{:S(2)}, u32[]{:S(2)}) async-start(bf16[16,64,256]{2,1,0:T(8,128)(2,1)} %shard_map.212.refs_6_), calls=%async_computation | async-start | bytes 1048576 | tf_op jit(solution)/shard_map/all_to_all | solution.py:615
  13.1 7.4 %collective-permute-start.1 = (bf16[640,256]{1,0:T(8,128)(2,1)}, bf16[640,256]{1,0:T(8,128)(2,1)S(1)}, u32[]{:S(2)}, u32[]{:S(2)}) collective-permute-start(bf16[640,256]{1,0:T(8,128)(2,1)} %fusion.2), channel_id=1, source_target_pairs={{0,1},{1,0},{2,3},{3,2},{4,5},{5,4},{6,7},{7,6},{8,9},{9,8},{10,11... | collective-permute-start | bytes 983048 | tf_op jit(solution)/shard_map/ppermute | solution.py:612
  13.1 7.4 %collective-permute-start = (bf16[64,128]{1,0:T(8,128)(2,1)S(1)}, bf16[64,128]{1,0:T(8,128)(2,1)S(1)}, u32[]{:S(2)}, u32[]{:S(2)}) collective-permute-start(bf16[64,128]{1,0:T(8,128)(2,1)S(1)} %bitcast.9), channel_id=1, source_target_pairs={{0,1},{1,0},{2,3},{3,2},{4,5},{5,4},{6,7},{7,6},{8,9},{9,8},{10,11... | collective-permute-start | bytes 49160 | tf_op jit(solution)/shard_map/ppermute | solution.py:612
  13.7 6.9 %copy-start.9 = (s32[128,2]{0,1:T(2,128)S(1)}, s32[128,2]{0,1:T(2,128)}, u32[]{:S(2)}) copy-start(s32[128,2]{0,1:T(2,128)} %param.25) | copy-start | bytes 3076
  20.5 1.2 %copy-start.1 = (bf16[16,128,256]{2,1,0:T(8,128)(2,1)S(1)}, bf16[16,128,256]{2,1,0:T(8,128)(2,1)}, u32[]{:S(2)}) copy-start(bf16[16,128,256]{2,1,0:T(8,128)(2,1)} %get-tuple-element.23.refs_1_.refs_4_) | copy-start | bytes 3145732
  27.5 3.3 %copy-start = (bf16[16,64,256]{2,1,0:T(8,128)(2,1)}, bf16[16,64,256]{2,1,0:T(8,128)(2,1)S(1)}, u32[]{:S(2)}) copy-start(bf16[16,64,256]{2,1,0:T(8,128)(2,1)S(1)} %all-to-all-done.own_ref.refs_0_) | copy-start | bytes 1572868
  27.5 1.9 %collective-permute-start.2 = (bf16[16,64,256]{2,1,0:T(8,128)(2,1)S(1)}, bf16[16,64,256]{2,1,0:T(8,128)(2,1)S(1)}, u32[]{:S(2)}, u32[]{:S(2)}) collective-permute-start(bf16[16,64,256]{2,1,0:T(8,128)(2,1)S(1)} %all-to-all-done.own_ref.refs_0_), channel_id=1, source_target_pairs={{0,1},{1,0},{2,3},{3,2},{4,5},{5,4},{6,7},{7,6},{8,9},{9,8},{10,11... | collective-permute-start | bytes 1572872 | tf_op jit(solution)/shard_map/ppermute | solution.py:612
  28.1 6.5 %copy-start.10 = (bf16[256,512]{1,0:T(8,128)(2,1)S(1)}, bf16[256,512]{1,0:T(8,128)(2,1)}, u32[]{:S(2)}) copy-start(bf16[256,512]{1,0:T(8,128)(2,1)} %refs_8_.3) | copy-start | bytes 786436
  28.1 6.5 %copy-start.12 = (s32[128,2,16]{0,2,1:T(8,128)S(1)}, s32[128,2,16]{0,2,1:T(8,128)}, u32[]{:S(2)}) copy-start(s32[128,2,16]{0,2,1:T(8,128)} %param.26) | copy-start | bytes 49156
  28.1 6.5 %copy-start.13 = (f32[128]{0:T(128)S(1)}, f32[128]{0:T(128)}, u32[]{:S(2)}) copy-start(f32[128]{0:T(128)} %param.30) | copy-start | bytes 1540
  29.4 1.3 %copy-start.4 = (bf16[16,64,256]{2,1,0:T(8,128)(2,1)}, bf16[16,64,256]{2,1,0:T(8,128)(2,1)S(1)}, u32[]{:S(2)}) copy-start(bf16[16,64,256]{2,1,0:T(8,128)(2,1)S(1)} %collective-permute-done.2.oth_ref.refs_1_) | copy-start | bytes 1572868
  30.7 15.6 %all-to-all-start.1 = ((bf16[16,8,1152]{2,1,0:T(8,128)(2,1)}), bf16[16,8,1152]{2,1,0:T(8,128)(2,1)S(1)}, u32[]{:S(2)}, u32[]{:S(2)}) async-start(bf16[16,8,1152]{2,1,0:T(8,128)(2,1)} %shard_map.216), calls=%async_computation.1 | async-start | bytes 589824 | tf_op jit(solution)/shard_map/all_to_all | solution.py:615
  34.7 1.0 %copy-start.11 = (bf16[256,512]{1,0:T(8,128)(2,1)S(1)}, bf16[256,512]{1,0:T(8,128)(2,1)}, u32[]{:S(2)}) copy-start(bf16[256,512]{1,0:T(8,128)(2,1)} %refs_9_.3) | copy-start | bytes 786436
  35.6 12.4 %copy-start.8 = (s32[1,16,32]{2,1,0:T(8,128)S(1)}, s32[1,16,32]{2,1,0:T(8,128)}, u32[]{:S(2)}) copy-start(s32[1,16,32]{2,1,0:T(8,128)} %refs_3_.1) | copy-start | bytes 6148
  43.6 1.6 %collective-permute-start.3 = (bf16[256,512]{1,0:T(8,128)(2,1)S(1)}, bf16[256,512]{1,0:T(8,128)(2,1)S(1)}, u32[]{:S(2)}, u32[]{:S(2)}) collective-permute-start(bf16[256,512]{1,0:T(8,128)(2,1)S(1)} %shard_map.217.refs_0_), channel_id=1, source_target_pairs={{0,1},{1,0},{2,3},{3,2},{4,5},{5,4},{6,7},{7,6},{8,9},{9,8},{10,11... | collective-permute-start | bytes 786440 | tf_op jit(solution)/shard_map/ppermute | solution.py:612
  46.4 1.6 %collective-permute-start.4 = (bf16[16,8,1152]{2,1,0:T(8,128)(2,1)S(1)}, bf16[16,8,1152]{2,1,0:T(8,128)(2,1)S(1)}, u32[]{:S(2)}, u32[]{:S(2)}) collective-permute-start(bf16[16,8,1152]{2,1,0:T(8,128)(2,1)S(1)} %all-to-all-done.1.refs_0_.refs_2_), channel_id=1, source_target_pairs={{0,1},{1,0},{2,3},{3,2},{4,5},{5,4},{6,7},{7,6},{8,9},{9,8},{10,11... | collective-permute-start | bytes 884744 | tf_op jit(solution)/shard_map/ppermute | solution.py:612

commit v5 on v4

--- a/solution.py
+++ b/solution.py
@@ -210,21 +210,32 @@
     return jnp.broadcast_to(line, (count, line.shape[1])).T
 
 
-def time_kernel(ev_ref, nbr_ref, freq_ref, phase_ref, wq_ref, wk_ref, wv_ref, te_ref, wqt_ref, wkvt_ref):
-    neigh, tdim, ends = te_ref.shape
+def time_kernel(
+    ev_ref, nbr_ref, freq_ref, phase_ref, wq_ref, wk_ref, wv_ref, te_ref, wqt_ref, wkvt_ref, kvte_ref
+):
+    neigh, ends = kvte_ref.shape[0] - 3, kvte_ref.shape[2]
+    tdim = te_ref.shape[1]
     events = ends // 2
     freq = down(freq_ref[...], events)
     phase = down(phase_ref[...], events)
     time = ev_ref[...]
-    for k in range(neigh):
-        for j in range(2):
-            delta = (time - nbr_ref[j, k : k + 1, :]).astype(F32)
-            enc = encode_turns(delta * freq + phase)
-            te_ref[k, :, j * events : (j + 1) * events] = enc.astype(BF)
     half = wq_ref.shape[1]
     wqt_ref[...] = wq_ref[...].T
     wkvt_ref[:half, :] = wk_ref[...].T
     wkvt_ref[half:, :] = wv_ref[...].T
+    wqt_ref.send(0)
+    wkvt_ref.send(0)
+    weight = wkvt_ref[:, wkvt_ref.shape[1] - tdim :]
+    for k in range(neigh):
+        enc = []
+        for j in range(2):
+            delta = (time - nbr_ref[j, k : k + 1, :]).astype(F32)
+            enc.append(encode_turns(delta * freq + phase).astype(BF))
+        enc = jnp.concatenate(enc, axis=1)
+        if k == 0:
+            te_ref[0] = enc
+        kvte_ref[k] = dot(weight, enc).astype(BF)
+        kvte_ref.send(k)
 
 
 def tall_one_hot(slot_t_ref, slots):
@@ -306,16 +317,22 @@
     wq_ref,
     wk_ref,
     wv_ref,
+    win_ref,
     gh_ref,
     te_ref,
     wqt_ref,
     wkvt_ref,
     base_ref,
+    kvte_ref,
 ):
-    time_kernel(ev_ref, nbr_ref, freq_ref, phase_ref, wq_ref, wk_ref, wv_ref, te_ref, wqt_ref, wkvt_ref)
+    time_kernel(
+        ev_ref, nbr_ref, freq_ref, phase_ref, wq_ref, wk_ref, wv_ref, te_ref, wqt_ref, wkvt_ref, kvte_ref
+    )
     te_ref.send(0)
-    wqt_ref.send(0)
-    wkvt_ref.send(0)
+    planes = kvte_ref.shape[0]
+    for g in range(3):
+        kvte_ref[planes - 3 + g] = win_ref[g]
+        kvte_ref.send(planes - 3 + g)
     count, width = mem_ref.shape
     serve = self_ref[0]
     slots = serve.size
@@ -385,8 +402,8 @@
     own_refs, oth_refs, refs = (refs[:1], refs[1:2], refs[2:]) if packed else (
         refs[:2], refs[2:4], refs[4:]
     )
-    wkvt_ref, nslot_ref, te_ref, wqt_ref, slot_t_ref, phase_ref, wout_ref, wself_ref = refs[:8]
-    emb_ref, kv_w, value_ref = refs[8:]
+    wkvt_ref, nslot_ref, wqt_ref, slot_t_ref, phase_ref, wout_ref, wself_ref = refs[:7]
+    te_refs, (emb_ref, kv_w, value_ref) = refs[7:-3], refs[-3:]
     nown_ref, sown_ref = own_refs[0], own_refs[-1]
     noth_ref, soth_ref = oth_refs[0], oth_refs[-1]
     core = lax.axis_index("mp")
@@ -397,11 +414,10 @@
     mine, theirs = half_of(core, half), half_of(1 - core, half)
     fown = part_of(nown_ref, packed, 0, cap)
     foth = part_of(noth_ref, packed, 0, cap)
-    for ref in (te_ref, wout_ref, wself_ref):
+    for ref in (*te_refs, wout_ref, wself_ref):
         ref.start()
     slots = fown.shape[0]
-    kv_w[:, :slots] = (dot_nt(wkvt_ref[:, mine], fown) + dot_nt(wkvt_ref[:, theirs], foth)).astype(BF)
-    kv_w[:, slots:] = wkvt_ref[:, width:]
+    kv_w[...] = (dot_nt(wkvt_ref[:, mine], fown) + dot_nt(wkvt_ref[:, theirs], foth)).astype(BF)
     xown = part_of(sown_ref, packed, cap, cap_self)
     xoth = part_of(soth_ref, packed, cap, cap_self)
     slots_s = xown.shape[0]
@@ -412,7 +428,8 @@
     query = (query + jnp.concatenate([query_te] * (slots_s // 128), axis=1)).astype(BF)
     find = jnp.concatenate(tall_one_hot(slot_t_ref, slots_s), axis=1)
     q = dot(query, find) * (1.0 / size**0.5)
-    neigh, _, ends = te_ref.shape
+    neigh, depth = nslot_ref.shape[1], te_refs[0].shape[0]
+    ends = te_refs[0].shape[2]
     at = lax.broadcasted_iota(jnp.int16, (slots, ends), 0)
     one, zero = jnp.ones((), BF), jnp.zeros((), BF)
     weights = []
@@ -421,8 +438,7 @@
         line = jnp.broadcast_to(line, (16, ends)).astype(jnp.int16)
         line = jnp.concatenate([line] * (slots // 16), axis=0)
         hot = jnp.where(at == line, one, zero)
-        right = jnp.concatenate([hot, te_ref[k]], axis=0)
-        kv = dot(kv_w[...], right)
+        kv = dot(kv_w[...], hot) + te_refs[k // depth][k % depth].astype(F32)
         value_ref[k] = kv[half:].astype(BF)
         score = q * kv[:half]
         score = [
@@ -451,10 +467,17 @@
     emb_ref[...] = (dot(att, wout_ref[...]) + dot(self_own, wself_ref[...])).astype(BF)
 
 
-def sum_kernel(own_ref, oth_ref, out_ref):
+def sum_kernel(own_ref, oth_ref, _, out_ref):
     total = own_ref[...].astype(F32) + oth_ref[...].astype(F32)
     events = out_ref.shape[0]
     out_ref[...] = jnp.stack([total[:events], total[events:]], axis=1).astype(BF)
+
+
+def touch_kernel(*refs):
+    refs[-1][...] = sum(
+        (ref[:8, :128] if len(ref.shape) == 2 else ref[0, :8, :128]).astype(F32)
+        for ref in refs[:-1]
+    )
 
 
 def update_kernel(
@@ -510,7 +533,7 @@
     reset = jax.nn.sigmoid(gi[0] + gh_ref[0])
     gate = jax.nn.sigmoid(gi[1] + gh_ref[1])
     cand = jnp.tanh(gi[2] + reset * gh_ref[2])
-    old = old_ref[...].reshape(slots, half).astype(F32)
+    old = part_of(old_ref, packed, old_ref.shape[1] - cap_self, cap_self).astype(F32)
     fresh = jnp.where(count > 0, (1.0 - gate) * cand + gate * old, old).astype(BF)
     for part in range(out_ref.parts):
         at = slice(part * step, (part + 1) * step)
@@ -580,7 +603,7 @@
                 pltpu.SemaphoreType.DMA((len(args),)),
                 pltpu.SemaphoreType.DMA((len(outs), max(parts))),
             ],
-            compiler_params=pltpu.CompilerParams(vmem_limit_bytes=limit * 1024 * 1024),
+            compiler_params=pltpu.CompilerParams(vmem_limit_bytes=int(limit * 1024 * 1024)),
             cost_estimate=pl.CostEstimate(
                 flops=int(flops), bytes_accessed=1 if small else int(size), transcendentals=0
             ),
@@ -593,7 +616,7 @@
             out_shape=out_shape,
             in_specs=[VMEM] * len(args),
             out_specs=VMEM,
-            compiler_params=pltpu.CompilerParams(vmem_limit_bytes=limit * 1024 * 1024),
+            compiler_params=pltpu.CompilerParams(vmem_limit_bytes=int(limit * 1024 * 1024)),
             cost_estimate=pl.CostEstimate(
                 flops=int(flops), bytes_accessed=int(size), transcendentals=0
             ),
@@ -651,14 +674,15 @@
     edge_swap = swap(edge_t)
     nslot = nbr_slot.transpose(1, 2, 0)
     slot_t = self_slot.T
-    gh, te, wq_t, wkv_t, base = call(
+    gh, te, wq_t, wkv_t, base, kvte = call(
         prepare_kernel,
         [
             shape((3, slots_s, half), F32),
-            shape((neigh, tdim, ends), BF),
+            shape((1, tdim, ends), BF),
             shape((half, width + tdim), BF),
             shape((2 * half, width + tdim), BF),
             shape((owned, half), BF),
+            shape((neigh + 3, 2 * half, ends), BF),
         ],
         (
             serve_self,
@@ -671,9 +695,10 @@
             w_query,
             w_key,
             w_value,
+            w_in.transpose(1, 0, 2),
         ),
         2 * slots_s * (owned * width + width * 3 * half),
-        parts=[1, 1, 1, 1, 8],
+        parts=[1, 1, 1, 1, 8, neigh + 3],
     )
     tpart = w_msg_time.shape[0]
     pack = call(
@@ -693,14 +718,13 @@
         4 * slots_s * events * (slots_s + half),
         limit=50,
         views={
-            1: (lambda ref: ref.at[pl.ds(0, 1)], (1, tdim, ends)),
             4: columns(tpart),
             5: columns(w_msg_edge.shape[0]),
             6: columns(half),
             7: columns(half),
         },
     )
-    fetched, te, pack, gh, base = lax.optimization_barrier((fetched, te, pack, gh, base))
+    fetched, kvte, pack, gh, base = lax.optimization_barrier((fetched, kvte, pack, gh, base))
     fetched_x = swap(fetched)
     if packed:
         both = (fetched, fetched_x)
@@ -729,15 +753,24 @@
     part = call(
         functools.partial(attention_kernel, packed, cap, cap_self),
         shape((ends, width), BF),
-        (*both, wkv_t, nslot, te, wq_t, slot_t2, phase[None], w_out, w_self),
+        (*both, wkv_t, nslot, wq_t, slot_t2, phase[None], w_out, w_self, *[kvte] * 4),
         2 * ends * neigh * (slots_n + tdim) * width,
-        [pltpu.VMEM((2 * half, slots_n + tdim), BF), pltpu.VMEM((neigh, half, ends), BF)],
+        [pltpu.VMEM((2 * half, slots_n), BF), pltpu.VMEM((neigh, half, ends), BF)],
         direct=range(len(both)),
-        late=[len(both) + n for n in (2, 6, 7)],
+        late=[len(both) + n for n in range(5, 11)],
+        views={
+            len(both) + 7 + n: (
+                lambda ref, n=n: ref.at[pl.ds(n * (neigh // 4), neigh // 4)],
+                (neigh // 4, 2 * half, ends),
+            )
+            for n in range(4)
+        },
         limit=53,
     )
+    part, gh, base = lax.optimization_barrier((part, gh, base))
+    ready = plain(touch_kernel, shape((8, 128), F32), (gh,), 0, 49)
     embedding = call(
-        sum_kernel, shape((events, 2, width), BF), (part, swap(part)), direct=(0, 1), small=True, limit=52
+        sum_kernel, shape((events, 2, width), BF), (part, swap(part), ready), direct=(0, 1, 2), small=True, limit=49
     )
     if not packed:
         message = jnp.concatenate(
@@ -758,13 +791,13 @@
     memory_out = call(
         functools.partial(update_kernel, packed, cap_self),
         shape((owned, half), BF),
-        (back, back_x, counts, serve_self, w_in.transpose(1, 0, 2), gh, old, base),
+        (back, back_x, counts, serve_self, kvte, gh, old, base),
         2 * slots_s * (slots_s * width + width * 3 * half + owned * half),
         [pltpu.VMEM((owned, slots_s), BF)],
-        direct=(0, 1, 2),
-        views={6: old_view},
+        direct=(0,1,2,5,6,7),
+        views={4: (lambda ref: ref.at[pl.ds(neigh, 3)], (3, width, half))},
         parts=[8],
-        limit=53,
+        limit=49,
     )
     return (embedding, memory_out)
 

time: 52.6 us -> 52.3 us (level)
  Pallas kernels: 26.7 us -> 28.3 us
  waiting for transfers between devices: 8.32 us -> 6.8 us
  local copies, waits for them, and re-layouts: 2.22 us -> 0.91 us
  starting transfers between devices: 13 us -> 13.9 us
    all_to_all x2, waiting for transfers between devices: 4.09 us -> 2.47 us  [exchange(): return lax.all_to_all(x, 'nodes', split_axis=0, concat_axis=0, tiled=True)]
    pallas_call x6, Pallas kernels: 24.8 us -> 26.4 us  [call(): pl.pallas_call(functools.partial(staged, kernel, whole, parts, late), out...]
    unnamed x28 -> x34, local copies, waits for them, and re-layouts: 2.22 us -> 0.91 us
    all_to_all x2, starting transfers between devices: 12.2 us -> 13.4 us  [exchange(): return lax.all_to_all(x, 'nodes', split_axis=0, concat_axis=0, tiled=True)]
    pallas_call x2 -> x3, Pallas kernels: 1.95 us -> 1.93 us  [plain(): pl.pallas_call(kernel, out_shape=out_shape, in_specs=[VMEM] * len(args),...]
  transfers between devices with their start and end apart: 7 -> 7, of which waited for: 4 -> 5; matrix products, arithmetic and copies ran while one was open for 1% -> 2% of each run, Pallas kernels for 35% -> 39%
where the time goes in v5:
time: 52.3 us; the launch traced here: 51.8 us
  Pallas kernels  28.3 us (54%)
  starting transfers between devices  13.9 us (27%)
  waiting for transfers between devices  6.8 us (13%)
  between operations  1.1 us (2%)
  local copies, waits for them, and re-layouts  0.91 us (2%)
  other arithmetic  0.8 us (2%)
    pallas_call x6, Pallas kernels, call(): pl.pallas_call(functools.partial(staged, kernel, whole, parts, late), out...  26.4 us
    all_to_all x2, starting transfers between devices, exchange(): return lax.all_to_all(x, 'nodes', split_axis=0, concat_axis=0, tiled=True)  13.4 us
    ppermute x5, waiting for transfers between devices, swap(): return lax.ppermute(x, 'mp', [(0, 1), (1, 0)])  4.33 us
    all_to_all x2, waiting for transfers between devices, exchange(): return lax.all_to_all(x, 'nodes', split_axis=0, concat_axis=0, tiled=True)  2.47 us
    pallas_call x3, Pallas kernels, plain(): pl.pallas_call(kernel, out_shape=out_shape, in_specs=[VMEM] * len(args),...  1.93 us
  transfers between devices with their start and end apart: 7, of which 5 were waited for; matrix products, arithmetic and copies ran while one was open for 2% of the time, Pallas kernels for 39%

profile of v5, /device:TPU:0, one launch (start us, length us, event | category | flops | bytes accessed | tf_op | source)
XLA Modules:
  0.0 51.8 jit_solution(2554810373679875103)
XLA Ops:
  0.6 0.0 copy-start.10
  0.6 0.0 copy-start.9
  0.7 0.0 copy-start.5
  0.7 0.0 copy-start.4
  0.7 0.0 copy-start.12
  0.7 3.3 %shard_map.212.refs_6_ = bf16[16,64,256]{2,1,0:T(8,128)(2,1)} custom-call(s32[1,16,32]{2,1,0:T(8,128)} %refs_0_.2, s32[1,16,32]{2,1,0:T(8,128)} %refs_3_.1, bf16[2048,512]{1,0:T(8,128)(2,1)} %refs_5_.2), custom_call_target="tpu_custom_call" | custom-call | flops 1073741824 | bytes 2625536 | tf_op jit(solution)/shard_map/pallas_call | solution.py:595
  4.0 8.3 %all-to-all-start = ((bf16[16,64,256]{2,1,0:T(8,128)(2,1)}), bf16[16,64,256]{2,1,0:T(8,128)(2,1)S(1)}, u32[]{:S(2)}, u32[]{:S(2)}) async-start(bf16[16,64,256]{2,1,0:T(8,128)(2,1)} %shard_map.212.refs_6_), calls=%async_computation | async-start | bytes 1048576 | tf_op jit(solution)/shard_map/all_to_all | solution.py:638
  12.3 0.0 copy-done.10
  12.4 0.0 copy-done.9
  12.4 0.0 copy-done.5
  12.4 0.0 copy-done.4
  12.4 0.8 %fusion.2 = bf16[640,256]{1,0:T(8,128)(2,1)} fusion(s32[]{:T(128)S(6)} %select_n.3, bf16[256,512]{1,0:T(8,128)(2,1)S(1)} %copy-done.4, bf16[256,512]{1,0:T(8,128)(2,1)S(1)} %copy-done.5, bf16[64,512]{1,0:T(8,128)(2,1)S(1)} %copy-done.9, bf16[64,512]{1,0:T(8,128)(2,1)S(1)} %copy-done.10), kind=kLoop, calls=%fused_computation.6 | loop fusion | flops 1310720 | bytes 983044 | tf_op jit(solution)/shard_map/concatenate | solution.py:667
  13.2 0.0 collective-permute-start.1
  13.2 0.0 copy-done.12
  13.2 0.5 collective-permute-start
  13.7 9.3 %shard_map.213 = (f32[3,512,256]{2,1,0:T(8,128)}, bf16[1,128,256]{2,1,0:T(8,128)(2,1)}, bf16[256,640]{1,0:T(8,128)(2,1)}, bf16[512,640]{1,0:T(8,128)(2,1)}, bf16...) custom-call(s32[1,16,32]{2,1,0:T(8,128)} %refs_3_.1, s32[1,128]{1,0:T(1,128)} %bitcast.19, s32[2,16,128]{2,1,0:T(8,128)} %bitcast.18, ...), custom_call_target="tpu_custom_call" | custom-call | flops 1476395008 | bytes 13323776 | tf_op jit(solution)/shard_map/pallas_call | solution.py:595
  23.0 0.0 collective-permute-done.refs_3_
  23.0 0.0 collective-permute-done.1.refs_8_
  23.0 0.0 copy-done.15
  23.0 0.0 copy-start.11
  23.1 0.8 %copy-done.11 = bf16[1,128,256]{2,1,0:T(8,128)(2,1)S(1)} copy-done((bf16[1,128,256]{2,1,0:T(8,128)(2,1)S(1)}, bf16[1,128,256]{2,1,0:T(8,128)(2,1)}, u32[]{:S(2)}) %copy-start.11) | copy-done | bytes 65560
  23.9 1.6 %shard_map.214.pack_ref = bf16[512,1792]{1,0:T(8,128)(2,1)S(1)} custom-call(s32[2,128]{1,0:T(2,128)S(1)} %bitcast.12, bf16[1,128,256]{2,1,0:T(8,128)(2,1)S(1)} %copy-done.11, bf16[64,128]{1,0:T(8,128)(2,1)S(1)} %bitcast.10, bf16[64,128]{1,0:T(8,128)(2,1)S(1)} %collective-permute-done.refs_3_, bf16[64,512]{1,0:T(8,128)(2,1)S(1)} %copy-done.9, ...), custom_call_target="tpu_custom_call" | custom-call | flops 201326592 | bytes 2917376 | tf_op jit(solution)/shard_map/pallas_call | solution.py:595
  25.5 2.0 %all-to-all-done.own_ref.refs_0_ = bf16[16,64,256]{2,1,0:T(8,128)(2,1)S(1)} async-done(((bf16[16,64,256]{2,1,0:T(8,128)(2,1)}), bf16[16,64,256]{2,1,0:T(8,128)(2,1)S(1)}, u32[]{:S(2)}, u32[]{:S(2)}) %all-to-all-start) | async-done | bytes 524320 | tf_op jit(solution)/shard_map/all_to_all | solution.py:638
  27.5 0.0 collective-permute-start.2
  27.5 0.6 %shard_map.215.total_ref = f32[512,256]{1,0:T(8,128)S(1)} custom-call(bf16[16,64,256]{2,1,0:T(8,128)(2,1)S(1)} %all-to-all-done.own_ref.refs_0_, bf16[512,1792]{1,0:T(8,128)(2,1)S(1)} %shard_map.214.pack_ref), custom_call_target="tpu_custom_call" | custom-call | flops 201326592 | bytes 2883584 | tf_op jit(solution)/shard_map/pallas_call | solution.py:614
  28.1 0.0 copy-start.7
  28.1 0.0 copy-start.8
  28.1 0.0 copy-start.13
  28.1 0.0 copy-start.16
  28.1 1.2 %collective-permute-done.2.oth_ref.refs_1_ = bf16[16,64,256]{2,1,0:T(8,128)(2,1)S(1)} collective-permute-done((bf16[16,64,256]{2,1,0:T(8,128)(2,1)S(1)}, bf16[16,64,256]{2,1,0:T(8,128)(2,1)S(1)}, u32[]{:S(2)}, u32[]{:S(2)}) %collective-permute-start.2) | collective-permute-done | bytes 524320 | tf_op jit(solution)/shard_map/ppermute | solution.py:635
  29.4 1.3 %shard_map.216 = bf16[16,8,1152]{2,1,0:T(8,128)(2,1)} custom-call(bf16[16,64,256]{2,1,0:T(8,128)(2,1)S(1)} %collective-permute-done.2.oth_ref.refs_1_, bf16[512,1792]{1,0:T(8,128)(2,1)S(1)} %shard_map.214.pack_ref, f32[512,256]{1,0:T(8,128)S(1)} %shard_map.215.total_ref), custom_call_target="tpu_custom_call" | custom-call | flops 201326592 | bytes 3178496 | tf_op jit(solution)/shard_map/pallas_call | solution.py:614
  30.7 0.0 copy-done.1
  30.7 5.0 %all-to-all-start.1 = ((bf16[16,8,1152]{2,1,0:T(8,128)(2,1)}), bf16[16,8,1152]{2,1,0:T(8,128)(2,1)S(1)}, u32[]{:S(2)}, u32[]{:S(2)}) async-start(bf16[16,8,1152]{2,1,0:T(8,128)(2,1)} %shard_map.216), calls=%async_computation.1 | async-start | bytes 589824 | tf_op jit(solution)/shard_map/all_to_all | solution.py:638
  35.8 0.0 copy-done.2
  35.8 0.0 copy-done.7
  35.8 0.0 copy-done.8
  35.8 7.6 %shard_map.217.refs_0_ = bf16[256,512]{1,0:T(8,128)(2,1)S(1)} custom-call(bf16[16,64,256]{2,1,0:T(8,128)(2,1)} %copy-done.1, bf16[16,64,256]{2,1,0:T(8,128)(2,1)} %copy-done.2, bf16[512,640]{1,0:T(8,128)(2,1)} %get-tuple-element.27.refs_2_, s32[2,16,128]{2,1,0:T(8,128)S(1)} %bitcast.11, bf16[256,640]{1,0:T(8,128)(2,1)} %get-tuple-element.28.refs_4_, ...), custom_call_target="tpu_custom_call" | custom-call | flops 2684354560 | bytes 22758912 | tf_op jit(solution)/shard_map/pallas_call | solution.py:595
  43.4 0.0 copy-start.3
  43.4 0.0 copy-start.6
  43.4 0.0 copy-start.14
  43.4 0.1 collective-permute-start.3
  43.5 1.5 %collective-permute-done.3.refs_1_ = bf16[256,512]{1,0:T(8,128)(2,1)S(1)} collective-permute-done((bf16[256,512]{1,0:T(8,128)(2,1)S(1)}, bf16[256,512]{1,0:T(8,128)(2,1)S(1)}, u32[]{:S(2)}, u32[]{:S(2)}) %collective-permute-start.3) | collective-permute-done | bytes 262176 | tf_op jit(solution)/shard_map/ppermute | solution.py:635
  45.0 1.2 %shard_map.219 = bf16[128,2,512]{2,1,0:T(2,128)(2,1)} custom-call(bf16[256,512]{1,0:T(8,128)(2,1)S(1)} %shard_map.217.refs_0_, bf16[256,512]{1,0:T(8,128)(2,1)S(1)} %collective-permute-done.3.refs_1_, f32[8,128]{1,0:T(8,128)S(1)} %shard_map.218.refs_2_), custom_call_target="tpu_custom_call" | custom-call | bytes 1 | tf_op jit(solution)/shard_map/pallas_call | solution.py:595
  46.2 0.5 all-to-all-done.1.refs_0_.refs_2_
  46.7 0.0 collective-permute-start.4
  46.7 1.6 %collective-permute-done.4.refs_1_ = bf16[16,8,1152]{2,1,0:T(8,128)(2,1)S(1)} collective-permute-done((bf16[16,8,1152]{2,1,0:T(8,128)(2,1)S(1)}, bf16[16,8,1152]{2,1,0:T(8,128)(2,1)S(1)}, u32[]{:S(2)}, u32[]{:S(2)}) %collective-permute-start.4) | collective-permute-done | bytes 294944 | tf_op jit(solution)/shard_map/ppermute | solution.py:635
  48.3 0.0 copy-done.6
  48.3 3.4 %shard_map.220 = bf16[2048,256]{1,0:T(8,128)(2,1)} custom-call(bf16[16,8,1152]{2,1,0:T(8,128)(2,1)S(1)} %all-to-all-done.1.refs_0_.refs_2_, bf16[16,8,1152]{2,1,0:T(8,128)(2,1)S(1)} %collective-permute-done.4.refs_1_, bf16[16,8,1152]{2,1,0:T(8,128)(2,1)S(1)} %all-to-all-done.1.refs_0_.refs_2_, s32[1,16,32]{2,1,0:T(8,128)S(1)} %copy-done.14, ...), custom_call_target="tpu_custom_call" | custom-call | flops 1207959552 | bytes 10061824 | tf_op jit(solution)/shard_map/pallas_call | solution.py:595
  (10 shorter events, 0.0 us)
Async XLA Ops:
  0.6 11.7 %copy-start.10 = (bf16[64,512]{1,0:T(8,128)(2,1)S(1)}, bf16[64,512]{1,0:T(8,128)(2,1)}, u32[]{:S(2)}) copy-start(bf16[64,512]{1,0:T(8,128)(2,1)} %refs_5_.3) | copy-start | bytes 196612
  0.6 11.7 %copy-start.9 = (bf16[64,512]{1,0:T(8,128)(2,1)S(1)}, bf16[64,512]{1,0:T(8,128)(2,1)}, u32[]{:S(2)}) copy-start(bf16[64,512]{1,0:T(8,128)(2,1)} %refs_4_.1) | copy-start | bytes 196612
  0.7 11.7 %copy-start.5 = (bf16[256,512]{1,0:T(8,128)(2,1)S(1)}, bf16[256,512]{1,0:T(8,128)(2,1)}, u32[]{:S(2)}) copy-start(bf16[256,512]{1,0:T(8,128)(2,1)} %refs_7_.4) | copy-start | bytes 786436
  0.7 11.7 %copy-start.4 = (bf16[256,512]{1,0:T(8,128)(2,1)S(1)}, bf16[256,512]{1,0:T(8,128)(2,1)}, u32[]{:S(2)}) copy-start(bf16[256,512]{1,0:T(8,128)(2,1)} %refs_6_.1) | copy-start | bytes 786436
  0.7 12.5 %copy-start.12 = (bf16[128,64]{0,1:T(8,128)(2,1)S(1)}, bf16[128,64]{0,1:T(8,128)(2,1)}, u32[]{:S(2)}) copy-start(bf16[128,64]{0,1:T(8,128)(2,1)} %param.24) | copy-start | bytes 49156
  4.0 23.5 %all-to-all-start = ((bf16[16,64,256]{2,1,0:T(8,128)(2,1)}), bf16[16,64,256]{2,1,0:T(8,128)(2,1)S(1)}, u32[]{:S(2)}, u32[]{:S(2)}) async-start(bf16[16,64,256]{2,1,0:T(8,128)(2,1)} %shard_map.212.refs_6_), calls=%async_computation | async-start | bytes 1048576 | tf_op jit(solution)/shard_map/all_to_all | solution.py:638
  13.2 9.8 %collective-permute-start.1 = (bf16[640,256]{1,0:T(8,128)(2,1)}, bf16[640,256]{1,0:T(8,128)(2,1)S(1)}, u32[]{:S(2)}, u32[]{:S(2)}) collective-permute-start(bf16[640,256]{1,0:T(8,128)(2,1)} %fusion.2), channel_id=1, source_target_pairs={{0,1},{1,0},{2,3},{3,2},{4,5},{5,4},{6,7},{7,6},{8,9},{9,8},{10,11... | collective-permute-start | bytes 983048 | tf_op jit(solution)/shard_map/ppermute | solution.py:635
  13.2 9.8 %collective-permute-start = (bf16[64,128]{1,0:T(8,128)(2,1)S(1)}, bf16[64,128]{1,0:T(8,128)(2,1)S(1)}, u32[]{:S(2)}, u32[]{:S(2)}) collective-permute-start(bf16[64,128]{1,0:T(8,128)(2,1)S(1)} %bitcast.9), channel_id=1, source_target_pairs={{0,1},{1,0},{2,3},{3,2},{4,5},{5,4},{6,7},{7,6},{8,9},{9,8},{10,11... | collective-permute-start | bytes 49160 | tf_op jit(solution)/shard_map/ppermute | solution.py:635
  13.7 9.3 %copy-start.15 = (s32[128,2]{0,1:T(2,128)S(1)}, s32[128,2]{0,1:T(2,128)}, u32[]{:S(2)}) copy-start(s32[128,2]{0,1:T(2,128)} %param.25) | copy-start | bytes 3076
  23.0 0.8 %copy-start.11 = (bf16[1,128,256]{2,1,0:T(8,128)(2,1)S(1)}, bf16[1,128,256]{2,1,0:T(8,128)(2,1)}, u32[]{:S(2)}) copy-start(bf16[1,128,256]{2,1,0:T(8,128)(2,1)} %get-tuple-element.21.refs_1_) | copy-start | bytes 196612
  27.5 3.2 %copy-start.1 = (bf16[16,64,256]{2,1,0:T(8,128)(2,1)}, bf16[16,64,256]{2,1,0:T(8,128)(2,1)S(1)}, u32[]{:S(2)}) copy-start(bf16[16,64,256]{2,1,0:T(8,128)(2,1)S(1)} %all-to-all-done.own_ref.refs_0_) | copy-start | bytes 1572868
  27.5 1.9 %collective-permute-start.2 = (bf16[16,64,256]{2,1,0:T(8,128)(2,1)S(1)}, bf16[16,64,256]{2,1,0:T(8,128)(2,1)S(1)}, u32[]{:S(2)}, u32[]{:S(2)}) collective-permute-start(bf16[16,64,256]{2,1,0:T(8,128)(2,1)S(1)} %all-to-all-done.own_ref.refs_0_), channel_id=1, source_target_pairs={{0,1},{1,0},{2,3},{3,2},{4,5},{5,4},{6,7},{7,6},{8,9},{9,8},{10,11... | collective-permute-start | bytes 1572872 | tf_op jit(solution)/shard_map/ppermute | solution.py:635
  28.1 7.7 %copy-start.7 = (bf16[256,512]{1,0:T(8,128)(2,1)S(1)}, bf16[256,512]{1,0:T(8,128)(2,1)}, u32[]{:S(2)}) copy-start(bf16[256,512]{1,0:T(8,128)(2,1)} %refs_7_.5) | copy-start | bytes 786436
  28.1 7.7 %copy-start.8 = (bf16[256,512]{1,0:T(8,128)(2,1)S(1)}, bf16[256,512]{1,0:T(8,128)(2,1)}, u32[]{:S(2)}) copy-start(bf16[256,512]{1,0:T(8,128)(2,1)} %refs_8_.3) | copy-start | bytes 786436
  28.1 7.7 %copy-start.13 = (s32[128,2,16]{0,2,1:T(8,128)S(1)}, s32[128,2,16]{0,2,1:T(8,128)}, u32[]{:S(2)}) copy-start(s32[128,2,16]{0,2,1:T(8,128)} %param.26) | copy-start | bytes 49156
  28.1 7.7 %copy-start.16 = (f32[128]{0:T(128)S(1)}, f32[128]{0:T(128)}, u32[]{:S(2)}) copy-start(f32[128]{0:T(128)} %param.30) | copy-start | bytes 1540
  29.4 6.4 %copy-start.2 = (bf16[16,64,256]{2,1,0:T(8,128)(2,1)}, bf16[16,64,256]{2,1,0:T(8,128)(2,1)S(1)}, u32[]{:S(2)}) copy-start(bf16[16,64,256]{2,1,0:T(8,128)(2,1)S(1)} %collective-permute-done.2.oth_ref.refs_1_) | copy-start | bytes 1572868
  30.7 16.0 %all-to-all-start.1 = ((bf16[16,8,1152]{2,1,0:T(8,128)(2,1)}), bf16[16,8,1152]{2,1,0:T(8,128)(2,1)S(1)}, u32[]{:S(2)}, u32[]{:S(2)}) async-start(bf16[16,8,1152]{2,1,0:T(8,128)(2,1)} %shard_map.216), calls=%async_computation.1 | async-start | bytes 589824 | tf_op jit(solution)/shard_map/all_to_all | solution.py:638
  35.8 7.7 %copy-start = (f32[3,512,256]{2,1,0:T(8,128)S(1)}, f32[3,512,256]{2,1,0:T(8,128)}, u32[]{:S(2)}) copy-start(f32[3,512,256]{2,1,0:T(8,128)} %get-tuple-element.34.refs_0_.refs_5_) | copy-start | bytes 4718596
  43.4 4.9 %copy-start.3 = (bf16[16,64,256]{2,1,0:T(8,128)(2,1)S(1)}, bf16[16,64,256]{2,1,0:T(8,128)(2,1)}, u32[]{:S(2)}) copy-start(bf16[16,64,256]{2,1,0:T(8,128)(2,1)} %shard_map.212.refs_6_) | copy-start | bytes 1572868
  43.4 4.9 %copy-start.6 = (bf16[2048,256]{1,0:T(8,128)(2,1)S(1)}, bf16[2048,256]{1,0:T(8,128)(2,1)}, u32[]{:S(2)}) copy-start(bf16[2048,256]{1,0:T(8,128)(2,1)} %get-tuple-element.37.refs_7_) | copy-start | bytes 3145732
  43.4 4.9 %copy-start.14 = (s32[1,16,32]{2,1,0:T(8,128)S(1)}, s32[1,16,32]{2,1,0:T(8,128)}, u32[]{:S(2)}) copy-start(s32[1,16,32]{2,1,0:T(8,128)} %refs_3_.1) | copy-start | bytes 6148
  43.4 1.6 %collective-permute-start.3 = (bf16[256,512]{1,0:T(8,128)(2,1)S(1)}, bf16[256,512]{1,0:T(8,128)(2,1)S(1)}, u32[]{:S(2)}, u32[]{:S(2)}) collective-permute-start(bf16[256,512]{1,0:T(8,128)(2,1)S(1)} %shard_map.217.refs_0_), channel_id=1, source_target_pairs={{0,1},{1,0},{2,3},{3,2},{4,5},{5,4},{6,7},{7,6},{8,9},{9,8},{10,11... | collective-permute-start | bytes 786440 | tf_op jit(solution)/shard_map/ppermute | solution.py:635
  46.7 1.6 %collective-permute-start.4 = (bf16[16,8,1152]{2,1,0:T(8,128)(2,1)S(1)}, bf16[16,8,1152]{2,1,0:T(8,128)(2,1)S(1)}, u32[]{:S(2)}, u32[]{:S(2)}) collective-permute-start(bf16[16,8,1152]{2,1,0:T(8,128)(2,1)S(1)} %all-to-all-done.1.refs_0_.refs_2_), channel_id=1, source_target_pairs={{0,1},{1,0},{2,3},{3,2},{4,5},{5,4},{6,7},{7,6},{8,9},{9,8},{10,11... | collective-permute-start | bytes 884744 | tf_op jit(solution)/shard_map/ppermute | solution.py:635

commit v6 on v4

--- a/solution.py
+++ b/solution.py
@@ -366,14 +366,19 @@
     half = oth_ref.shape[-1]
     at_sent = pack_places(pack_ref.shape[0], half)[3]
     oth = part_of(oth_ref, packed, cap, cap_self)
-    out = total_ref[...] + message_part(oth, pack_ref, half, half)
+    out = (total_ref[...] + message_part(oth, pack_ref, half, half)).astype(BF)
     if not packed:
-        out_ref[...] = out.astype(BF)
+        out_ref[...] = out
         return
-    parts = out.reshape(peers, cap_self // 8, 8, half)
-    parts = [parts[:, n] for n in range(cap_self // 8)]
-    parts.append(jnp.broadcast_to(pack_ref[:peers, at_sent:].astype(F32)[:, None, :], (peers, 8, 128)))
-    out_ref[...] = jnp.concatenate(parts, axis=2).astype(BF)
+    tiles = half // 128
+    for tile in range(tiles):
+        out_ref[:, tile * cap_self : (tile + 1) * cap_self, :] = out[
+            :, tile * 128 : (tile + 1) * 128
+        ].reshape(peers, cap_self, 128)
+    sent = pack_ref[:peers, at_sent:].astype(F32)
+    out_ref[:, tiles * cap_self :, :] = jnp.broadcast_to(sent[:, None, :], (peers, 16, 128)).astype(
+        BF
+    )
 
 
 def attention_kernel(
@@ -475,15 +480,18 @@
     rows, half = base_ref.shape
     serve = serve_ref[0]
     slots = serve.size
+    tiles = half // 128
 
     def messages(ref):
         if not packed:
             return ref[...]
-        values = ref[...].astype(F32)
-        parts = [
-            values[:, None, :, n * half : (n + 1) * half] for n in range(cap_self // 8)
-        ]
-        return jnp.concatenate(parts, axis=1).reshape(slots, half).astype(BF)
+        return jnp.concatenate(
+            [
+                ref[:, tile * cap_self : (tile + 1) * cap_self, :].reshape(slots, 128)
+                for tile in range(tiles)
+            ],
+            axis=1,
+        )
 
     line = row(serve)
     match = column(serve, 0, slots) == line
@@ -495,9 +503,7 @@
     for part in range(out_ref.parts):
         put[part * step : (part + 1) * step, :] = hot_rows(line, part * step, step)
     peers = slots // cap_self
-    counts = count_ref[...]
-    if packed:
-        counts = counts.astype(F32)[:, 0, counts.shape[2] - 128 :].astype(BF)
+    counts = count_ref[:, tiles * cap_self :, :][:, 0, :] if packed else count_ref[...]
     spread = dot(one_hot(iota((slots, peers), 0) // cap_self == iota((slots, peers), 1)), counts)
     lane = iota((slots, 128), 1)
     spread = jnp.where(iota((slots, 128), 0) % cap_self == lane, spread, 0.0).astype(BF)
@@ -705,7 +711,7 @@
     if packed:
         both = (fetched, fetched_x)
         mine = (fetched, fetched_x)
-        back_shape = shape((peers, 8, cap_self // 8 * half + 128), BF)
+        back_shape = shape((peers, (half // 128) * cap_self + 16, 128), BF)
     else:
         nbr = [f[:, :cap].reshape(slots_n, half) for f in (fetched, fetched_x)]
         mine = [f[:, cap:].reshape(slots_s, half) for f in (fetched, fetched_x)]

time: 52.6 us -> 52.6 us (level)
  no operation moved by 1% of the time
where the time goes in v6:
time: 52.6 us; the launch traced here: 52.1 us
  Pallas kernels  26.7 us (51%)
  starting transfers between devices  13 us (25%)
  waiting for transfers between devices  8.37 us (16%)
  local copies, waits for them, and re-layouts  2.22 us (4%)
  between operations  1.04 us (2%)
  other arithmetic  0.75 us (1%)
    pallas_call x6, Pallas kernels, call(): pl.pallas_call(functools.partial(staged, kernel, whole, parts, late), out...  24.8 us
    all_to_all x2, starting transfers between devices, exchange(): return lax.all_to_all(x, 'nodes', split_axis=0, concat_axis=0, tiled=True)  12.2 us
    ppermute x5, waiting for transfers between devices, swap(): return lax.ppermute(x, 'mp', [(0, 1), (1, 0)])  4.27 us
    all_to_all x2, waiting for transfers between devices, exchange(): return lax.all_to_all(x, 'nodes', split_axis=0, concat_axis=0, tiled=True)  4.09 us
    unnamed x28, local copies, waits for them, and re-layouts  2.22 us
    pallas_call x2, Pallas kernels, plain(): pl.pallas_call(kernel, out_shape=out_shape, in_specs=[VMEM] * len(args),...  1.95 us
  transfers between devices with their start and end apart: 7, of which 4 were waited for; matrix products, arithmetic and copies ran while one was open for 1% of the time, Pallas kernels for 35%

profile of v6, /device:TPU:0, one launch (start us, length us, event | category | flops | bytes accessed | tf_op | source)
XLA Modules:
  0.0 52.1 jit_solution(17315005287365142168)
XLA Ops:
  0.6 0.0 copy-start.6
  0.6 0.0 copy-start.5
  0.7 0.0 copy-start.3
  0.7 0.0 copy-start.2
  0.7 3.3 %shard_map.212.refs_6_ = bf16[16,64,256]{2,1,0:T(8,128)(2,1)} custom-call(s32[1,16,32]{2,1,0:T(8,128)} %refs_0_.2, s32[1,16,32]{2,1,0:T(8,128)} %refs_3_.1, bf16[2048,512]{1,0:T(8,128)(2,1)} %refs_5_.2), custom_call_target="tpu_custom_call" | custom-call | flops 1073741824 | bytes 2625536 | tf_op jit(solution)/shard_map/pallas_call | solution.py:578
  4.0 0.0 copy-start.7
  4.0 8.3 %all-to-all-start = ((bf16[16,64,256]{2,1,0:T(8,128)(2,1)}), bf16[16,64,256]{2,1,0:T(8,128)(2,1)S(1)}, u32[]{:S(2)}, u32[]{:S(2)}) async-start(bf16[16,64,256]{2,1,0:T(8,128)(2,1)} %shard_map.212.refs_6_), calls=%async_computation | async-start | bytes 1048576 | tf_op jit(solution)/shard_map/all_to_all | solution.py:621
  12.3 0.0 copy-done.6
  12.4 0.0 copy-done.5
  12.4 0.0 copy-done.3
  12.4 0.0 copy-done.2
  12.4 0.7 %fusion.2 = bf16[640,256]{1,0:T(8,128)(2,1)} fusion(s32[]{:T(128)S(6)} %select_n.3, bf16[256,512]{1,0:T(8,128)(2,1)S(1)} %copy-done.2, bf16[256,512]{1,0:T(8,128)(2,1)S(1)} %copy-done.3, bf16[64,512]{1,0:T(8,128)(2,1)S(1)} %copy-done.5, bf16[64,512]{1,0:T(8,128)(2,1)S(1)} %copy-done.6), kind=kLoop, calls=%fused_computation.6 | loop fusion | flops 1310720 | bytes 983044 | tf_op jit(solution)/shard_map/concatenate | solution.py:650
  13.1 0.0 collective-permute-start.1
  13.1 0.0 copy-done.7
  13.1 0.5 collective-permute-start
  13.7 0.0 copy-start.9
  13.7 6.8 %shard_map.213 = (f32[3,512,256]{2,1,0:T(8,128)}, bf16[16,128,256]{2,1,0:T(8,128)(2,1)}, bf16[256,640]{1,0:T(8,128)(2,1)}, bf16[512,640]{1,0:T(8,128)(2,1)}, bf16[2048,256]{1,0:T(8,128)(2,1)}) custom-call(s32[1,16,32]{2,1,0:T(8,128)} %refs_3_.1, s32[1,128]{1,0:T(1,128)} %bitcast.19, s32[2,16,128]{2,1,0:T(8,128)} %bitcast.18, f32[1,128]{1,0:T(1,128)} %bitcast.20, ...), custom_call_target="tpu_custom_call" | custom-call | flops 1476395008 | bytes 8539648 | tf_op jit(solution)/shard_map/pallas_call | solution.py:578
  20.5 0.0 collective-permute-done.refs_3_
  20.5 0.0 collective-permute-done.1.refs_8_
  20.5 0.0 copy-done.9
  20.5 0.0 copy-start.1
  20.5 1.2 %copy-done.1 = bf16[16,128,256]{2,1,0:T(8,128)(2,1)S(1)} copy-done((bf16[16,128,256]{2,1,0:T(8,128)(2,1)S(1)}, bf16[16,128,256]{2,1,0:T(8,128)(2,1)}, u32[]{:S(2)}) %copy-start.1) | copy-done | bytes 1048600
  21.8 1.6 %shard_map.214.pack_ref = bf16[512,1792]{1,0:T(8,128)(2,1)S(1)} custom-call(s32[2,128]{1,0:T(2,128)S(1)} %bitcast.11, bf16[16,128,256]{2,1,0:T(8,128)(2,1)S(1)} %copy-done.1, bf16[64,128]{1,0:T(8,128)(2,1)S(1)} %bitcast.10, bf16[64,128]{1,0:T(8,128)(2,1)S(1)} %collective-permute-done.refs_3_, bf16[64,512]{1,0:T(8,128)(2,1)S(1)} %copy-done.5, ...), custom_call_target="tpu_custom_call" | custom-call | flops 201326592 | bytes 3900416 | tf_op jit(solution)/shard_map/pallas_call | solution.py:578
  23.4 4.1 %all-to-all-done.own_ref.refs_0_ = bf16[16,64,256]{2,1,0:T(8,128)(2,1)S(1)} async-done(((bf16[16,64,256]{2,1,0:T(8,128)(2,1)}), bf16[16,64,256]{2,1,0:T(8,128)(2,1)S(1)}, u32[]{:S(2)}, u32[]{:S(2)}) %all-to-all-start) | async-done | bytes 524320 | tf_op jit(solution)/shard_map/all_to_all | solution.py:621
  27.5 0.0 collective-permute-start.2
  27.5 0.6 %shard_map.215.total_ref = f32[512,256]{1,0:T(8,128)S(1)} custom-call(bf16[16,64,256]{2,1,0:T(8,128)(2,1)S(1)} %all-to-all-done.own_ref.refs_0_, bf16[512,1792]{1,0:T(8,128)(2,1)S(1)} %shard_map.214.pack_ref), custom_call_target="tpu_custom_call" | custom-call | flops 201326592 | bytes 2883584 | tf_op jit(solution)/shard_map/pallas_call | solution.py:597
  28.1 0.0 copy-start.10
  28.1 0.0 copy-start.12
  28.1 0.0 copy-start.13
  28.1 1.3 %collective-permute-done.2.oth_ref.refs_1_ = bf16[16,64,256]{2,1,0:T(8,128)(2,1)S(1)} collective-permute-done((bf16[16,64,256]{2,1,0:T(8,128)(2,1)S(1)}, bf16[16,64,256]{2,1,0:T(8,128)(2,1)S(1)}, u32[]{:S(2)}, u32[]{:S(2)}) %collective-permute-start.2) | collective-permute-done | bytes 524320 | tf_op jit(solution)/shard_map/ppermute | solution.py:618
  29.4 1.3 %shard_map.216 = bf16[16,80,128]{2,1,0:T(8,128)(2,1)} custom-call(bf16[16,64,256]{2,1,0:T(8,128)(2,1)S(1)} %collective-permute-done.2.oth_ref.refs_1_, bf16[512,1792]{1,0:T(8,128)(2,1)S(1)} %shard_map.214.pack_ref, f32[512,256]{1,0:T(8,128)S(1)} %shard_map.215.total_ref), custom_call_target="tpu_custom_call" | custom-call | flops 201326592 | bytes 3211264 | tf_op jit(solution)/shard_map/pallas_call | solution.py:597
  30.7 0.0 copy-done
  30.7 0.0 copy-done.4
  30.7 3.9 %all-to-all-start.1 = ((bf16[16,80,128]{2,1,0:T(8,128)(2,1)}), bf16[16,80,128]{2,1,0:T(8,128)(2,1)S(1)}, u32[]{:S(2)}, u32[]{:S(2)}) async-start(bf16[16,80,128]{2,1,0:T(8,128)(2,1)} %shard_map.216), calls=%async_computation.1 | async-start | bytes 655360 | tf_op jit(solution)/shard_map/all_to_all | solution.py:621
  34.7 0.0 copy-done.10
  34.7 0.0 copy-done.12
  34.7 0.0 copy-done.13
  34.7 0.0 copy-start.11
  34.7 0.9 %copy-done.11 = bf16[256,512]{1,0:T(8,128)(2,1)S(1)} copy-done((bf16[256,512]{1,0:T(8,128)(2,1)S(1)}, bf16[256,512]{1,0:T(8,128)(2,1)}, u32[]{:S(2)}) %copy-start.11) | copy-done | bytes 262168
  35.6 7.9 %shard_map.217.refs_0_ = bf16[256,512]{1,0:T(8,128)(2,1)S(1)} custom-call(bf16[16,64,256]{2,1,0:T(8,128)(2,1)} %copy-done, bf16[16,64,256]{2,1,0:T(8,128)(2,1)} %copy-done.4, bf16[512,640]{1,0:T(8,128)(2,1)} %get-tuple-element.22.refs_2_, s32[2,16,128]{2,1,0:T(8,128)S(1)} %bitcast.13, bf16[16,128,256]{2,1,0:T(8,128)(2,1)} %get-tuple-element.23.refs_1_.refs_4_, ...), custom_call_target="tpu_custom_call" | custom-call | flops 2684354560 | bytes 3884544 | tf_op jit(solution)/shard_map/pallas_call | solution.py:578
  43.6 0.1 collective-permute-start.3
  43.7 1.5 %collective-permute-done.3.refs_1_ = bf16[256,512]{1,0:T(8,128)(2,1)S(1)} collective-permute-done((bf16[256,512]{1,0:T(8,128)(2,1)S(1)}, bf16[256,512]{1,0:T(8,128)(2,1)S(1)}, u32[]{:S(2)}, u32[]{:S(2)}) %collective-permute-start.3) | collective-permute-done | bytes 262176 | tf_op jit(solution)/shard_map/ppermute | solution.py:618
  45.2 1.2 %shard_map.218 = bf16[128,2,512]{2,1,0:T(2,128)(2,1)} custom-call(bf16[256,512]{1,0:T(8,128)(2,1)S(1)} %shard_map.217.refs_0_, bf16[256,512]{1,0:T(8,128)(2,1)S(1)} %collective-permute-done.3.refs_1_), custom_call_target="tpu_custom_call" | custom-call | bytes 1 | tf_op jit(solution)/shard_map/pallas_call | solution.py:578
  46.3 0.0 all-to-all-done.1.refs_0_.refs_2_
  46.4 0.2 collective-permute-start.4
  46.6 1.5 %collective-permute-done.4.refs_1_ = bf16[16,80,128]{2,1,0:T(8,128)(2,1)S(1)} collective-permute-done((bf16[16,80,128]{2,1,0:T(8,128)(2,1)S(1)}, bf16[16,80,128]{2,1,0:T(8,128)(2,1)S(1)}, u32[]{:S(2)}, u32[]{:S(2)}) %collective-permute-start.4) | collective-permute-done | bytes 327712 | tf_op jit(solution)/shard_map/ppermute | solution.py:618
  48.1 0.0 copy-done.8
  48.1 3.9 %shard_map.219 = bf16[2048,256]{1,0:T(8,128)(2,1)} custom-call(bf16[16,80,128]{2,1,0:T(8,128)(2,1)S(1)} %all-to-all-done.1.refs_0_.refs_2_, bf16[16,80,128]{2,1,0:T(8,128)(2,1)S(1)} %collective-permute-done.4.refs_1_, bf16[16,80,128]{2,1,0:T(8,128)(2,1)S(1)} %all-to-all-done.1.refs_0_.refs_2_, s32[1,16,32]{2,1,0:T(8,128)S(1)} %copy-done.8, ...), custom_call_target="tpu_custom_call" | custom-call | flops 1207959552 | bytes 5965824 | tf_op jit(solution)/shard_map/pallas_call | solution.py:578
  (3 shorter events, 0.0 us)
Async XLA Ops:
  0.6 11.7 %copy-start.6 = (bf16[64,512]{1,0:T(8,128)(2,1)S(1)}, bf16[64,512]{1,0:T(8,128)(2,1)}, u32[]{:S(2)}) copy-start(bf16[64,512]{1,0:T(8,128)(2,1)} %refs_5_.3) | copy-start | bytes 196612
  0.6 11.7 %copy-start.5 = (bf16[64,512]{1,0:T(8,128)(2,1)S(1)}, bf16[64,512]{1,0:T(8,128)(2,1)}, u32[]{:S(2)}) copy-start(bf16[64,512]{1,0:T(8,128)(2,1)} %refs_4_.1) | copy-start | bytes 196612
  0.7 11.7 %copy-start.3 = (bf16[256,512]{1,0:T(8,128)(2,1)S(1)}, bf16[256,512]{1,0:T(8,128)(2,1)}, u32[]{:S(2)}) copy-start(bf16[256,512]{1,0:T(8,128)(2,1)} %refs_7_.3) | copy-start | bytes 786436
  0.7 11.7 %copy-start.2 = (bf16[256,512]{1,0:T(8,128)(2,1)S(1)}, bf16[256,512]{1,0:T(8,128)(2,1)}, u32[]{:S(2)}) copy-start(bf16[256,512]{1,0:T(8,128)(2,1)} %refs_6_.1) | copy-start | bytes 786436
  4.0 9.1 %copy-start.7 = (bf16[128,64]{0,1:T(8,128)(2,1)S(1)}, bf16[128,64]{0,1:T(8,128)(2,1)}, u32[]{:S(2)}) copy-start(bf16[128,64]{0,1:T(8,128)(2,1)} %param.24) | copy-start | bytes 49156
  4.0 23.5 %all-to-all-start = ((bf16[16,64,256]{2,1,0:T(8,128)(2,1)}), bf16[16,64,256]{2,1,0:T(8,128)(2,1)S(1)}, u32[]{:S(2)}, u32[]{:S(2)}) async-start(bf16[16,64,256]{2,1,0:T(8,128)(2,1)} %shard_map.212.refs_6_), calls=%async_computation | async-start | bytes 1048576 | tf_op jit(solution)/shard_map/all_to_all | solution.py:621
  13.1 7.4 %collective-permute-start.1 = (bf16[640,256]{1,0:T(8,128)(2,1)}, bf16[640,256]{1,0:T(8,128)(2,1)S(1)}, u32[]{:S(2)}, u32[]{:S(2)}) collective-permute-start(bf16[640,256]{1,0:T(8,128)(2,1)} %fusion.2), channel_id=1, source_target_pairs={{0,1},{1,0},{2,3},{3,2},{4,5},{5,4},{6,7},{7,6},{8,9},{9,8},{10,11... | collective-permute-start | bytes 983048 | tf_op jit(solution)/shard_map/ppermute | solution.py:618
  13.1 7.4 %collective-permute-start = (bf16[64,128]{1,0:T(8,128)(2,1)S(1)}, bf16[64,128]{1,0:T(8,128)(2,1)S(1)}, u32[]{:S(2)}, u32[]{:S(2)}) collective-permute-start(bf16[64,128]{1,0:T(8,128)(2,1)S(1)} %bitcast.9), channel_id=1, source_target_pairs={{0,1},{1,0},{2,3},{3,2},{4,5},{5,4},{6,7},{7,6},{8,9},{9,8},{10,11... | collective-permute-start | bytes 49160 | tf_op jit(solution)/shard_map/ppermute | solution.py:618
  13.7 6.9 %copy-start.9 = (s32[128,2]{0,1:T(2,128)S(1)}, s32[128,2]{0,1:T(2,128)}, u32[]{:S(2)}) copy-start(s32[128,2]{0,1:T(2,128)} %param.25) | copy-start | bytes 3076
  20.5 1.2 %copy-start.1 = (bf16[16,128,256]{2,1,0:T(8,128)(2,1)S(1)}, bf16[16,128,256]{2,1,0:T(8,128)(2,1)}, u32[]{:S(2)}) copy-start(bf16[16,128,256]{2,1,0:T(8,128)(2,1)} %get-tuple-element.23.refs_1_.refs_4_) | copy-start | bytes 3145732
  27.5 3.3 %copy-start = (bf16[16,64,256]{2,1,0:T(8,128)(2,1)}, bf16[16,64,256]{2,1,0:T(8,128)(2,1)S(1)}, u32[]{:S(2)}) copy-start(bf16[16,64,256]{2,1,0:T(8,128)(2,1)S(1)} %all-to-all-done.own_ref.refs_0_) | copy-start | bytes 1572868
  27.5 1.9 %collective-permute-start.2 = (bf16[16,64,256]{2,1,0:T(8,128)(2,1)S(1)}, bf16[16,64,256]{2,1,0:T(8,128)(2,1)S(1)}, u32[]{:S(2)}, u32[]{:S(2)}) collective-permute-start(bf16[16,64,256]{2,1,0:T(8,128)(2,1)S(1)} %all-to-all-done.own_ref.refs_0_), channel_id=1, source_target_pairs={{0,1},{1,0},{2,3},{3,2},{4,5},{5,4},{6,7},{7,6},{8,9},{9,8},{10,11... | collective-permute-start | bytes 1572872 | tf_op jit(solution)/shard_map/ppermute | solution.py:618
  28.1 6.5 %copy-start.10 = (bf16[256,512]{1,0:T(8,128)(2,1)S(1)}, bf16[256,512]{1,0:T(8,128)(2,1)}, u32[]{:S(2)}) copy-start(bf16[256,512]{1,0:T(8,128)(2,1)} %refs_8_.3) | copy-start | bytes 786436
  28.1 6.5 %copy-start.12 = (s32[128,2,16]{0,2,1:T(8,128)S(1)}, s32[128,2,16]{0,2,1:T(8,128)}, u32[]{:S(2)}) copy-start(s32[128,2,16]{0,2,1:T(8,128)} %param.26) | copy-start | bytes 49156
  28.1 6.5 %copy-start.13 = (f32[128]{0:T(128)S(1)}, f32[128]{0:T(128)}, u32[]{:S(2)}) copy-start(f32[128]{0:T(128)} %param.30) | copy-start | bytes 1540
  29.4 1.3 %copy-start.4 = (bf16[16,64,256]{2,1,0:T(8,128)(2,1)}, bf16[16,64,256]{2,1,0:T(8,128)(2,1)S(1)}, u32[]{:S(2)}) copy-start(bf16[16,64,256]{2,1,0:T(8,128)(2,1)S(1)} %collective-permute-done.2.oth_ref.refs_1_) | copy-start | bytes 1572868
  30.7 15.6 %all-to-all-start.1 = ((bf16[16,80,128]{2,1,0:T(8,128)(2,1)}), bf16[16,80,128]{2,1,0:T(8,128)(2,1)S(1)}, u32[]{:S(2)}, u32[]{:S(2)}) async-start(bf16[16,80,128]{2,1,0:T(8,128)(2,1)} %shard_map.216), calls=%async_computation.1 | async-start | bytes 655360 | tf_op jit(solution)/shard_map/all_to_all | solution.py:621
  34.7 1.0 %copy-start.11 = (bf16[256,512]{1,0:T(8,128)(2,1)S(1)}, bf16[256,512]{1,0:T(8,128)(2,1)}, u32[]{:S(2)}) copy-start(bf16[256,512]{1,0:T(8,128)(2,1)} %refs_9_.3) | copy-start | bytes 786436
  35.6 12.4 %copy-start.8 = (s32[1,16,32]{2,1,0:T(8,128)S(1)}, s32[1,16,32]{2,1,0:T(8,128)}, u32[]{:S(2)}) copy-start(s32[1,16,32]{2,1,0:T(8,128)} %refs_3_.1) | copy-start | bytes 6148
  43.6 1.6 %collective-permute-start.3 = (bf16[256,512]{1,0:T(8,128)(2,1)S(1)}, bf16[256,512]{1,0:T(8,128)(2,1)S(1)}, u32[]{:S(2)}, u32[]{:S(2)}) collective-permute-start(bf16[256,512]{1,0:T(8,128)(2,1)S(1)} %shard_map.217.refs_0_), channel_id=1, source_target_pairs={{0,1},{1,0},{2,3},{3,2},{4,5},{5,4},{6,7},{7,6},{8,9},{9,8},{10,11... | collective-permute-start | bytes 786440 | tf_op jit(solution)/shard_map/ppermute | solution.py:618
  46.4 1.7 %collective-permute-start.4 = (bf16[16,80,128]{2,1,0:T(8,128)(2,1)S(1)}, bf16[16,80,128]{2,1,0:T(8,128)(2,1)S(1)}, u32[]{:S(2)}, u32[]{:S(2)}) collective-permute-start(bf16[16,80,128]{2,1,0:T(8,128)(2,1)S(1)} %all-to-all-done.1.refs_0_.refs_2_), channel_id=1, source_target_pairs={{0,1},{1,0},{2,3},{3,2},{4,5},{5,4},{6,7},{7,6},{8,9},{9,8},{10,11... | collective-permute-start | bytes 983048 | tf_op jit(solution)/shard_map/ppermute | solution.py:618
